TPU v7x, 128 devices: a whole 4x4x4 slice. The times are simulated.
128 devices in a mesh: ctx: 32 (over x, y, core), head: 4 (over z).
Axes of the slice: x: 4, y: 4, z: 4, core: 2. Of those that a mesh axis runs over, the one named last changes fastest.
Arguments:
- queries: bfloat16 [32, 8, 64, 3072], P('ctx', None, None, 'head'), may hold values from -160 to 160
- keys: bfloat16 [32, 8, 64, 3072], P('ctx', None, None, 'head'), may hold values from -7 to 7
- values: bfloat16 [32, 8, 64, 3072], P('ctx', None, None, 'head'), may hold values from -6 to 6
- out_grad: bfloat16 [32, 8, 64, 3072], P('ctx', None, None, 'head'), may hold values from -6 to 6
- window_mask: int32 [32, 8, 27], P('ctx'), may hold values 0 or 1
Outputs:
- query_gradient: bfloat16 [32, 8, 64, 3072], P('ctx', None, None, 'head')
- key_gradient: bfloat16 [32, 8, 64, 3072], P('ctx', None, None, 'head')
- value_gradient: bfloat16 [32, 8, 64, 3072], P('ctx', None, None, 'head')
All inputs are finite; a program needn't handle non-finite values. No bound on the sum of `window_mask` on one device may be relied on, other than what follows from the above.
Results may differ from a plain program's by a relative error of at most 0.015.
Values may be sent and summed in bfloat16 or wider, within the bound.
No kernel may reach another device: no remote copies, remote signals or barrier semaphores. Data moves between devices by JAX's collectives and lax.ppermute only.
A program may use at most 192 MiB of HBM per device.

v0:
```python
import jax
import jax.numpy as jnp
from jax import lax
from jax.sharding import PartitionSpec as P

HEAD_DIM = 128
TILE = 4
ROW_BLOCKS = 2


NEG_FILL = -1e30


def from_behind(shard, axis, by):
    peers = lax.axis_size(axis)
    pairs = [(i, i + by) for i in range(peers) if 0 <= i + by < peers]
    return lax.ppermute(shard, axis, pairs)


def to_pillars(tensor):
    frames, height, columns_all, channels = tensor.shape
    col_blocks = columns_all // TILE
    shaped = tensor.reshape(frames, ROW_BLOCKS, TILE, col_blocks, TILE, channels)
    shaped = shaped.transpose(1, 3, 0, 2, 4, 5)
    return shaped.reshape(ROW_BLOCKS * col_blocks, frames, TILE, TILE, channels)


def from_pillars(pillars):
    devices, frames, channels = (pillars.shape[0], pillars.shape[1], pillars.shape[4])
    col_blocks = devices // ROW_BLOCKS
    shaped = pillars.reshape(ROW_BLOCKS, col_blocks, frames, TILE, TILE, channels)
    shaped = shaped.transpose(2, 0, 3, 1, 4, 5)
    return shaped.reshape(frames, ROW_BLOCKS * TILE, col_blocks * TILE, channels)


def cube_grads(query_row_matrix, key_row_matrix, value_row_matrix, gradient_row_values, allowed):
    softmax_scale_factor = HEAD_DIM ** (-0.5)
    mask_rows = allowed[:, None, None, :]
    score_matrix = (
        jnp.einsum(
            "tqhd,tkhd->thqk", query_row_matrix, key_row_matrix, preferred_element_type=jnp.float32
        )
        * softmax_scale_factor
    )
    score_matrix = jnp.where(mask_rows, score_matrix, NEG_FILL)
    row_max = jnp.max(score_matrix, axis=-1, keepdims=True)
    weights = jnp.where(mask_rows, jnp.exp(score_matrix - row_max), 0.0)
    attention = weights / jnp.sum(weights, axis=-1, keepdims=True)
    attention_lower_precision = attention.astype(jnp.bfloat16)
    output_rows = jnp.einsum(
        "thqk,tkhd->tqhd",
        attention_lower_precision,
        value_row_matrix,
        preferred_element_type=jnp.float32,
    )
    row_dot = jnp.sum(gradient_row_values.astype(jnp.float32) * output_rows, axis=-1)
    probability_gradient = jnp.einsum(
        "tqhd,tkhd->thqk", gradient_row_values, value_row_matrix, preferred_element_type=jnp.float32
    )
    score_gradient = (
        attention
        * (probability_gradient - jnp.transpose(row_dot, (0, 2, 1))[..., None])
        * softmax_scale_factor
    ).astype(jnp.bfloat16)
    query_gradient = jnp.einsum(
        "thqk,tkhd->tqhd", score_gradient, key_row_matrix, preferred_element_type=jnp.float32
    )
    key_gradient = jnp.einsum(
        "thqk,tqhd->tkhd", score_gradient, query_row_matrix, preferred_element_type=jnp.float32
    )
    value_gradient = jnp.einsum(
        "thqk,tqhd->tkhd",
        attention_lower_precision,
        gradient_row_values,
        preferred_element_type=jnp.float32,
    )
    return (query_gradient, key_gradient, value_gradient)


def shards(queries, keys, values, out_grad, window_mask):
    devices = lax.axis_size("ctx")
    place = lax.axis_index("ctx")
    col_blocks = devices // ROW_BLOCKS
    channels = queries.shape[3]
    heads_local = channels // HEAD_DIM
    cube_cells = TILE**3
    query_p, grad_p, key_p, value_p = (
        lax.all_to_all(to_pillars(queries), "ctx", split_axis=0, concat_axis=1, tiled=True),
        lax.all_to_all(to_pillars(out_grad), "ctx", split_axis=0, concat_axis=1, tiled=True),
        lax.all_to_all(to_pillars(keys), "ctx", split_axis=0, concat_axis=1, tiled=True),
        lax.all_to_all(to_pillars(values), "ctx", split_axis=0, concat_axis=1, tiled=True),
    )
    frames_all = query_p.shape[1]
    time_blocks = frames_all // TILE
    joined = jnp.stack([key_p[0], value_p[0]])
    steps = (-1, 0, 1)
    window = jnp.stack(
        [
            jnp.stack(
                [
                    (
                        joined
                        if row_step == 0 and col_step == 0
                        else from_behind(joined, "ctx", -(row_step * col_blocks + col_step))
                    )
                    for col_step in steps
                ],
                axis=1,
            )
            for row_step in steps
        ],
        axis=1,
    )
    window = window.reshape(2, 3, 3, time_blocks, cube_cells, heads_local, HEAD_DIM).transpose(
        0, 3, 1, 2, 4, 5, 6
    )
    window = jnp.pad(window, ((0, 0), (1, 1), (0, 0), (0, 0), (0, 0), (0, 0), (0, 0)))
    key_pad, value_pad = (window[0], window[1])
    query_cubes = query_p[0].reshape(time_blocks, cube_cells, heads_local, HEAD_DIM)
    grad_cubes = grad_p[0].reshape(time_blocks, cube_cells, heads_local, HEAD_DIM)
    row_here = place // col_blocks
    col_here = place % col_blocks
    offset = jnp.arange(27)
    time_pos = jnp.arange(time_blocks)[:, None] + offset // 9 - 1
    row_pos = row_here + offset // 3 % 3 - 1
    col_pos = col_here + offset % 3 - 1
    inside = (time_pos >= 0) & (time_pos < time_blocks) & (row_pos >= 0) & (row_pos < ROW_BLOCKS)
    inside = inside & (col_pos >= 0) & (col_pos < col_blocks)
    allowed = inside & ((window_mask[0] == 1) | (offset == 13))

    def spread(grad_acc, contrib, frame_block):
        contrib = contrib.reshape(3, 3, 3, cube_cells, heads_local, HEAD_DIM)
        acc_slab = lax.dynamic_slice_in_dim(grad_acc, frame_block, 3, 0) + contrib
        return lax.dynamic_update_slice_in_dim(grad_acc, acc_slab, frame_block, 0)

    def one_block(accums, frame_block):
        key_acc, value_acc = accums
        key_row_matrix = lax.dynamic_slice_in_dim(key_pad, frame_block, 3, 0).reshape(
            1, 27 * cube_cells, heads_local, HEAD_DIM
        )
        value_row_matrix = lax.dynamic_slice_in_dim(value_pad, frame_block, 3, 0).reshape(
            1, 27 * cube_cells, heads_local, HEAD_DIM
        )
        rows_allowed = jnp.repeat(
            lax.dynamic_index_in_dim(allowed, frame_block, 0, keepdims=True), cube_cells, axis=1
        )
        query_row_matrix = lax.dynamic_index_in_dim(query_cubes, frame_block, 0, keepdims=True)
        gradient_row_values = lax.dynamic_index_in_dim(grad_cubes, frame_block, 0, keepdims=True)
        query_gradient, key_gradient, value_gradient = cube_grads(
            query_row_matrix, key_row_matrix, value_row_matrix, gradient_row_values, rows_allowed
        )
        key_acc = spread(key_acc, key_gradient, frame_block)
        value_acc = spread(value_acc, value_gradient, frame_block)
        return ((key_acc, value_acc), query_gradient[0].astype(jnp.bfloat16))

    acc_shape = (time_blocks + 2, 3, 3, cube_cells, heads_local, HEAD_DIM)
    zero_acc = jnp.zeros(acc_shape, jnp.float32)
    (key_acc, value_acc), query_gradient = lax.scan(
        one_block, (zero_acc, zero_acc), jnp.arange(time_blocks)
    )
    key_parts = lax.optimization_barrier(key_acc[1:-1].astype(jnp.bfloat16))
    value_parts = lax.optimization_barrier(value_acc[1:-1].astype(jnp.bfloat16))
    stacked = jnp.stack([key_parts, value_parts])
    total = stacked[:, :, 1, 1].astype(jnp.float32)
    for row_step in steps:
        for col_step in steps:
            if row_step != 0 or col_step != 0:
                arrived = from_behind(
                    stacked[:, :, row_step + 1, col_step + 1],
                    "ctx",
                    row_step * col_blocks + col_step,
                )
                total = total + arrived.astype(jnp.float32)
    summed = total.astype(jnp.bfloat16).reshape(2, 1, frames_all, TILE, TILE, channels)
    query_pillar = query_gradient.reshape(1, frames_all, TILE, TILE, channels)
    query_back, key_back, value_back = (
        lax.all_to_all(query_pillar, "ctx", split_axis=1, concat_axis=0, tiled=True),
        lax.all_to_all(summed[0], "ctx", split_axis=1, concat_axis=0, tiled=True),
        lax.all_to_all(summed[1], "ctx", split_axis=1, concat_axis=0, tiled=True),
    )
    return (from_pillars(query_back), from_pillars(key_back), from_pillars(value_back))


def solution(mesh):
    in_specs = (
        P("ctx", None, None, "head"),
        P("ctx", None, None, "head"),
        P("ctx", None, None, "head"),
        P("ctx", None, None, "head"),
        P("ctx", None, None),
    )
    out_specs = (
        P("ctx", None, None, "head"),
        P("ctx", None, None, "head"),
        P("ctx", None, None, "head"),
    )
    return jax.shard_map(shards, mesh=mesh, in_specs=in_specs, out_specs=out_specs, check_vma=False)
```

profile of v0, /device:TPU:1, one launch (start us, length us, event | category | flops | bytes accessed | tf_op | source)
XLA Modules:
  0.0 888.1 jit_solution(2487428702476224321)
XLA Ops:
  3.9 8.6 all-to-all-start.1
  13.5 13.3 %all-to-all-done.1 = bf16[32,1,4,4,768]{4,3,2,1,0:T(4,128)(2,1)S(1)} async-done(((bf16[32,1,4,4,768]{4,3,2,1,0:T(4,128)(2,1)}), bf16[32,1,4,4,768]{4,3,2,1,0:T(4,128)(2,1)S(1)}, u32[]{:S(2)}, u32[]{:S(2)}) %all-to-all-start.1) | async-done | bytes 786464 | tf_op jit(solution)/shard_map/all_to_all | solution.py:90
  26.8 17.8 %all_to_all.34 = bf16[32,1,4,4,768]{4,3,2,1,0:T(4,128)(2,1)S(1)} all-to-all(bf16[32,1,4,4,768]{4,3,2,1,0:T(4,128)(2,1)S(1)} %copy.92), channel_id=1, replica_groups=mesh['ctx'=32,'head'=4] {'ctx'}, dimensions={0} | all-to-all | bytes 1572864 | tf_op jit(solution)/shard_map/all_to_all | solution.py:91
  56.4 31.8 %collective-permute-done.7 = bf16[2,32,4,4,768]{4,3,2,1,0:T(4,128)(2,1)S(1)} collective-permute-done((bf16[2,32,4,4,768]{4,3,2,1,0:T(4,128)(2,1)}, bf16[2,32,4,4,768]{4,3,2,1,0:T(4,128)(2,1)S(1)}, u32[]{:S(2)}, u32[]{:S(2)}) %collective-permute-start.7) | collective-permute-done | bytes 1572896 | tf_op jit(solution)/shard_map/ppermute | solution.py:17
  90.6 27.6 %collective-permute-done.6 = bf16[2,32,4,4,768]{4,3,2,1,0:T(4,128)(2,1)S(1)} collective-permute-done((bf16[2,32,4,4,768]{4,3,2,1,0:T(4,128)(2,1)}, bf16[2,32,4,4,768]{4,3,2,1,0:T(4,128)(2,1)S(1)}, u32[]{:S(2)}, u32[]{:S(2)}) %collective-permute-start.6) | collective-permute-done | bytes 1572896 | tf_op jit(solution)/shard_map/ppermute | solution.py:17
  123.3 35.0 %collective-permute-start = (bf16[2,32,4,4,768]{4,3,2,1,0:T(4,128)(2,1)}, bf16[2,32,4,4,768]{4,3,2,1,0:T(4,128)(2,1)}, u32[]{:S(2)}, u32[]{:S(2)}) collective-permute-start(bf16[2,32,4,4,768]{4,3,2,1,0:T(4,128)(2,1)} %pad_maximum_fusion.1), channel_id=1, source_target_pairs={{0,68},{4,72},{8,76},{12,80},{16,84},{20,88},{24,92},{28,96},{32,1... | collective-permute-start | bytes 4718600 | tf_op jit(solution)/shard_map/ppermute | solution.py:17
  160.0 8.3 all-to-all-start
  172.1 76.2 %all-to-all-done = bf16[32,1,4,4,768]{4,3,2,1,0:T(4,128)(2,1)S(1)} async-done(((bf16[32,1,4,4,768]{4,3,2,1,0:T(4,128)(2,1)}), bf16[32,1,4,4,768]{4,3,2,1,0:T(4,128)(2,1)S(1)}, u32[]{:S(2)}, u32[]{:S(2)}) %all-to-all-start) | async-done | bytes 786464 | tf_op jit(solution)/shard_map/all_to_all | solution.py:88
  248.3 8.8 all-to-all-start.3
  258.7 12.5 %all-to-all-done.3 = bf16[32,1,4,4,768]{4,3,2,1,0:T(4,128)(2,1)} async-done(((bf16[32,1,4,4,768]{4,3,2,1,0:T(4,128)(2,1)}), bf16[32,1,4,4,768]{4,3,2,1,0:T(4,128)(2,1)}, u32[]{:S(2)}, u32[]{:S(2)}) %all-to-all-start.3) | async-done | bytes 786464 | tf_op jit(solution)/shard_map/all_to_all | solution.py:89
  278.5 4.1 stack.70
  282.6 4.1 stack.69
  286.7 4.1 stack.67
  290.7 4.1 stack.63
  294.8 4.1 stack.61
  298.9 4.1 stack.60
  303.0 4.1 stack.59
  307.1 9.3 %maximum_bitcast_fusion = bf16[2,8,3,3,64,6,128]{6,5,4,1,0,3,2:T(8,128)(2,1)S(1)} fusion(bf16[2,1,1,8,64,6,128]{6,5,4,3,0,2,1:T(8,128)(2,1)S(1)} %stack.71, bf16[2,1,1,8,64,6,128]{6,5,4,3,0,2,1:T(8,128)(2,1)} %stack.70, bf16[2,1,1,8,64,6,128]{6,5,4,3,0,2,1:T(8,128)(2,1)} %stack.69, bf16[2,1,1,8,64,6,128]{6,5,4,3,0,2,1:T(8,128)(2,1)} %stack.67, ...), kind=kLoop, calls=%fused_computation.60 | loop fusion | flops 63700992 | bytes 28311552 | tf_op jit(solution)/shard_map/transpose | solution.py:114
  316.4 11.4 %fusion.40 = (bf16[10,3,3,64,6,128]{5,4,3,0,2,1:T(8,128)(2,1)}, bf16[10,3,3,64,6,128]{5,4,3,0,2,1:T(8,128)(2,1)}) fusion(bf16[2,8,3,3,64,6,128]{6,5,4,1,0,3,2:T(8,128)(2,1)S(1)} %maximum_bitcast_fusion), kind=kLoop, calls=%fused_computation.64 | loop fusion | bytes 31850496 | tf_op jit(solution)/shard_map/squeeze | solution.py:118
  327.8 10.3 %copy.100 = bf16[10,3,3,64,6,128]{5,3,2,1,0,4:T(8,128)(2,1)} copy(bf16[10,3,3,64,6,128]{5,4,3,0,2,1:T(8,128)(2,1)} %get-tuple-element.114) | data formatting | bytes 17694720 | tf_op jit(solution)/shard_map/while | solution.py:158
  338.1 10.3 %copy.98 = bf16[10,3,3,64,6,128]{5,3,2,1,0,4:T(8,128)(2,1)} copy(bf16[10,3,3,64,6,128]{5,4,3,0,2,1:T(8,128)(2,1)} %get-tuple-element.115) | data formatting | bytes 17694720 | tf_op jit(solution)/shard_map/while | solution.py:158
  348.3 8.3 broadcast_in_dim.41.clone
  356.6 8.4 broadcast_in_dim.41
  365.0 265.4 %while.14 = (s32[]{:T(128)}, f32[10,3,3,64,6,128]{5,3,2,1,0,4:T(8,128)}, f32[10,3,3,64,6,128]{5,3,2,1,0,4:T(8,128)}, bf16[8,64,6,128]{3,1,2,0:T(8,128)(2,1)}, s3...) while((s32[]{:T(128)}, ...), condition=%wide.region_4.5_spmd, body=%wide.region_0.4_spmd.sunk | while | flops 1031357760 | bytes 100141512 | solution.py:158
  390.6 7.8 add_dynamic-update-slice_fusion.3
  423.7 7.8 add_dynamic-update-slice_fusion.3
  456.9 7.8 add_dynamic-update-slice_fusion.3
  490.1 7.8 add_dynamic-update-slice_fusion.3
  523.3 7.7 add_dynamic-update-slice_fusion.3
  556.4 7.7 add_dynamic-update-slice_fusion.3
  568.1 4.0 constant_dynamic-slice_fusion.6
  589.5 7.7 add_dynamic-update-slice_fusion.3
  601.2 4.0 constant_dynamic-slice_fusion.6
  622.6 7.8 add_dynamic-update-slice_fusion.3
  630.4 9.8 %slice.173 = bf16[8,3,3,64,6,128]{5,3,2,1,0,4:T(8,128)(2,1)} slice(f32[10,3,3,64,6,128]{5,3,2,1,0,4:T(8,128)} %get-tuple-element.58), slice={[1:9], [0:3], [0:3], [0:64], [0:6], [0:128]} | slice | bytes 14155776 | tf_op jit(solution)/shard_map/slice | solution.py:161
  640.3 9.8 %slice.172 = bf16[8,3,3,64,6,128]{5,3,2,1,0,4:T(8,128)(2,1)} slice(f32[10,3,3,64,6,128]{5,3,2,1,0,4:T(8,128)} %get-tuple-element.59), slice={[1:9], [0:3], [0:3], [0:64], [0:6], [0:128]} | slice | bytes 14155776 | tf_op jit(solution)/shard_map/slice | solution.py:162
  650.1 8.7 fusion.63
  668.5 31.6 %collective-permute-done.8 = bf16[2,8,64,6,128]{4,2,1,3,0:T(8,128)(2,1)S(1)} collective-permute-done((bf16[2,8,64,6,128]{4,2,1,3,0:T(8,128)(2,1)S(1)}, bf16[2,8,64,6,128]{4,2,1,3,0:T(8,128)(2,1)S(1)}, u32[]{:S(2)}, u32[]{:S(2)}) %collective-permute-start.8) | collective-permute-done | bytes 1572896 | tf_op jit(solution)/shard_map/ppermute | solution.py:17
  702.5 27.7 %collective-permute-done.9 = bf16[2,8,64,6,128]{4,2,1,3,0:T(8,128)(2,1)S(1)} collective-permute-done((bf16[2,8,64,6,128]{4,2,1,3,0:T(8,128)(2,1)S(1)}, bf16[2,8,64,6,128]{4,2,1,3,0:T(8,128)(2,1)S(1)}, u32[]{:S(2)}, u32[]{:S(2)}) %collective-permute-start.9) | collective-permute-done | bytes 1572896 | tf_op jit(solution)/shard_map/ppermute | solution.py:17
  730.2 6.5 collective-permute-start.15
  736.7 29.8 %collective-permute-start.14 = (bf16[2,8,64,6,128]{4,2,1,3,0:T(8,128)(2,1)}, bf16[2,8,64,6,128]{4,2,1,3,0:T(8,128)(2,1)}, u32[]{:S(2)}, u32[]{:S(2)}) collective-permute-start(bf16[2,8,64,6,128]{4,2,1,3,0:T(8,128)(2,1)} %get-tuple-element.123), channel_id=1, source_target_pairs={{0,64},{4,68},{8,72},{12,76},{16,80},{20,84},{24,88},{28,92},{32,9... | collective-permute-start | bytes 4718600 | tf_op jit(solution)/shard_map/ppermute | solution.py:17
  768.4 10.9 %all-to-all-start.4 = ((bf16[1,32,4,4,768]{4,3,2,0,1:T(4,128)(2,1)}), bf16[1,32,4,4,768]{4,3,2,0,1:T(4,128)(2,1)S(1)}, u32[]{:S(2)}, u32[]{:S(2)}) async-start(bf16[1,32,4,4,768]{4,3,2,0,1:T(4,128)(2,1)} %bitcast.35), calls=%async_computation.4 | async-start | bytes 1572864 | tf_op jit(solution)/shard_map/all_to_all | solution.py:177
  779.3 16.6 %collective-permute-done.14 = bf16[2,8,64,6,128]{4,2,1,3,0:T(8,128)(2,1)} collective-permute-done((bf16[2,8,64,6,128]{4,2,1,3,0:T(8,128)(2,1)}, bf16[2,8,64,6,128]{4,2,1,3,0:T(8,128)(2,1)}, u32[]{:S(2)}, u32[]{:S(2)}) %collective-permute-start.14) | collective-permute-done | bytes 1572896 | tf_op jit(solution)/shard_map/ppermute | solution.py:17
  795.9 6.2 fusion.48
  804.1 39.3 %all-to-all-done.4 = bf16[1,32,4,4,768]{4,3,2,0,1:T(4,128)(2,1)S(1)} async-done(((bf16[1,32,4,4,768]{4,3,2,0,1:T(4,128)(2,1)}), bf16[1,32,4,4,768]{4,3,2,0,1:T(4,128)(2,1)S(1)}, u32[]{:S(2)}, u32[]{:S(2)}) %all-to-all-start.4) | async-done | bytes 786464 | tf_op jit(solution)/shard_map/all_to_all | solution.py:177
  843.4 10.1 %all-to-all-start.6 = ((bf16[1,32,4,4,768]{4,3,2,0,1:T(4,128)(2,1)}), bf16[1,32,4,4,768]{4,3,2,0,1:T(4,128)(2,1)S(1)}, u32[]{:S(2)}, u32[]{:S(2)}) async-start(bf16[1,32,4,4,768]{4,3,2,0,1:T(4,128)(2,1)} %bitcast.52), calls=%async_computation.6 | async-start | bytes 1572864 | tf_op jit(solution)/shard_map/all_to_all | solution.py:179
  855.3 12.3 %all-to-all-done.6 = bf16[1,32,4,4,768]{4,3,2,0,1:T(4,128)(2,1)S(1)} async-done(((bf16[1,32,4,4,768]{4,3,2,0,1:T(4,128)(2,1)}), bf16[1,32,4,4,768]{4,3,2,0,1:T(4,128)(2,1)S(1)}, u32[]{:S(2)}, u32[]{:S(2)}) %all-to-all-start.6) | async-done | bytes 786464 | tf_op jit(solution)/shard_map/all_to_all | solution.py:179
  875.3 10.4 %all-to-all-done.5 = bf16[1,32,4,4,768]{4,3,2,0,1:T(4,128)(2,1)S(1)} async-done(((bf16[1,32,4,4,768]{4,3,2,0,1:T(4,128)(2,1)}), bf16[1,32,4,4,768]{4,3,2,0,1:T(4,128)(2,1)S(1)}, u32[]{:S(2)}, u32[]{:S(2)}) %all-to-all-start.5) | async-done | bytes 786464 | tf_op jit(solution)/shard_map/all_to_all | solution.py:178
  (214 shorter events, 234.9 us)
Async XLA Ops:
  2.3 10.2 %copy-start.7 = (bf16[1,8,64,768]{3,2,1,0:T(8,128)(2,1)S(1)}, bf16[1,8,64,768]{3,2,1,0:T(8,128)(2,1)}, u32[]{:S(2)}) copy-start(bf16[1,8,64,768]{3,2,1,0:T(8,128)(2,1)} %param.9) | copy-start | bytes 2359300
  3.9 22.8 %all-to-all-start.1 = ((bf16[32,1,4,4,768]{4,3,2,1,0:T(4,128)(2,1)}), bf16[32,1,4,4,768]{4,3,2,1,0:T(4,128)(2,1)S(1)}, u32[]{:S(2)}, u32[]{:S(2)}) async-start(bf16[32,1,4,4,768]{4,3,2,1,0:T(4,128)(2,1)} %copy.90), calls=%async_computation.1 | async-start | bytes 1572864 | tf_op jit(solution)/shard_map/all_to_all | solution.py:90
  13.5 144.8 %copy-start.8 = (bf16[1,8,64,768]{3,2,1,0:T(8,128)(2,1)S(1)}, bf16[1,8,64,768]{3,2,1,0:T(8,128)(2,1)}, u32[]{:S(2)}) copy-start(bf16[1,8,64,768]{3,2,1,0:T(8,128)(2,1)} %param.7) | copy-start | bytes 2359300
  46.9 41.3 %collective-permute-start.7 = (bf16[2,32,4,4,768]{4,3,2,1,0:T(4,128)(2,1)}, bf16[2,32,4,4,768]{4,3,2,1,0:T(4,128)(2,1)S(1)}, u32[]{:S(2)}, u32[]{:S(2)}) collective-permute-start(bf16[2,32,4,4,768]{4,3,2,1,0:T(4,128)(2,1)} %pad_maximum_fusion.1), channel_id=1, source_target_pairs={{68,0},{72,4},{76,8},{80,12},{84,16},{88,20},{92,24},{96,28},{100,... | collective-permute-start | bytes 4718600 | tf_op jit(solution)/shard_map/ppermute | solution.py:17
  48.2 70.0 %collective-permute-start.6 = (bf16[2,32,4,4,768]{4,3,2,1,0:T(4,128)(2,1)}, bf16[2,32,4,4,768]{4,3,2,1,0:T(4,128)(2,1)S(1)}, u32[]{:S(2)}, u32[]{:S(2)}) collective-permute-start(bf16[2,32,4,4,768]{4,3,2,1,0:T(4,128)(2,1)} %pad_maximum_fusion.1), channel_id=1, source_target_pairs={{64,0},{68,4},{72,8},{76,12},{80,16},{84,20},{88,24},{92,28},{96,3... | collective-permute-start | bytes 4718600 | tf_op jit(solution)/shard_map/ppermute | solution.py:17
  49.5 72.6 %collective-permute-start.5 = (bf16[2,32,4,4,768]{4,3,2,1,0:T(4,128)(2,1)}, bf16[2,32,4,4,768]{4,3,2,1,0:T(4,128)(2,1)S(1)}, u32[]{:S(2)}, u32[]{:S(2)}) collective-permute-start(bf16[2,32,4,4,768]{4,3,2,1,0:T(4,128)(2,1)} %pad_maximum_fusion.1), channel_id=1, source_target_pairs={{60,0},{64,4},{68,8},{72,12},{76,16},{80,20},{84,24},{88,28},{92,3... | collective-permute-start | bytes 4718600 | tf_op jit(solution)/shard_map/ppermute | solution.py:17
  50.8 235.9 %collective-permute-start.4 = (bf16[2,32,4,4,768]{4,3,2,1,0:T(4,128)(2,1)}, bf16[2,32,4,4,768]{4,3,2,1,0:T(4,128)(2,1)}, u32[]{:S(2)}, u32[]{:S(2)}) collective-permute-start(bf16[2,32,4,4,768]{4,3,2,1,0:T(4,128)(2,1)} %pad_maximum_fusion.1), channel_id=1, source_target_pairs={{4,0},{8,4},{12,8},{16,12},{20,16},{24,20},{28,24},{32,28},{36,32}... | collective-permute-start | bytes 4718600 | tf_op jit(solution)/shard_map/ppermute | solution.py:17
  52.7 238.0 %collective-permute-start.3 = (bf16[2,32,4,4,768]{4,3,2,1,0:T(4,128)(2,1)}, bf16[2,32,4,4,768]{4,3,2,1,0:T(4,128)(2,1)}, u32[]{:S(2)}, u32[]{:S(2)}) collective-permute-start(bf16[2,32,4,4,768]{4,3,2,1,0:T(4,128)(2,1)} %pad_maximum_fusion.1), channel_id=1, source_target_pairs={{0,4},{4,8},{8,12},{12,16},{16,20},{20,24},{24,28},{28,32},{32,36}... | collective-permute-start | bytes 4718600 | tf_op jit(solution)/shard_map/ppermute | solution.py:17
  88.1 34.0 %copy-start.1 = (bf16[2,32,4,4,768]{4,3,2,1,0:T(4,128)(2,1)}, bf16[2,32,4,4,768]{4,3,2,1,0:T(4,128)(2,1)S(1)}, u32[]{:S(2)}) copy-start(bf16[2,32,4,4,768]{4,3,2,1,0:T(4,128)(2,1)S(1)} %collective-permute-done.7) | copy-start | bytes 4718596
  88.1 206.7 %collective-permute-start.2 = (bf16[2,32,4,4,768]{4,3,2,1,0:T(4,128)(2,1)}, bf16[2,32,4,4,768]{4,3,2,1,0:T(4,128)(2,1)}, u32[]{:S(2)}, u32[]{:S(2)}) collective-permute-start(bf16[2,32,4,4,768]{4,3,2,1,0:T(4,128)(2,1)} %pad_maximum_fusion.1), channel_id=1, source_target_pairs={{0,60},{4,64},{8,68},{12,72},{16,76},{20,80},{24,84},{28,88},{32,9... | collective-permute-start | bytes 4718600 | tf_op jit(solution)/shard_map/ppermute | solution.py:17
  118.2 3.9 copy-start.2
  118.2 180.7 %collective-permute-start.1 = (bf16[2,32,4,4,768]{4,3,2,1,0:T(4,128)(2,1)}, bf16[2,32,4,4,768]{4,3,2,1,0:T(4,128)(2,1)}, u32[]{:S(2)}, u32[]{:S(2)}) collective-permute-start(bf16[2,32,4,4,768]{4,3,2,1,0:T(4,128)(2,1)} %pad_maximum_fusion.1), channel_id=1, source_target_pairs={{0,64},{4,68},{8,72},{12,76},{16,80},{20,84},{24,88},{28,92},{32,9... | collective-permute-start | bytes 4718600 | tf_op jit(solution)/shard_map/ppermute | solution.py:17
  122.1 1.2 copy-start.3
  123.3 179.7 %collective-permute-start = (bf16[2,32,4,4,768]{4,3,2,1,0:T(4,128)(2,1)}, bf16[2,32,4,4,768]{4,3,2,1,0:T(4,128)(2,1)}, u32[]{:S(2)}, u32[]{:S(2)}) collective-permute-start(bf16[2,32,4,4,768]{4,3,2,1,0:T(4,128)(2,1)} %pad_maximum_fusion.1), channel_id=1, source_target_pairs={{0,68},{4,72},{8,76},{12,80},{16,84},{20,88},{24,92},{28,96},{32,1... | collective-permute-start | bytes 4718600 | tf_op jit(solution)/shard_map/ppermute | solution.py:17
  158.5 9.8 %copy-start.9 = (bf16[1,8,64,768]{3,2,1,0:T(8,128)(2,1)S(1)}, bf16[1,8,64,768]{3,2,1,0:T(8,128)(2,1)}, u32[]{:S(2)}) copy-start(bf16[1,8,64,768]{3,2,1,0:T(8,128)(2,1)} %param.10) | copy-start | bytes 2359300
  160.0 88.3 %all-to-all-start = ((bf16[32,1,4,4,768]{4,3,2,1,0:T(4,128)(2,1)}), bf16[32,1,4,4,768]{4,3,2,1,0:T(4,128)(2,1)S(1)}, u32[]{:S(2)}, u32[]{:S(2)}) async-start(bf16[32,1,4,4,768]{4,3,2,1,0:T(4,128)(2,1)} %copy.88), calls=%async_computation | async-start | bytes 1572864 | tf_op jit(solution)/shard_map/all_to_all | solution.py:88
  169.4 87.8 %copy-start.10 = (s32[1,8,27]{2,1,0:T(8,128)S(1)}, s32[1,8,27]{2,1,0:T(8,128)}, u32[]{:S(2)}) copy-start(s32[1,8,27]{2,1,0:T(8,128)} %param.11) | copy-start | bytes 2596
  248.3 22.9 %all-to-all-start.3 = ((bf16[32,1,4,4,768]{4,3,2,1,0:T(4,128)(2,1)}), bf16[32,1,4,4,768]{4,3,2,1,0:T(4,128)(2,1)}, u32[]{:S(2)}, u32[]{:S(2)}) async-start(bf16[32,1,4,4,768]{4,3,2,1,0:T(4,128)(2,1)} %copy.96), calls=%async_computation.3 | async-start | bytes 1572864 | tf_op jit(solution)/shard_map/all_to_all | solution.py:89
  379.2 3.4 copy-start
  379.2 4.2 copy-start.11
  412.3 3.4 copy-start
  412.3 4.2 copy-start.11
  445.5 3.4 copy-start
  445.5 4.2 copy-start.11
  478.7 3.4 copy-start
  478.7 4.2 copy-start.11
  511.8 3.4 copy-start
  511.8 4.2 copy-start.11
  545.0 3.4 copy-start
  545.0 4.2 copy-start.11
  578.1 3.4 copy-start
  578.1 4.2 copy-start.11
  611.2 3.4 copy-start
  611.2 4.2 copy-start.11
  650.1 116.4 %copy-start.6 = (bf16[8,64,6,128]{3,1,2,0:T(8,128)(2,1)S(1)}, bf16[8,64,6,128]{3,1,2,0:T(8,128)(2,1)}, u32[]{:S(2)}) copy-start(bf16[8,64,6,128]{3,1,2,0:T(8,128)(2,1)} %get-tuple-element.57) | copy-start | bytes 2359300
  658.8 41.3 %collective-permute-start.8 = (bf16[2,8,64,6,128]{4,2,1,3,0:T(8,128)(2,1)S(1)}, bf16[2,8,64,6,128]{4,2,1,3,0:T(8,128)(2,1)S(1)}, u32[]{:S(2)}, u32[]{:S(2)}) collective-permute-start(bf16[2,8,64,6,128]{4,2,1,3,0:T(8,128)(2,1)S(1)} %get-tuple-element.116), channel_id=1, source_target_pairs={{68,0},{72,4},{76,8},{80,12},{84,16},{88,20},{92,24},{96,28},{100,... | collective-permute-start | bytes 4718600 | tf_op jit(solution)/shard_map/ppermute | solution.py:17
  660.3 69.9 %collective-permute-start.9 = (bf16[2,8,64,6,128]{4,2,1,3,0:T(8,128)(2,1)S(1)}, bf16[2,8,64,6,128]{4,2,1,3,0:T(8,128)(2,1)S(1)}, u32[]{:S(2)}, u32[]{:S(2)}) collective-permute-start(bf16[2,8,64,6,128]{4,2,1,3,0:T(8,128)(2,1)S(1)} %get-tuple-element.117), channel_id=1, source_target_pairs={{64,0},{68,4},{72,8},{76,12},{80,16},{84,20},{88,24},{92,28},{96,3... | collective-permute-start | bytes 4718600 | tf_op jit(solution)/shard_map/ppermute | solution.py:17
  661.6 75.1 %collective-permute-start.10 = (bf16[2,8,64,6,128]{4,2,1,3,0:T(8,128)(2,1)S(1)}, bf16[2,8,64,6,128]{4,2,1,3,0:T(8,128)(2,1)S(1)}, u32[]{:S(2)}, u32[]{:S(2)}) collective-permute-start(bf16[2,8,64,6,128]{4,2,1,3,0:T(8,128)(2,1)S(1)} %get-tuple-element.118), channel_id=1, source_target_pairs={{60,0},{64,4},{68,8},{72,12},{76,16},{80,20},{84,24},{88,28},{92,3... | collective-permute-start | bytes 4718600 | tf_op jit(solution)/shard_map/ppermute | solution.py:17
  662.9 116.3 %collective-permute-start.11 = (bf16[2,8,64,6,128]{4,2,1,3,0:T(8,128)(2,1)}, bf16[2,8,64,6,128]{4,2,1,3,0:T(8,128)(2,1)}, u32[]{:S(2)}, u32[]{:S(2)}) collective-permute-start(bf16[2,8,64,6,128]{4,2,1,3,0:T(8,128)(2,1)} %get-tuple-element.119), channel_id=1, source_target_pairs={{4,0},{8,4},{12,8},{16,12},{20,16},{24,20},{28,24},{32,28},{36,32}... | collective-permute-start | bytes 4718600 | tf_op jit(solution)/shard_map/ppermute | solution.py:17
  664.8 114.4 %collective-permute-start.12 = (bf16[2,8,64,6,128]{4,2,1,3,0:T(8,128)(2,1)}, bf16[2,8,64,6,128]{4,2,1,3,0:T(8,128)(2,1)}, u32[]{:S(2)}, u32[]{:S(2)}) collective-permute-start(bf16[2,8,64,6,128]{4,2,1,3,0:T(8,128)(2,1)} %get-tuple-element.120), channel_id=1, source_target_pairs={{0,4},{4,8},{8,12},{12,16},{16,20},{20,24},{24,28},{28,32},{32,36}... | collective-permute-start | bytes 4718600 | tf_op jit(solution)/shard_map/ppermute | solution.py:17
  700.0 79.2 %collective-permute-start.13 = (bf16[2,8,64,6,128]{4,2,1,3,0:T(8,128)(2,1)}, bf16[2,8,64,6,128]{4,2,1,3,0:T(8,128)(2,1)}, u32[]{:S(2)}, u32[]{:S(2)}) collective-permute-start(bf16[2,8,64,6,128]{4,2,1,3,0:T(8,128)(2,1)} %get-tuple-element.121), channel_id=1, source_target_pairs={{0,60},{4,64},{8,68},{12,72},{16,76},{20,80},{24,84},{28,88},{32,9... | collective-permute-start | bytes 4718600 | tf_op jit(solution)/shard_map/ppermute | solution.py:17
  730.2 36.3 %copy-start.4 = (bf16[2,8,64,6,128]{4,2,1,3,0:T(8,128)(2,1)}, bf16[2,8,64,6,128]{4,2,1,3,0:T(8,128)(2,1)S(1)}, u32[]{:S(2)}) copy-start(bf16[2,8,64,6,128]{4,2,1,3,0:T(8,128)(2,1)S(1)} %collective-permute-done.9) | copy-start | bytes 4718596
  730.2 49.1 %collective-permute-start.15 = (bf16[2,8,64,6,128]{4,2,1,3,0:T(8,128)(2,1)}, bf16[2,8,64,6,128]{4,2,1,3,0:T(8,128)(2,1)}, u32[]{:S(2)}, u32[]{:S(2)}) collective-permute-start(bf16[2,8,64,6,128]{4,2,1,3,0:T(8,128)(2,1)} %get-tuple-element.122), channel_id=1, source_target_pairs={{0,68},{4,72},{8,76},{12,80},{16,84},{20,88},{24,92},{28,96},{32,1... | collective-permute-start | bytes 4718600 | tf_op jit(solution)/shard_map/ppermute | solution.py:17
  736.7 29.8 %copy-start.5 = (bf16[2,8,64,6,128]{4,2,1,3,0:T(8,128)(2,1)}, bf16[2,8,64,6,128]{4,2,1,3,0:T(8,128)(2,1)S(1)}, u32[]{:S(2)}) copy-start(bf16[2,8,64,6,128]{4,2,1,3,0:T(8,128)(2,1)S(1)} %collective-permute-done.10) | copy-start | bytes 4718596
  736.7 59.1 %collective-permute-start.14 = (bf16[2,8,64,6,128]{4,2,1,3,0:T(8,128)(2,1)}, bf16[2,8,64,6,128]{4,2,1,3,0:T(8,128)(2,1)}, u32[]{:S(2)}, u32[]{:S(2)}) collective-permute-start(bf16[2,8,64,6,128]{4,2,1,3,0:T(8,128)(2,1)} %get-tuple-element.123), channel_id=1, source_target_pairs={{0,64},{4,68},{8,72},{12,76},{16,80},{20,84},{24,88},{28,92},{32,9... | collective-permute-start | bytes 4718600 | tf_op jit(solution)/shard_map/ppermute | solution.py:17
  768.4 75.0 %all-to-all-start.4 = ((bf16[1,32,4,4,768]{4,3,2,0,1:T(4,128)(2,1)}), bf16[1,32,4,4,768]{4,3,2,0,1:T(4,128)(2,1)S(1)}, u32[]{:S(2)}, u32[]{:S(2)}) async-start(bf16[1,32,4,4,768]{4,3,2,0,1:T(4,128)(2,1)} %bitcast.35), calls=%async_computation.4 | async-start | bytes 1572864 | tf_op jit(solution)/shard_map/all_to_all | solution.py:177
  843.4 24.3 %all-to-all-start.6 = ((bf16[1,32,4,4,768]{4,3,2,0,1:T(4,128)(2,1)}), bf16[1,32,4,4,768]{4,3,2,0,1:T(4,128)(2,1)S(1)}, u32[]{:S(2)}, u32[]{:S(2)}) async-start(bf16[1,32,4,4,768]{4,3,2,0,1:T(4,128)(2,1)} %bitcast.52), calls=%async_computation.6 | async-start | bytes 1572864 | tf_op jit(solution)/shard_map/all_to_all | solution.py:179
  867.7 18.1 %all-to-all-start.5 = ((bf16[1,32,4,4,768]{4,3,2,0,1:T(4,128)(2,1)}), bf16[1,32,4,4,768]{4,3,2,0,1:T(4,128)(2,1)S(1)}, u32[]{:S(2)}, u32[]{:S(2)}) async-start(bf16[1,32,4,4,768]{4,3,2,0,1:T(4,128)(2,1)} %bitcast.49), calls=%async_computation.5 | async-start | bytes 1572864 | tf_op jit(solution)/shard_map/all_to_all | solution.py:178
where the time goes:
time: 898 us; the launch traced here: 888 us
  waiting for transfers between devices  301 us (34%)
  local copies, waits for them, and re-layouts  191 us (21%)
  starting transfers between devices  148 us (16%)
  matrix products  114 us (13%)
  other arithmetic  88.7 us (10%)
  loops' own time  25.5 us (3%)
  blocking collectives  17.8 us (2%)
    ppermute x16, waiting for transfers between devices, from_behind(): return lax.ppermute(shard, axis, pairs)  137 us
    ppermute x16, starting transfers between devices, from_behind(): return lax.ppermute(shard, axis, pairs)  97.9 us
    all_to_all x1, waiting for transfers between devices, shards(): lax.all_to_all(to_pillars(queries), 'ctx', split_axis=0, concat_axis=1, t...  76.2 us
    dynamic_update_slice x8, other arithmetic, spread(): return lax.dynamic_update_slice_in_dim(grad_acc, acc_slab, frame_block, 0)  62.2 us
    all_to_all x1, waiting for transfers between devices, shards(): lax.all_to_all(query_pillar, 'ctx', split_axis=1, concat_axis=0, tiled=True)  39.3 us
    dynamic_slice x8, local copies, waits for them, and re-layouts, one_block(): lax.dynamic_slice_in_dim(value_pad, frame_block, 3, 0)  32.1 us
    another operation x8, local copies, waits for them, and re-layouts, shards(): jnp.stack([joined if row_step == 0 and col_step == 0 else from_behind(joi...  31.4 us
    sub x8, matrix products, cube_grads(): weights = jnp.where(mask_rows, jnp.exp(score_matrix - row_max), 0.0)  29.5 us
  transfers between devices with their start and end apart: 22, of which 12 were waited for; matrix products, arithmetic and copies ran while one was open for 6% of the time, Pallas kernels for 0%

commit v1 on v0

v1 whole, which is shorter than its diff:
```python
import functools

import jax
import jax.numpy as jnp
from jax import lax
from jax.experimental import pallas as pl
from jax.experimental.pallas import tpu as pltpu
from jax.sharding import PartitionSpec as P

HEAD_DIM = 128
TILE = 4
ROW_BLOCKS = 2
NEG_FILL = -1e30
SCALE = HEAD_DIM ** (-0.5)
LOG2E = 1.4426950408889634
HEADS_LOCAL = 3
BLOCK = ROW_BLOCKS * TILE**3
STEPS = (-1, 0, 1)

XS, HALVES, STRIPS, CORES = 4, 2, 2, 2


def ctx_of(x, half, strip, core):
    return ((x * HALVES + half) * STRIPS + strip) * CORES + core


def swap_pairs():
    return [(i, i ^ 1) for i in range(32)]


def chain_pairs():
    pairs = []
    for half in range(HALVES):
        for link in range(XS * STRIPS - 1):
            a = ctx_of(link % XS, half, link // XS, 1)
            b = ctx_of((link + 1) % XS, half, (link + 1) // XS, 0)
            pairs += [(a, b), (b, a)]
    return pairs


def to_columns(tensor):
    frames, height, width, channels = tensor.shape
    shaped = tensor.reshape(height, STRIPS, XS, CORES, TILE, HALVES, channels // HALVES)
    shaped = shaped.transpose(2, 5, 1, 3, 0, 4, 6)
    return shaped.reshape(32, height * TILE, channels // HALVES)


def from_columns(arrived):
    channels = arrived.shape[-1]
    shaped = arrived.reshape(XS, HALVES, STRIPS, CORES, 8, TILE, channels)
    shaped = shaped.transpose(4, 2, 0, 3, 5, 1, 6)
    return shaped.reshape(1, 8, 64, HALVES * channels)


def mask_bias(window_mask):
    place = lax.axis_index("ctx")
    x, strip, core = place // 8, place // 2 % 2, place % 2
    col = strip * 8 + x * 2 + core
    every = lax.all_gather(window_mask, "ctx", tiled=True)
    time_blocks = every.shape[1]
    rows = jnp.stack([lax.dynamic_index_in_dim(every, col + 16 * r, 0, keepdims=False) for r in range(ROW_BLOCKS)])
    rows = rows.reshape(ROW_BLOCKS, time_blocks, 3, 3, 3) == 1
    time_pos = jnp.arange(time_blocks)
    has_left = col > 0
    has_right = col < 15
    per_query_row = []
    for rq in range(ROW_BLOCKS):
        per_dt = []
        for dt in range(3):
            inside_t = (time_pos + dt - 1 >= 0) & (time_pos + dt - 1 < time_blocks)
            per_block = []
            for block in range(3):
                per_key_row = []
                for rk in range(ROW_BLOCKS):
                    window = rows[rq, :, dt, rk - rq + 1]
                    left = window[:, 0] & has_left
                    right = window[:, 2] & has_right
                    if block == 0:
                        allowed = window[:, 1]
                        if dt == 1 and rk == rq:
                            allowed = jnp.ones_like(allowed)
                    elif block == 1:
                        allowed = jnp.where(core == 0, right, left)
                    else:
                        allowed = jnp.where(core == 0, left, right)
                    per_key_row.append(allowed & inside_t)
                per_block.append(jnp.stack(per_key_row, axis=1))
            per_dt.append(jnp.stack(per_block, axis=1))
        per_query_row.append(jnp.stack(per_dt, axis=1))
    allowed = jnp.stack(per_query_row, axis=-1).reshape(time_blocks, 18, ROW_BLOCKS)
    bias = jnp.where(allowed, 0.0, NEG_FILL).astype(jnp.float32)
    bias = jnp.broadcast_to(bias[:, :, None, :, None], (time_blocks, 18, TILE, ROW_BLOCKS, TILE * TILE))
    return bias.reshape(time_blocks, 18, BLOCK)


def grads_kernel(bias_ref, q_ref, g_ref, k0, v0, k1, v1, k2, v2, dq_ref, o0, o1, o2, a0, a1, a2):
    time_blocks = bias_ref.shape[0]
    accs = (a0, a1, a2)
    for acc in accs:
        acc[...] = jnp.zeros_like(acc)
    pairs = ((k0, v0), (k1, v1), (k2, v2))

    def one_block(t, _):
        here = pl.ds(pl.multiple_of(t * BLOCK, BLOCK), BLOCK)
        q = q_ref[here, :]
        g = g_ref[here, :]
        zero = jnp.zeros_like(q)
        both = jnp.concatenate(
            [jnp.concatenate([q, zero], axis=1), jnp.concatenate([zero, g], axis=1)], axis=0
        )
        at = []
        for dt in STEPS:
            near = jnp.clip(t + dt, 0, time_blocks - 1)
            at.append(pl.ds(pl.multiple_of(near * BLOCK, BLOCK), BLOCK))
        scores, probs, keys = [], [], []
        top = None
        for dt in range(3):
            for block, (k_ref, v_ref) in enumerate(pairs):
                k = k_ref[at[dt], :]
                kv = jnp.concatenate([k, v_ref[at[dt], :]], axis=1)
                r = lax.dot_general(kv, both, (((1,), (1,)), ((), ())), preferred_element_type=jnp.float32)
                rows = []
                for rk in range(ROW_BLOCKS):
                    row = (dt * 3 + block) * 2 + rk
                    rows.append(jnp.broadcast_to(bias_ref[t, row : row + 1, :], (16, BLOCK)))
                bias = jnp.concatenate(rows * TILE, axis=0)
                s = r[:, :BLOCK] * (SCALE * LOG2E) + bias
                here_top = jnp.max(s, axis=0, keepdims=True)
                top = here_top if top is None else jnp.maximum(top, here_top)
                scores.append(s)
                probs.append(r[:, BLOCK:])
                keys.append(k)
        total = jnp.zeros((1, BLOCK), jnp.float32)
        dots = jnp.zeros((1, BLOCK), jnp.float32)
        weights = []
        for s, pg in zip(scores, probs):
            e = jnp.exp2(s - top)
            total += jnp.sum(e, axis=0, keepdims=True)
            dots += jnp.sum(e * pg, axis=0, keepdims=True)
            weights.append(e)
        inv = 1.0 / total
        row_dot = dots * inv
        dqt = jnp.zeros((HEAD_DIM, BLOCK), jnp.float32)
        for n, (e, pg, k) in enumerate(zip(weights, probs, keys)):
            p = e * inv
            ds = (p * (pg - row_dot) * SCALE).astype(jnp.bfloat16)
            pair = jnp.concatenate([ds, p.astype(jnp.bfloat16)], axis=1)
            dkv = jnp.dot(pair, both, preferred_element_type=jnp.float32)
            dt, block = n // 3, n % 3
            accs[block][at[dt], :] += dkv
            dqt += lax.dot_general(k, ds, (((0,), (0,)), ((), ())), preferred_element_type=jnp.float32)
        dq_ref[here, :] = dqt.T.astype(jnp.bfloat16)
        return 0

    lax.fori_loop(0, time_blocks, one_block, 0)
    for acc, out in zip(accs, (o0, o1, o2)):
        out[...] = acc[...].astype(jnp.bfloat16)


def column_grads(bias, qg, own, near, far):
    rows = qg.shape[0]
    first = pl.BlockSpec((rows, HEAD_DIM), lambda h: (0, h))
    second = pl.BlockSpec((rows, HEAD_DIM), lambda h: (0, h + HEADS_LOCAL))
    pair = pl.BlockSpec((rows, 2 * HEAD_DIM), lambda h: (0, h))
    out = jax.ShapeDtypeStruct((rows, 2 * HEADS_LOCAL * HEAD_DIM), jnp.bfloat16)
    return pl.pallas_call(
        grads_kernel,
        grid=(HEADS_LOCAL,),
        in_specs=[pl.BlockSpec(bias.shape, lambda h: (0, 0, 0))] + [first, second] * 4,
        out_specs=[first, pair, pair, pair],
        out_shape=[jax.ShapeDtypeStruct((rows, HEADS_LOCAL * HEAD_DIM), jnp.bfloat16), out, out, out],
        scratch_shapes=[pltpu.VMEM((rows, 2 * HEAD_DIM), jnp.float32)] * 3,
        compiler_params=pltpu.CompilerParams(vmem_limit_bytes=48 * 1024 * 1024),
        cost_estimate=pl.CostEstimate(flops=20_000_000_000, bytes_accessed=20_000_000, transcendentals=4_000_000),
        name="column_grads",
    )(bias, qg, qg, own, own, near, near, far, far)


def shards(queries, keys, values, out_grad, window_mask):
    swap, chain = swap_pairs(), chain_pairs()
    bias = mask_bias(window_mask)
    exchange = functools.partial(lax.all_to_all, axis_name="ctx", split_axis=0, concat_axis=0, tiled=True)
    kv = exchange(jnp.concatenate([to_columns(keys), to_columns(values)], axis=-1)).reshape(1024, 768)
    near = lax.ppermute(kv, "ctx", swap)
    far = lax.ppermute(kv, "ctx", chain)
    qg = exchange(jnp.concatenate([to_columns(queries), to_columns(out_grad)], axis=-1)).reshape(1024, 768)
    dq, own, to_near, to_far = column_grads(bias, qg, kv, near, far)
    from_near = lax.ppermute(to_near, "ctx", swap)
    from_far = lax.ppermute(to_far, "ctx", chain)
    dq_back = exchange(dq.reshape(32, 32, 384))
    total = own.astype(jnp.float32) + from_near.astype(jnp.float32) + from_far.astype(jnp.float32)
    dkv_back = exchange(total.astype(jnp.bfloat16).reshape(32, 32, 768)).reshape(32, 32, 3, 2, 128)
    dk = dkv_back[:, :, :, 0].reshape(32, 32, 384)
    dv = dkv_back[:, :, :, 1].reshape(32, 32, 384)
    return from_columns(dq_back), from_columns(dk), from_columns(dv)


def solution(mesh):
    tokens = P("ctx", None, None, "head")
    return jax.shard_map(
        shards,
        mesh=mesh,
        in_specs=(tokens, tokens, tokens, tokens, P("ctx", None, None)),
        out_specs=(tokens, tokens, tokens),
        check_vma=False,
    )
```

time: 898 us -> 213 us (0.24); the launches traced: 888 us -> 212 us
  waiting for transfers between devices: 301 us -> 70.3 us
  local copies, waits for them, and re-layouts: 191 us -> 30.4 us
  starting transfers between devices: 148 us -> 32.9 us
  matrix products: 114 us -> 0 us
  other arithmetic: 88.7 us -> 6.69 us
  Pallas kernels: 0 us -> 33 us
  loops' own time: 25.5 us -> 0 us
  blocking collectives: 17.8 us -> 37.9 us
    all_to_all x6 -> x4, waiting for transfers between devices: 164 us -> 41.8 us  [the longest x1 18.5 us: shards(): exchange(total.astype(jnp.bfloat16).reshape(32, 32, 768))]
    ppermute x16 -> x4, waiting for transfers between devices: 137 us -> 28.5 us  [the longest x1 14.8 us: shards(): from_far = lax.ppermute(to_far, 'ctx', chain)]
    ppermute x16 -> x4, starting transfers between devices: 97.9 us -> 6.97 us  [the longest x1 3.54 us: shards(): far = lax.ppermute(kv, 'ctx', chain)]
    dot_general x40 -> x0, matrix products: 85 us -> none  [the longest x8 27.5 us: cube_grads(): jnp.einsum('thqk,tkhd->tqhd', attention_lower_precision, value_row_matrix...]
    dynamic_update_slice x8 -> x0, other arithmetic: 62.2 us -> none  [spread(): return lax.dynamic_update_slice_in_dim(grad_acc, acc_slab, frame_block, 0)]
    dynamic_slice x32 -> x1, local copies, waits for them, and re-layouts: 55.8 us -> 0.01 us  [mask_bias(): lax.dynamic_index_in_dim(every, col + 16 * r, 0, keepdims=False)]
    all_gather x0 -> x1, blocking collectives: none -> 37.9 us  [mask_bias(): every = lax.all_gather(window_mask, 'ctx', tiled=True)]
    pallas_call x0 -> x1, Pallas kernels: none -> 33 us  [column_grads(): pl.pallas_call(grads_kernel, grid=(HEADS_LOCAL,), in_specs=[pl.BlockSpec(...]
  transfers between devices with their start and end apart: 22 -> 8, of which waited for: 12 -> 5; matrix products, arithmetic and copies ran while one was open for 6% -> 6% of each run, Pallas kernels for 0% -> 0%
where the time goes in v1:
time: 213 us; the launch traced here: 212 us
  waiting for transfers between devices  70.3 us (33%)
  blocking collectives  37.9 us (18%)
  Pallas kernels  33 us (15%)
  starting transfers between devices  32.9 us (15%)
  local copies, waits for them, and re-layouts  30.4 us (14%)
  other arithmetic  6.69 us (3%)
    all_gather x1, blocking collectives, mask_bias(): every = lax.all_gather(window_mask, 'ctx', tiled=True)  37.9 us
    pallas_call x1, Pallas kernels, column_grads(): pl.pallas_call(grads_kernel, grid=(HEADS_LOCAL,), in_specs=[pl.BlockSpec(...  33 us
    all_to_all x1, waiting for transfers between devices, shards(): exchange(total.astype(jnp.bfloat16).reshape(32, 32, 768))  18.5 us
    all_to_all x1, waiting for transfers between devices, shards(): exchange(jnp.concatenate([to_columns(queries), to_columns(out_grad)], axi...  17.3 us
    ppermute x1, waiting for transfers between devices, shards(): from_far = lax.ppermute(to_far, 'ctx', chain)  14.8 us
    ppermute x1, waiting for transfers between devices, shards(): far = lax.ppermute(kv, 'ctx', chain)  13.7 us
    slice x1, local copies, waits for them, and re-layouts, shards(): dv = dkv_back[:, :, :, 1].reshape(32, 32, 384)  9.89 us
    all_to_all x1, starting transfers between devices, shards(): exchange(jnp.concatenate([to_columns(keys), to_columns(values)], axis=-1))  8.77 us
  transfers between devices with their start and end apart: 8, of which 5 were waited for; matrix products, arithmetic and copies ran while one was open for 6% of the time, Pallas kernels for 0%

profile of v1, /device:TPU:1, one launch (start us, length us, event | category | flops | bytes accessed | tf_op | source)
XLA Modules:
  0.0 212.4 jit_solution(17029502941071626755)
XLA Ops:
  0.6 2.1 reshape.165
  2.7 0.3 copy.79
  3.1 0.2 reshape.166
  3.2 0.6 copy-done.1
  3.8 0.2 reshape.167
  4.0 0.3 copy.80
  4.4 0.2 reshape.168
  4.5 1.4 pad_maximum_fusion.1
  5.9 8.8 %all-to-all-start.1 = ((bf16[32,32,768]{2,1,0:T(8,128)(2,1)}), bf16[32,32,768]{2,1,0:T(8,128)(2,1)}, u32[]{:S(2)}, u32[]{:S(2)}) async-start(bf16[32,32,768]{2,1,0:T(8,128)(2,1)} %pad_maximum_fusion.1), calls=%async_computation.1 | async-start | bytes 3145728 | tf_op jit(solution)/shard_map/all_to_all | solution.py:183
  14.8 37.9 %all_gather.3 = s32[32,8,27]{2,1,0:T(8,128)S(1)} all-gather(s32[1,8,27]{2,1,0:T(8,128)S(1)} %copy-done.4), channel_id=1, replica_groups=mesh['ctx'=32,'head'=4] {'ctx'}, dimensions={0}, use_global_device_ids=true | all-gather | bytes 28512 | tf_op jit(solution)/shard_map/all_gather | solution.py:59
  52.7 0.1 copy.65
  53.0 0.2 reshape.160
  53.2 0.3 copy.77
  53.5 0.2 reshape.161
  53.7 0.6 copy-done.3
  54.3 0.2 reshape.162
  54.5 0.3 copy.78
  54.9 0.2 reshape.163
  55.2 1.4 pad_maximum_fusion
  56.6 4.6 %all-to-all-start = ((bf16[32,32,768]{2,1,0:T(8,128)(2,1)}), bf16[32,32,768]{2,1,0:T(8,128)(2,1)S(1)}, u32[]{:S(2)}, u32[]{:S(2)}) async-start(bf16[32,32,768]{2,1,0:T(8,128)(2,1)} %pad_maximum_fusion), calls=%async_computation | async-start | bytes 3145728 | tf_op jit(solution)/shard_map/all_to_all | solution.py:186
  61.2 3.5 %collective-permute-start.1 = (bf16[1024,768]{1,0:T(8,128)(2,1)}, bf16[1024,768]{1,0:T(8,128)(2,1)}, u32[]{:S(2)}, u32[]{:S(2)}) collective-permute-start(bf16[1024,768]{1,0:T(8,128)(2,1)} %bitcast.41.k0.v0), channel_id=1, source_target_pairs={{4,32},{32,4},{36,64},{64,36},{68,96},{96,68},{100,8},{8,100},{12,... | collective-permute-start | bytes 4718600 | tf_op jit(solution)/shard_map/ppermute | solution.py:185
  64.7 0.1 collective-permute-start
  65.2 0.1 copy.74
  65.3 0.1 copy.75
  65.4 0.1 copy.76
  65.5 0.2 broadcast_in_dim.16
  65.8 0.7 reshape.159
  66.5 17.3 %all-to-all-done = bf16[32,32,768]{2,1,0:T(8,128)(2,1)S(1)} async-done(((bf16[32,32,768]{2,1,0:T(8,128)(2,1)}), bf16[32,32,768]{2,1,0:T(8,128)(2,1)S(1)}, u32[]{:S(2)}, u32[]{:S(2)}) %all-to-all-start) | async-done | bytes 1572896 | tf_op jit(solution)/shard_map/all_to_all | solution.py:186
  83.9 13.7 %collective-permute-done.1.k2.v2 = bf16[1024,768]{1,0:T(8,128)(2,1)} collective-permute-done((bf16[1024,768]{1,0:T(8,128)(2,1)}, bf16[1024,768]{1,0:T(8,128)(2,1)}, u32[]{:S(2)}, u32[]{:S(2)}) %collective-permute-start.1) | collective-permute-done | bytes 1572896 | tf_op jit(solution)/shard_map/ppermute | solution.py:185
  97.6 33.0 %column_grads.1 = (bf16[1024,384]{1,0:T(8,128)(2,1)}, bf16[1024,768]{1,0:T(8,128)(2,1)S(1)}, bf16[1024,768]{1,0:T(8,128)(2,1)}, bf16[1024,768]{1,0:T(8,128)(2,1)S(1)}) custom-call(f32[8,18,128]{2,1,0:T(8,128)S(1)} %copy.81.bias_ref, bf16[1024,768]{1,0:T(8,128)(2,1)} %bitcast.114, bf16[1024,768]{1,0:T(8,128)(2,1)} %bitcast.115, ...), custom_call_target="tpu_custom_call" | custom-call | flops 20000000000 | bytes 20000000 | tf_op jit(solution)/shard_map/column_grads/pallas_call | solution.py:166
  130.5 3.3 %collective-permute-start.3 = (bf16[1024,768]{1,0:T(8,128)(2,1)S(1)}, bf16[1024,768]{1,0:T(8,128)(2,1)}, u32[]{:S(2)}, u32[]{:S(2)}) collective-permute-start(bf16[1024,768]{1,0:T(8,128)(2,1)S(1)} %get-tuple-element.10), channel_id=1, source_target_pairs={{4,32},{32,4},{36,64},{64,36},{68,96},{96,68},{100,8},{8,100},{12,... | collective-permute-start | bytes 4718600 | tf_op jit(solution)/shard_map/ppermute | solution.py:189
  133.9 8.2 %all-to-all-start.2 = ((bf16[32,32,384]{2,1,0:T(8,128)(2,1)}), bf16[32,32,384]{2,1,0:T(8,128)(2,1)}, u32[]{:S(2)}, u32[]{:S(2)}) async-start(bf16[32,32,384]{2,1,0:T(8,128)(2,1)} %bitcast.42), calls=%async_computation.2 | async-start | bytes 1572864 | tf_op jit(solution)/shard_map/all_to_all | solution.py:190
  142.1 14.8 %collective-permute-done.3 = bf16[1024,768]{1,0:T(8,128)(2,1)} collective-permute-done((bf16[1024,768]{1,0:T(8,128)(2,1)S(1)}, bf16[1024,768]{1,0:T(8,128)(2,1)}, u32[]{:S(2)}, u32[]{:S(2)}) %collective-permute-start.3) | collective-permute-done | bytes 1572896 | tf_op jit(solution)/shard_map/ppermute | solution.py:189
  156.9 3.6 %add_convert_fusion = bf16[1024,768]{1,0:T(8,128)(2,1)} fusion(bf16[1024,768]{1,0:T(8,128)(2,1)} %collective-permute-done.3, bf16[1024,768]{1,0:T(8,128)(2,1)} %collective-permute-done.2, bf16[1024,768]{1,0:T(8,128)(2,1)S(1)} %get-tuple-element.8), kind=kLoop, calls=%fused_computation | loop fusion | flops 4718592 | bytes 6291456 | tf_op jit(solution)/shard_map/convert_element_type | solution.py:192
  160.5 6.0 %all-to-all-done.2 = bf16[32,32,384]{2,1,0:T(8,128)(2,1)} async-done(((bf16[32,32,384]{2,1,0:T(8,128)(2,1)}), bf16[32,32,384]{2,1,0:T(8,128)(2,1)}, u32[]{:S(2)}, u32[]{:S(2)}) %all-to-all-start.2) | async-done | bytes 786464 | tf_op jit(solution)/shard_map/all_to_all | solution.py:190
  166.5 4.4 %all-to-all-start.3 = ((bf16[32,32,768]{2,1,0:T(8,128)(2,1)}), bf16[32,32,768]{2,1,0:T(8,128)(2,1)S(1)}, u32[]{:S(2)}, u32[]{:S(2)}) async-start(bf16[32,32,768]{2,1,0:T(8,128)(2,1)} %bitcast.44), calls=%async_computation.3 | async-start | bytes 3145728 | tf_op jit(solution)/shard_map/all_to_all | solution.py:192
  170.8 1.7 reshape.171
  172.5 1.2 copy.92
  173.8 1.4 reshape.172
  175.1 18.5 %all-to-all-done.3 = bf16[32,32,768]{2,1,0:T(8,128)(2,1)S(1)} async-done(((bf16[32,32,768]{2,1,0:T(8,128)(2,1)}), bf16[32,32,768]{2,1,0:T(8,128)(2,1)S(1)}, u32[]{:S(2)}, u32[]{:S(2)}) %all-to-all-start.3) | async-done | bytes 1572896 | tf_op jit(solution)/shard_map/all_to_all | solution.py:192
  193.6 0.4 reshape.174
  194.0 9.9 %slice_reduce_fusion = (bf16[32,32,3,128]{3,2,1,0:T(4,128)(2,1)}, bf16[32,32,3,128]{3,2,1,0:T(4,128)(2,1)S(1)}) fusion(bf16[32,32,3,2,128]{4,3,2,1,0:T(2,128)(2,1)S(1)} %reshape.174), kind=kLoop, calls=%fused_computation.1 | loop fusion | bytes 3145728 | tf_op jit(solution)/shard_map/slice | solution.py:194
  203.9 2.6 %reshape_reshape_squeeze.7 = bf16[4,2,2,2,8,4,384]{6,5,4,3,2,1,0:T(4,128)(2,1)S(1)} reshape(bf16[32,32,3,128]{3,2,1,0:T(4,128)(2,1)} %get-tuple-element.11) | data formatting | bytes 1572864 | tf_op jit(solution)/shard_map/reshape;reshape;squeeze | solution.py:50
  206.5 1.2 copy.84
  207.7 1.4 reshape.176
  209.1 0.7 reshape_reshape_squeeze.6
  209.8 1.2 copy.83
  211.0 1.4 reshape.175
  (60 shorter events, 0.6 us)
Async XLA Ops:
  2.7 1.1 copy-start.1
  5.9 8.9 %copy-start.4 = (s32[1,8,27]{2,1,0:T(8,128)S(1)}, s32[1,8,27]{2,1,0:T(8,128)}, u32[]{:S(2)}) copy-start(s32[1,8,27]{2,1,0:T(8,128)} %param.9) | copy-start | bytes 2596
  5.9 47.1 %copy-start.2 = (bf16[1,8,64,768]{3,2,1,0:T(8,128)(2,1)S(1)}, bf16[1,8,64,768]{3,2,1,0:T(8,128)(2,1)}, u32[]{:S(2)}) copy-start(bf16[1,8,64,768]{3,2,1,0:T(8,128)(2,1)} %param.5) | copy-start | bytes 2359300
  5.9 50.6 %all-to-all-start.1 = ((bf16[32,32,768]{2,1,0:T(8,128)(2,1)}), bf16[32,32,768]{2,1,0:T(8,128)(2,1)}, u32[]{:S(2)}, u32[]{:S(2)}) async-start(bf16[32,32,768]{2,1,0:T(8,128)(2,1)} %pad_maximum_fusion.1), calls=%async_computation.1 | async-start | bytes 3145728 | tf_op jit(solution)/shard_map/all_to_all | solution.py:183
  53.2 1.1 copy-start.3
  56.6 27.3 %all-to-all-start = ((bf16[32,32,768]{2,1,0:T(8,128)(2,1)}), bf16[32,32,768]{2,1,0:T(8,128)(2,1)S(1)}, u32[]{:S(2)}, u32[]{:S(2)}) async-start(bf16[32,32,768]{2,1,0:T(8,128)(2,1)} %pad_maximum_fusion), calls=%async_computation | async-start | bytes 3145728 | tf_op jit(solution)/shard_map/all_to_all | solution.py:186
  61.2 36.4 %collective-permute-start.1 = (bf16[1024,768]{1,0:T(8,128)(2,1)}, bf16[1024,768]{1,0:T(8,128)(2,1)}, u32[]{:S(2)}, u32[]{:S(2)}) collective-permute-start(bf16[1024,768]{1,0:T(8,128)(2,1)} %bitcast.41.k0.v0), channel_id=1, source_target_pairs={{4,32},{32,4},{36,64},{64,36},{68,96},{96,68},{100,8},{8,100},{12,... | collective-permute-start | bytes 4718600 | tf_op jit(solution)/shard_map/ppermute | solution.py:185
  64.7 32.8 %collective-permute-start = (bf16[1024,768]{1,0:T(8,128)(2,1)}, bf16[1024,768]{1,0:T(8,128)(2,1)}, u32[]{:S(2)}, u32[]{:S(2)}) collective-permute-start(bf16[1024,768]{1,0:T(8,128)(2,1)} %bitcast.41.k0.v0), channel_id=1, source_target_pairs={{0,4},{4,0},{8,12},{12,8},{16,20},{20,16},{24,28},{28,24},{32,36},... | collective-permute-start | bytes 4718600 | tf_op jit(solution)/shard_map/ppermute | solution.py:184
  83.9 13.7 %copy-start = (bf16[32,32,768]{2,1,0:T(8,128)(2,1)}, bf16[32,32,768]{2,1,0:T(8,128)(2,1)S(1)}, u32[]{:S(2)}) copy-start(bf16[32,32,768]{2,1,0:T(8,128)(2,1)S(1)} %all-to-all-done) | copy-start | bytes 4718596
  130.5 11.5 %collective-permute-start.2 = (bf16[1024,768]{1,0:T(8,128)(2,1)}, bf16[1024,768]{1,0:T(8,128)(2,1)}, u32[]{:S(2)}, u32[]{:S(2)}) collective-permute-start(bf16[1024,768]{1,0:T(8,128)(2,1)} %get-tuple-element.9), channel_id=1, source_target_pairs={{0,4},{4,0},{8,12},{12,8},{16,20},{20,16},{24,28},{28,24},{32,36},... | collective-permute-start | bytes 4718600 | tf_op jit(solution)/shard_map/ppermute | solution.py:188
  130.5 26.4 %collective-permute-start.3 = (bf16[1024,768]{1,0:T(8,128)(2,1)S(1)}, bf16[1024,768]{1,0:T(8,128)(2,1)}, u32[]{:S(2)}, u32[]{:S(2)}) collective-permute-start(bf16[1024,768]{1,0:T(8,128)(2,1)S(1)} %get-tuple-element.10), channel_id=1, source_target_pairs={{4,32},{32,4},{36,64},{64,36},{68,96},{96,68},{100,8},{8,100},{12,... | collective-permute-start | bytes 4718600 | tf_op jit(solution)/shard_map/ppermute | solution.py:189
  133.9 32.6 %all-to-all-start.2 = ((bf16[32,32,384]{2,1,0:T(8,128)(2,1)}), bf16[32,32,384]{2,1,0:T(8,128)(2,1)}, u32[]{:S(2)}, u32[]{:S(2)}) async-start(bf16[32,32,384]{2,1,0:T(8,128)(2,1)} %bitcast.42), calls=%async_computation.2 | async-start | bytes 1572864 | tf_op jit(solution)/shard_map/all_to_all | solution.py:190
  166.5 27.1 %all-to-all-start.3 = ((bf16[32,32,768]{2,1,0:T(8,128)(2,1)}), bf16[32,32,768]{2,1,0:T(8,128)(2,1)S(1)}, u32[]{:S(2)}, u32[]{:S(2)}) async-start(bf16[32,32,768]{2,1,0:T(8,128)(2,1)} %bitcast.44), calls=%async_computation.3 | async-start | bytes 3145728 | tf_op jit(solution)/shard_map/all_to_all | solution.py:192

commit v2 on v1

v2 whole, which is shorter than its diff:
```python
import jax
import jax.numpy as jnp
from jax import lax
from jax.experimental import pallas as pl
from jax.experimental.pallas import tpu as pltpu
from jax.sharding import PartitionSpec as P

HEAD_DIM = 128
TILE = 4
ROW_BLOCKS = 2
NEG_FILL = -1e30
SCALE = HEAD_DIM ** (-0.5)
LOG2E = 1.4426950408889634
HEADS_LOCAL = 3
BLOCK = ROW_BLOCKS * TILE**3
STEPS = (-1, 0, 1)

XS, HALVES, STRIPS, CORES = 4, 2, 2, 2


def ctx_of(x, half, strip, core):
    return ((x * HALVES + half) * STRIPS + strip) * CORES + core


def swap_pairs():
    return [(i, i ^ 1) for i in range(32)]


def mask_pairs(flip):
    pairs = []
    for row in range(ROW_BLOCKS):
        for col in range(16):
            pairs.append((row * 16 + col, ctx_of(col % 8 // 2, row ^ flip, col // 8, col % 2)))
    return pairs


def chain_pairs():
    pairs = []
    for half in range(HALVES):
        for link in range(XS * STRIPS - 1):
            a = ctx_of(link % XS, half, link // XS, 1)
            b = ctx_of((link + 1) % XS, half, (link + 1) // XS, 0)
            pairs += [(a, b), (b, a)]
    return pairs


def mask_bias(window_mask):
    place = lax.axis_index("ctx")
    x, strip, core = place // 8, place // 2 % 2, place % 2
    col = strip * 8 + x * 2 + core
    half = place // 4 % 2
    time_blocks = window_mask.shape[1]
    mine = lax.ppermute(window_mask[0], "ctx", mask_pairs(0))
    other = lax.ppermute(window_mask[0], "ctx", mask_pairs(1))
    rows = jnp.stack([jnp.where(half == 0, mine, other), jnp.where(half == 0, other, mine)])
    rows = rows.reshape(ROW_BLOCKS, time_blocks, 3, 3, 3) == 1
    time_pos = jnp.arange(time_blocks)
    has_left = col > 0
    has_right = col < 15
    per_query_row = []
    for rq in range(ROW_BLOCKS):
        per_dt = []
        for dt in range(3):
            inside_t = (time_pos + dt - 1 >= 0) & (time_pos + dt - 1 < time_blocks)
            per_block = []
            for block in range(3):
                per_key_row = []
                for rk in range(ROW_BLOCKS):
                    window = rows[rq, :, dt, rk - rq + 1]
                    left = window[:, 0] & has_left
                    right = window[:, 2] & has_right
                    if block == 0:
                        allowed = window[:, 1]
                        if dt == 1 and rk == rq:
                            allowed = jnp.ones_like(allowed)
                    elif block == 1:
                        allowed = jnp.where(core == 0, right, left)
                    else:
                        allowed = jnp.where(core == 0, left, right)
                    per_key_row.append(allowed & inside_t)
                per_block.append(jnp.stack(per_key_row, axis=1))
            per_dt.append(jnp.stack(per_block, axis=1))
        per_query_row.append(jnp.stack(per_dt, axis=1))
    allowed = jnp.stack(per_query_row, axis=-1).reshape(time_blocks, 18, ROW_BLOCKS)
    bias = jnp.where(allowed, 0.0, NEG_FILL).astype(jnp.float32)
    bias = jnp.broadcast_to(bias[:, :, None, :, None], (time_blocks, 18, TILE, ROW_BLOCKS, TILE * TILE))
    return bias.reshape(time_blocks, 18, BLOCK)


VMEM_LIMIT = 62 * 1024 * 1024


def pack_kernel(k, v, q, g, out, taken, packed, in_sems, out_sems):
    reads, writes = [], []
    for x in range(XS):
        for i, ref in enumerate((k, v, q, g)):
            reads.append(pltpu.make_async_copy(ref.at[:, :, x], taken.at[i, x], in_sems.at[x, i]))
            reads[-1].start()
    for x in range(XS):
        for i in range(4):
            reads[x * 4 + i].wait()
        for half in range(HALVES):
            for strip in range(STRIPS):
                for core in range(CORES):
                    for i in range(4):
                        for j in range(HEADS_LOCAL):
                            lane = (half * HEADS_LOCAL + j) * HEAD_DIM
                            cells = taken[i, x, :, strip, :, lane : lane + HEAD_DIM].astype(jnp.float32)
                            cells = cells[:, core * TILE : (core + 1) * TILE].reshape(32, HEAD_DIM)
                            to = ((i // 2 * HEADS_LOCAL + j) * 2 + i % 2) * HEAD_DIM
                            packed[x, half, strip, core, :, to : to + HEAD_DIM] = cells.astype(jnp.bfloat16)
            writes.append(pltpu.make_async_copy(packed.at[x, half], out.at[x, half], out_sems.at[x, half]))
            writes[-1].start()
    for write in writes:
        write.wait()


def pack(tensors):
    views = [t.reshape(8, STRIPS, XS, 8, 768) for t in tensors]
    out = (XS, HALVES, STRIPS, CORES, 32, 12 * HEAD_DIM)
    return pl.pallas_call(
        pack_kernel,
        in_specs=[pl.BlockSpec(memory_space=pl.ANY)] * 4,
        out_specs=pl.BlockSpec(memory_space=pl.ANY),
        out_shape=jax.ShapeDtypeStruct(out, jnp.bfloat16),
        scratch_shapes=[
            pltpu.VMEM((4, XS, 8, STRIPS, 8, 768), jnp.bfloat16),
            pltpu.VMEM(out, jnp.bfloat16),
            pltpu.SemaphoreType.DMA((XS, 4)),
            pltpu.SemaphoreType.DMA((XS, HALVES)),
        ],
        compiler_params=pltpu.CompilerParams(vmem_limit_bytes=VMEM_LIMIT),
        cost_estimate=pl.CostEstimate(flops=0, bytes_accessed=6_300_000, transcendentals=0),
        name="pack",
    )(*views).reshape(32, 32, 12 * HEAD_DIM)


def unpack_kernel(arrived, dk, dv, dq, taken, b0, b1, b2, in_sems, out_sems):
    reads, writes = [], []
    for x in range(XS):
        reads.append(pltpu.make_async_copy(arrived.at[x], taken.at[x], in_sems.at[x]))
        reads[-1].start()
    for x in range(XS):
        reads[x].wait()
        for i, (ref, buf) in enumerate(((dk, b0), (dv, b1), (dq, b2))):
            for strip in range(STRIPS):
                for half in range(HALVES):
                    parts = []
                    for core in range(CORES):
                        cells = taken[x, half, strip, core, :, i * 384 : (i + 1) * 384]
                        parts.append(cells.astype(jnp.float32).reshape(8, TILE, 384))
                    joined = jnp.concatenate(parts, axis=1).astype(jnp.bfloat16)
                    buf[x, :, strip, :, half * 384 : (half + 1) * 384] = joined
            writes.append(pltpu.make_async_copy(buf.at[x], ref.at[:, :, x], out_sems.at[x, i]))
            writes[-1].start()
    for write in writes:
        write.wait()


def unpack(arrived):
    out = jax.ShapeDtypeStruct((8, STRIPS, XS, 8, 768), jnp.bfloat16)
    buf = pltpu.VMEM((XS, 8, STRIPS, 8, 768), jnp.bfloat16)
    lanes = arrived.shape[-1]
    results = pl.pallas_call(
        unpack_kernel,
        in_specs=[pl.BlockSpec(memory_space=pl.ANY)],
        out_specs=[pl.BlockSpec(memory_space=pl.ANY)] * 3,
        out_shape=[out] * 3,
        scratch_shapes=[
            pltpu.VMEM((XS, HALVES, STRIPS, CORES, 32, lanes), jnp.bfloat16),
            buf,
            buf,
            buf,
            pltpu.SemaphoreType.DMA((XS,)),
            pltpu.SemaphoreType.DMA((XS, 3)),
        ],
        compiler_params=pltpu.CompilerParams(vmem_limit_bytes=VMEM_LIMIT),
        cost_estimate=pl.CostEstimate(flops=0, bytes_accessed=4_700_000, transcendentals=0),
        name="unpack",
    )(arrived.reshape(XS, HALVES, STRIPS, CORES, 32, lanes))
    return [r.reshape(1, 8, 64, 768) for r in results]


def block_bias(bias_ref, t, dt, block):
    rows = []
    for rk in range(ROW_BLOCKS):
        row = (dt * 3 + block) * 2 + rk
        rows.append(jnp.broadcast_to(bias_ref[t, row : row + 1, :], (TILE * TILE, BLOCK)))
    return jnp.concatenate(rows * TILE, axis=0)


def grads_kernel(bias_ref, qg, own, near, far, dq_ref, o0, o1, o2, a0, a1, a2):
    time_blocks = bias_ref.shape[0]
    accs, sources = (a0, a1, a2), (own, near, far)
    for acc in accs:
        acc[...] = jnp.zeros_like(acc)
    for t in range(time_blocks):
        here = pl.ds(t * BLOCK, BLOCK)
        q = qg[here, :HEAD_DIM]
        g = qg[here, HEAD_DIM:]
        zero = jnp.zeros_like(q)
        both = jnp.concatenate(
            [jnp.concatenate([q, zero], axis=1), jnp.concatenate([zero, g], axis=1)], axis=0
        )
        low, high = max(t - 1, 0), min(t + 1, time_blocks - 1)
        window = pl.ds(low * BLOCK, (high - low + 1) * BLOCK)
        scores, probs = [], []
        top = None
        for block, source in enumerate(sources):
            r = lax.dot_general(
                source[window, :], both, (((1,), (1,)), ((), ())), preferred_element_type=jnp.float32
            )
            bias = [block_bias(bias_ref, t, near_t - t + 1, block) for near_t in range(low, high + 1)]
            s = r[:, :BLOCK] * (SCALE * LOG2E) + jnp.concatenate(bias, axis=0)
            block_top = jnp.max(s, axis=0, keepdims=True)
            top = block_top if top is None else jnp.maximum(top, block_top)
            scores.append(s)
            probs.append(r[:, BLOCK:])
        total = jnp.zeros((1, BLOCK), jnp.float32)
        dots = jnp.zeros((1, BLOCK), jnp.float32)
        weights = []
        for s, pg in zip(scores, probs):
            e = jnp.exp2(s - top)
            total += jnp.sum(e, axis=0, keepdims=True)
            dots += jnp.sum(e * pg, axis=0, keepdims=True)
            weights.append(e)
        inv = 1.0 / total
        row_dot = dots * inv
        inv_scaled = inv * SCALE
        dqt = jnp.zeros((HEAD_DIM, BLOCK), jnp.float32)
        for acc, source, e, pg in zip(accs, sources, weights, probs):
            p = (e * inv).astype(jnp.bfloat16)
            ds = ((e * inv_scaled) * (pg - row_dot)).astype(jnp.bfloat16)
            pair = jnp.concatenate([ds, p], axis=1)
            acc[window, :] += jnp.dot(pair, both, preferred_element_type=jnp.float32)
            dqt += lax.dot_general(
                source[window, :HEAD_DIM], ds, (((0,), (0,)), ((), ())), preferred_element_type=jnp.float32
            )
        dq_ref[here, :] = dqt.T.astype(jnp.bfloat16)
    for acc, out in zip(accs, (o0, o1, o2)):
        out[...] = acc[...].astype(jnp.bfloat16)


def head_grads(bias, everything, near, far, head):
    rows = everything.shape[0]
    wide = (rows, 2 * HEAD_DIM)
    whole = pl.BlockSpec(wide, lambda i: (0, 0))
    out = jax.ShapeDtypeStruct(wide, jnp.bfloat16)
    return pl.pallas_call(
        grads_kernel,
        grid=(1,),
        in_specs=[
            pl.BlockSpec(bias.shape, lambda i: (0, 0, 0)),
            pl.BlockSpec(wide, lambda i: (0, HEADS_LOCAL + head)),
            pl.BlockSpec(wide, lambda i: (0, head)),
            whole,
            whole,
        ],
        out_specs=[pl.BlockSpec((rows, HEAD_DIM), lambda i: (0, 0)), whole, whole, whole],
        out_shape=[jax.ShapeDtypeStruct((rows, HEAD_DIM), jnp.bfloat16), out, out, out],
        scratch_shapes=[pltpu.VMEM(wide, jnp.float32)] * 3,
        compiler_params=pltpu.CompilerParams(vmem_limit_bytes=VMEM_LIMIT),
        cost_estimate=pl.CostEstimate(flops=7_000_000_000, bytes_accessed=4_500_000, transcendentals=1_200_000),
        name="head_grads",
    )(bias, everything, everything, near, far)


def gather_kernel(*refs):
    out = refs[-1]
    for j in range(HEADS_LOCAL):
        dq, own, near, far = refs[4 * j : 4 * j + 4]
        total = own[...].astype(jnp.float32) + near[...].astype(jnp.float32) + far[...].astype(jnp.float32)
        total = total.astype(jnp.bfloat16)
        lane = j * HEAD_DIM
        out[:, lane : lane + HEAD_DIM] = total[:, :HEAD_DIM]
        out[:, 384 + lane : 384 + lane + HEAD_DIM] = total[:, HEAD_DIM:]
        out[:, 768 + lane : 768 + lane + HEAD_DIM] = dq[...]


def gather_grads(parts):
    rows = parts[0].shape[0]
    step = rows // 4
    return pl.pallas_call(
        gather_kernel,
        grid=(4,),
        in_specs=[pl.BlockSpec((step, part.shape[1]), lambda i: (i, 0)) for part in parts],
        out_specs=pl.BlockSpec((step, 9 * HEAD_DIM), lambda i: (i, 0)),
        out_shape=jax.ShapeDtypeStruct((rows, 9 * HEAD_DIM), jnp.bfloat16),
        compiler_params=pltpu.CompilerParams(vmem_limit_bytes=VMEM_LIMIT),
        cost_estimate=pl.CostEstimate(flops=0, bytes_accessed=8_000_000, transcendentals=0),
        name="gather_grads",
    )(*parts)


def shards(queries, keys, values, out_grad, window_mask):
    swap, chain = swap_pairs(), chain_pairs()
    bias = mask_bias(window_mask)
    packed = pack((keys, values, queries, out_grad))
    everything = lax.all_to_all(packed, "ctx", 0, 0, tiled=True).reshape(1024, 12 * HEAD_DIM)
    nears, fars = [], []
    for head in range(HEADS_LOCAL):
        kv = everything[:, 2 * head * HEAD_DIM : 2 * (head + 1) * HEAD_DIM]
        nears.append(lax.ppermute(kv, "ctx", swap))
        fars.append(lax.ppermute(kv, "ctx", chain))
    parts = []
    for head in range(HEADS_LOCAL):
        dq, own, to_near, to_far = head_grads(bias, everything, nears[head], fars[head], head)
        parts += [dq, own, lax.ppermute(to_near, "ctx", swap), lax.ppermute(to_far, "ctx", chain)]
    grads = gather_grads(parts).reshape(32, 32, 9 * HEAD_DIM)
    dk, dv, dq = unpack(lax.all_to_all(grads, "ctx", 0, 0, tiled=True))
    return dq, dk, dv


def solution(mesh):
    tokens = P("ctx", None, None, "head")
    return jax.shard_map(
        shards,
        mesh=mesh,
        in_specs=(tokens, tokens, tokens, tokens, P("ctx", None, None)),
        out_specs=(tokens, tokens, tokens),
        check_vma=False,
    )
```

time: 213 us -> 167 us (0.78)
  local copies, waits for them, and re-layouts: 30.4 us -> 5.85 us
  waiting for transfers between devices: 70.3 us -> 45.9 us
  other arithmetic: 6.69 us -> 0.39 us
  Pallas kernels: 33 us -> 36.7 us
  starting transfers between devices: 32.9 us -> 35.8 us
  blocking collectives: 37.9 us -> 40.3 us
    all_to_all x0 -> x1, blocking collectives: none -> 40.3 us  [shards(): dk, dv, dq = unpack(lax.all_to_all(grads, 'ctx', 0, 0, tiled=True))]
    all_gather x1 -> x0, blocking collectives: 37.9 us -> none  [mask_bias(): every = lax.all_gather(window_mask, 'ctx', tiled=True)]
    ppermute x4 -> x14, starting transfers between devices: 6.97 us -> 29.5 us  [the longest x3 12.2 us: shards(): lax.ppermute(to_far, 'ctx', chain)]
    ppermute x4 -> x14, waiting for transfers between devices: 28.5 us -> 7.17 us  [the longest x3 7.11 us: shards(): lax.ppermute(to_far, 'ctx', chain)]
    all_to_all x4 -> x1, starting transfers between devices: 25.9 us -> 6.27 us  [shards(): lax.all_to_all(packed, 'ctx', 0, 0, tiled=True).reshape(1024, 12 * HEAD_DIM)]
    reshape x14 -> x0, local copies, waits for them, and re-layouts: 10.7 us -> none  [the longest x3 4.13 us: from_columns(): return shaped.reshape(1, 8, 64, HALVES * channels)]
    slice x1, local copies, waits for them, and re-layouts: 9.89 us -> 1.17 us  [shards(): kv = everything[:, 2 * head * HEAD_DIM:2 * (head + 1) * HEAD_DIM]]
    transpose x6 -> x0, local copies, waits for them, and re-layouts: 3.77 us -> none  [the longest x2 2.43 us: from_columns(): shaped = shaped.transpose(4, 2, 0, 3, 5, 1, 6)]
  transfers between devices with their start and end apart: 8 -> 15, of which waited for: 5 -> 2; matrix products, arithmetic and copies ran while one was open for 6% -> 2% of each run, Pallas kernels for 0% -> 18%
where the time goes in v2:
time: 167 us; the launch traced here: 166 us
  waiting for transfers between devices  45.9 us (27%)
  blocking collectives  40.3 us (24%)
  Pallas kernels  36.7 us (22%)
  starting transfers between devices  35.8 us (21%)
  local copies, waits for them, and re-layouts  5.85 us (4%)
    all_to_all x1, blocking collectives, shards(): dk, dv, dq = unpack(lax.all_to_all(grads, 'ctx', 0, 0, tiled=True))  40.3 us
    all_to_all x1, waiting for transfers between devices, shards(): lax.all_to_all(packed, 'ctx', 0, 0, tiled=True).reshape(1024, 12 * HEAD_DIM)  38.7 us
    pallas_call x3, Pallas kernels, head_grads(): pl.pallas_call(grads_kernel, grid=(1,), in_specs=[pl.BlockSpec(bias.shape...  26.1 us
    ppermute x3, starting transfers between devices, shards(): lax.ppermute(to_far, 'ctx', chain)  12.2 us
    ppermute x3, starting transfers between devices, shards(): fars.append(lax.ppermute(kv, 'ctx', chain))  8.55 us
    ppermute x3, waiting for transfers between devices, shards(): lax.ppermute(to_far, 'ctx', chain)  7.11 us
    ppermute x1, starting transfers between devices, mask_bias(): other = lax.ppermute(window_mask[0], 'ctx', mask_pairs(1))  6.9 us
    all_to_all x1, starting transfers between devices, shards(): lax.all_to_all(packed, 'ctx', 0, 0, tiled=True).reshape(1024, 12 * HEAD_DIM)  6.27 us
  transfers between devices with their start and end apart: 15, of which 2 were waited for; matrix products, arithmetic and copies ran while one was open for 2% of the time, Pallas kernels for 18%

profile of v2, /device:TPU:1, one launch (start us, length us, event | category | flops | bytes accessed | tf_op | source)
XLA Modules:
  0.0 166.3 jit_solution(17121125484372148074)
XLA Ops:
  0.6 1.3 collective-permute-start
  2.0 6.9 %collective-permute-start.1 = (s32[8,27]{1,0:T(8,128)}, s32[8,27]{1,0:T(8,128)S(1)}, u32[]{:S(2)}, u32[]{:S(2)}) collective-permute-start(s32[8,27]{1,0:T(8,128)} %bitcast.124), channel_id=1, source_target_pairs={{0,16},{4,20},{8,48},{12,52},{16,80},{20,84},{24,112},{28,116},{32... | collective-permute-start | bytes 2600 | tf_op jit(solution)/shard_map/ppermute | solution.py:54
  8.9 3.2 %pack.1 = bf16[4,2,2,2,32,1536]{5,4,3,2,1,0:T(8,128)(2,1)} custom-call(bf16[8,2,4,8,768]{4,3,2,1,0:T(8,128)(2,1)} %bitcast.110, bf16[8,2,4,8,768]{4,3,2,1,0:T(8,128)(2,1)} %bitcast.111, bf16[8,2,4,8,768]{4,3,2,1,0:T(8,128)(2,1)} %bitcast.112, bf16[8,2,4,8,768]{4,3,2,1,0:T(8,128)(2,1)} %bitcast.113), custom_call_target="tpu_custom_call" | custom-call | bytes 6300000 | tf_op jit(solution)/shard_map/pack/pallas_call | solution.py:121
  12.0 6.3 %all-to-all-start = ((bf16[32,32,1536]{2,1,0:T(8,128)(2,1)}), bf16[32,32,1536]{2,1,0:T(8,128)(2,1)S(1)}, u32[]{:S(2)}, u32[]{:S(2)}) async-start(bf16[32,32,1536]{2,1,0:T(8,128)(2,1)} %bitcast.100), calls=%async_computation | async-start | bytes 6291456 | tf_op jit(solution)/shard_map/all_to_all | solution.py:299
  18.4 0.0 collective-permute-done
  18.4 0.0 collective-permute-done.1
  18.5 0.1 copy.30
  18.6 0.1 copy.31
  19.1 0.1 copy.40
  19.4 38.7 %all-to-all-done = bf16[32,32,1536]{2,1,0:T(8,128)(2,1)S(1)} async-done(((bf16[32,32,1536]{2,1,0:T(8,128)(2,1)}), bf16[32,32,1536]{2,1,0:T(8,128)(2,1)S(1)}, u32[]{:S(2)}, u32[]{:S(2)}) %all-to-all-start) | async-done | bytes 3145760 | tf_op jit(solution)/shard_map/all_to_all | solution.py:299
  58.1 1.6 copy-done
  59.7 1.2 fusion
  60.9 0.4 collective-permute-start.10
  61.3 1.9 %collective-permute-start.11 = (bf16[1024,256]{1,0:T(8,128)(2,1)}, bf16[1024,256]{1,0:T(8,128)(2,1)S(1)}, u32[]{:S(2)}, u32[]{:S(2)}) collective-permute-start(bf16[1024,256]{1,0:T(8,128)(2,1)} %get-tuple-element.33), channel_id=1, source_target_pairs={{4,32},{32,4},{36,64},{64,36},{68,96},{96,68},{100,8},{8,100},{12,... | collective-permute-start | bytes 1572872 | tf_op jit(solution)/shard_map/ppermute | solution.py:304
  63.3 0.1 copy.41
  63.4 0.1 copy.42
  63.6 0.2 broadcast_in_dim.16
  63.8 0.7 reshape.143
  64.5 0.7 copy.43.bias_ref
  65.2 0.0 collective-permute-start.6
  65.2 3.6 %collective-permute-start.7 = (bf16[1024,256]{1,0:T(8,128)(2,1)}, bf16[1024,256]{1,0:T(8,128)(2,1)}, u32[]{:S(2)}, u32[]{:S(2)}) collective-permute-start(bf16[1024,256]{1,0:T(8,128)(2,1)} %get-tuple-element.34), channel_id=1, source_target_pairs={{4,32},{32,4},{36,64},{64,36},{68,96},{96,68},{100,8},{8,100},{12,... | collective-permute-start | bytes 1572872 | tf_op jit(solution)/shard_map/ppermute | solution.py:304
  68.8 0.1 collective-permute-start.2
  68.9 0.0 collective-permute-done.10.near
  68.9 3.0 %collective-permute-start.3 = (bf16[1024,256]{1,0:T(8,128)(2,1)}, bf16[1024,256]{1,0:T(8,128)(2,1)}, u32[]{:S(2)}, u32[]{:S(2)}) collective-permute-start(bf16[1024,256]{1,0:T(8,128)(2,1)} %get-tuple-element.35), channel_id=1, source_target_pairs={{4,32},{32,4},{36,64},{64,36},{68,96},{96,68},{100,8},{8,100},{12,... | collective-permute-start | bytes 1572872 | tf_op jit(solution)/shard_map/ppermute | solution.py:304
  72.0 0.0 collective-permute-done.11.far
  72.0 0.8 copy-done.5
  72.8 8.7 %head_grads.5 = (bf16[1024,128]{1,0:T(8,128)(2,1)}, bf16[1024,256]{1,0:T(8,128)(2,1)}, bf16[1024,256]{1,0:T(8,128)(2,1)}, bf16[1024,256]{1,0:T(8,128)(2,1)}) custom-call(f32[8,18,128]{2,1,0:T(8,128)} %copy.43.bias_ref, bf16[1024,1536]{1,0:T(8,128)(2,1)} %bitcast.104, bf16[1024,1536]{1,0:T(8,128)(2,1)} %bitcast.105, bf16[1024,256]{1,0:T(8,128)(2,1)} %copy-done.4, ...), custom_call_target="tpu_custom_call" | custom-call | flops 7000000000 | bytes 4500000 | tf_op jit(solution)/shard_map/head_grads/pallas_call | solution.py:249
  81.5 0.0 collective-permute-start.12
  81.5 0.0 collective-permute-done.6.near
  81.5 0.0 copy-start.6
  81.5 4.6 %collective-permute-start.13 = (bf16[1024,256]{1,0:T(8,128)(2,1)}, bf16[1024,256]{1,0:T(8,128)(2,1)S(1)}, u32[]{:S(2)}, u32[]{:S(2)}) collective-permute-start(bf16[1024,256]{1,0:T(8,128)(2,1)} %get-tuple-element.29), channel_id=1, source_target_pairs={{4,32},{32,4},{36,64},{64,36},{68,96},{96,68},{100,8},{8,100},{12,... | collective-permute-start | bytes 1572872 | tf_op jit(solution)/shard_map/ppermute | solution.py:308
  86.1 0.0 collective-permute-done.7.far
  86.1 8.7 %head_grads.4 = (bf16[1024,128]{1,0:T(8,128)(2,1)}, bf16[1024,256]{1,0:T(8,128)(2,1)}, bf16[1024,256]{1,0:T(8,128)(2,1)}, bf16[1024,256]{1,0:T(8,128)(2,1)}) custom-call(f32[8,18,128]{2,1,0:T(8,128)} %copy.43.bias_ref, bf16[1024,1536]{1,0:T(8,128)(2,1)} %bitcast.106, bf16[1024,1536]{1,0:T(8,128)(2,1)} %bitcast.107, bf16[1024,256]{1,0:T(8,128)(2,1)} %copy-done.6, ...), custom_call_target="tpu_custom_call" | custom-call | flops 7000000000 | bytes 4500000 | tf_op jit(solution)/shard_map/head_grads/pallas_call | solution.py:249
  94.8 0.0 collective-permute-start.8
  94.8 0.0 collective-permute-done.2.near
  94.8 3.8 %collective-permute-start.9 = (bf16[1024,256]{1,0:T(8,128)(2,1)}, bf16[1024,256]{1,0:T(8,128)(2,1)}, u32[]{:S(2)}, u32[]{:S(2)}) collective-permute-start(bf16[1024,256]{1,0:T(8,128)(2,1)} %get-tuple-element.25), channel_id=1, source_target_pairs={{4,32},{32,4},{36,64},{64,36},{68,96},{96,68},{100,8},{8,100},{12,... | collective-permute-start | bytes 1572872 | tf_op jit(solution)/shard_map/ppermute | solution.py:308
  98.6 0.0 collective-permute-done.3.far
  98.6 8.7 %head_grads.3 = (bf16[1024,128]{1,0:T(8,128)(2,1)}, bf16[1024,256]{1,0:T(8,128)(2,1)}, bf16[1024,256]{1,0:T(8,128)(2,1)}, bf16[1024,256]{1,0:T(8,128)(2,1)}) custom-call(f32[8,18,128]{2,1,0:T(8,128)} %copy.43.bias_ref, bf16[1024,1536]{1,0:T(8,128)(2,1)} %bitcast.108, bf16[1024,1536]{1,0:T(8,128)(2,1)} %bitcast.109, ...), custom_call_target="tpu_custom_call" | custom-call | flops 7000000000 | bytes 4500000 | tf_op jit(solution)/shard_map/head_grads/pallas_call | solution.py:249
  107.3 0.0 collective-permute-start.4
  107.3 0.0 collective-permute-done.12.refs_10_
  107.3 3.9 %collective-permute-start.5 = (bf16[1024,256]{1,0:T(8,128)(2,1)}, bf16[1024,256]{1,0:T(8,128)(2,1)}, u32[]{:S(2)}, u32[]{:S(2)}) collective-permute-start(bf16[1024,256]{1,0:T(8,128)(2,1)} %get-tuple-element.21), channel_id=1, source_target_pairs={{4,32},{32,4},{36,64},{64,36},{68,96},{96,68},{100,8},{8,100},{12,... | collective-permute-start | bytes 1572872 | tf_op jit(solution)/shard_map/ppermute | solution.py:308
  111.2 0.0 collective-permute-done.13.refs_11_
  111.3 0.0 collective-permute-done.9.refs_7_
  111.3 0.0 collective-permute-done.4.refs_2_
  111.3 7.1 %collective-permute-done.5.refs_3_ = bf16[1024,256]{1,0:T(8,128)(2,1)} collective-permute-done((bf16[1024,256]{1,0:T(8,128)(2,1)}, bf16[1024,256]{1,0:T(8,128)(2,1)}, u32[]{:S(2)}, u32[]{:S(2)}) %collective-permute-start.5) | collective-permute-done | bytes 524320 | tf_op jit(solution)/shard_map/ppermute | solution.py:308
  118.4 4.8 %gather_grads.1 = bf16[1024,1152]{1,0:T(8,128)(2,1)} custom-call(bf16[1024,128]{1,0:T(8,128)(2,1)} %get-tuple-element.18.refs_0_, bf16[1024,256]{1,0:T(8,128)(2,1)} %get-tuple-element.19.refs_1_, bf16[1024,256]{1,0:T(8,128)(2,1)} %collective-permute-done.4.refs_2_, bf16[1024,256]{1,0:T(8,128)(2,1)} %collective-permute-done.5.refs_3_, ...), custom_call_target="tpu_custom_call" | custom-call | bytes 8000000 | tf_op jit(solution)/shard_map/gather_grads/pallas_call | solution.py:283
  123.2 40.3 %all_to_all.10 = bf16[32,32,1152]{2,1,0:T(8,128)(2,1)} all-to-all(bf16[32,32,1152]{2,1,0:T(8,128)(2,1)} %bitcast.102), channel_id=1, replica_groups=mesh['ctx'=32,'head'=4] {'ctx'}, dimensions={0} | all-to-all | bytes 4718592 | tf_op jit(solution)/shard_map/all_to_all | solution.py:310
  163.5 2.6 %unpack.1 = (bf16[8,2,4,8,768]{4,3,2,1,0:T(8,128)(2,1)}, bf16[8,2,4,8,768]{4,3,2,1,0:T(8,128)(2,1)}, bf16[8,2,4,8,768]{4,3,2,1,0:T(8,128)(2,1)}) custom-call(bf16[4,2,2,2,32,1152]{5,4,3,2,1,0:T(8,128)(2,1)} %bitcast.101), custom_call_target="tpu_custom_call" | custom-call | bytes 4700000 | tf_op jit(solution)/shard_map/unpack/pallas_call | solution.py:164
  (60 shorter events, 0.6 us)
Async XLA Ops:
  0.6 17.8 %collective-permute-start = (s32[8,27]{1,0:T(8,128)}, s32[8,27]{1,0:T(8,128)S(1)}, u32[]{:S(2)}, u32[]{:S(2)}) collective-permute-start(s32[8,27]{1,0:T(8,128)} %bitcast.123), channel_id=1, source_target_pairs={{0,0},{4,4},{8,32},{12,36},{16,64},{20,68},{24,96},{28,100},{32,8}... | collective-permute-start | bytes 2600 | tf_op jit(solution)/shard_map/ppermute | solution.py:53
  2.0 16.5 %collective-permute-start.1 = (s32[8,27]{1,0:T(8,128)}, s32[8,27]{1,0:T(8,128)S(1)}, u32[]{:S(2)}, u32[]{:S(2)}) collective-permute-start(s32[8,27]{1,0:T(8,128)} %bitcast.124), channel_id=1, source_target_pairs={{0,16},{4,20},{8,48},{12,52},{16,80},{20,84},{24,112},{28,116},{32... | collective-permute-start | bytes 2600 | tf_op jit(solution)/shard_map/ppermute | solution.py:54
  12.0 46.0 %all-to-all-start = ((bf16[32,32,1536]{2,1,0:T(8,128)(2,1)}), bf16[32,32,1536]{2,1,0:T(8,128)(2,1)S(1)}, u32[]{:S(2)}, u32[]{:S(2)}) async-start(bf16[32,32,1536]{2,1,0:T(8,128)(2,1)} %bitcast.100), calls=%async_computation | async-start | bytes 6291456 | tf_op jit(solution)/shard_map/all_to_all | solution.py:299
  58.1 1.6 copy-start
  60.9 8.0 %collective-permute-start.10 = (bf16[1024,256]{1,0:T(8,128)(2,1)}, bf16[1024,256]{1,0:T(8,128)(2,1)S(1)}, u32[]{:S(2)}, u32[]{:S(2)}) collective-permute-start(bf16[1024,256]{1,0:T(8,128)(2,1)} %get-tuple-element.33), channel_id=1, source_target_pairs={{0,4},{4,0},{8,12},{12,8},{16,20},{20,16},{24,28},{28,24},{32,36},... | collective-permute-start | bytes 1572872 | tf_op jit(solution)/shard_map/ppermute | solution.py:303
  61.3 10.7 %collective-permute-start.11 = (bf16[1024,256]{1,0:T(8,128)(2,1)}, bf16[1024,256]{1,0:T(8,128)(2,1)S(1)}, u32[]{:S(2)}, u32[]{:S(2)}) collective-permute-start(bf16[1024,256]{1,0:T(8,128)(2,1)} %get-tuple-element.33), channel_id=1, source_target_pairs={{4,32},{32,4},{36,64},{64,36},{68,96},{96,68},{100,8},{8,100},{12,... | collective-permute-start | bytes 1572872 | tf_op jit(solution)/shard_map/ppermute | solution.py:304
  65.2 16.3 %collective-permute-start.6 = (bf16[1024,256]{1,0:T(8,128)(2,1)}, bf16[1024,256]{1,0:T(8,128)(2,1)S(1)}, u32[]{:S(2)}, u32[]{:S(2)}) collective-permute-start(bf16[1024,256]{1,0:T(8,128)(2,1)} %get-tuple-element.34), channel_id=1, source_target_pairs={{0,4},{4,0},{8,12},{12,8},{16,20},{20,16},{24,28},{28,24},{32,36},... | collective-permute-start | bytes 1572872 | tf_op jit(solution)/shard_map/ppermute | solution.py:303
  65.2 20.9 %collective-permute-start.7 = (bf16[1024,256]{1,0:T(8,128)(2,1)}, bf16[1024,256]{1,0:T(8,128)(2,1)}, u32[]{:S(2)}, u32[]{:S(2)}) collective-permute-start(bf16[1024,256]{1,0:T(8,128)(2,1)} %get-tuple-element.34), channel_id=1, source_target_pairs={{4,32},{32,4},{36,64},{64,36},{68,96},{96,68},{100,8},{8,100},{12,... | collective-permute-start | bytes 1572872 | tf_op jit(solution)/shard_map/ppermute | solution.py:304
  68.8 26.0 %collective-permute-start.2 = (bf16[1024,256]{1,0:T(8,128)(2,1)}, bf16[1024,256]{1,0:T(8,128)(2,1)}, u32[]{:S(2)}, u32[]{:S(2)}) collective-permute-start(bf16[1024,256]{1,0:T(8,128)(2,1)} %get-tuple-element.35), channel_id=1, source_target_pairs={{0,4},{4,0},{8,12},{12,8},{16,20},{20,16},{24,28},{28,24},{32,36},... | collective-permute-start | bytes 1572872 | tf_op jit(solution)/shard_map/ppermute | solution.py:303
  68.9 3.1 %copy-start.4 = (bf16[1024,256]{1,0:T(8,128)(2,1)}, bf16[1024,256]{1,0:T(8,128)(2,1)S(1)}, u32[]{:S(2)}) copy-start(bf16[1024,256]{1,0:T(8,128)(2,1)S(1)} %collective-permute-done.10.near) | copy-start | bytes 1572868
  68.9 29.6 %collective-permute-start.3 = (bf16[1024,256]{1,0:T(8,128)(2,1)}, bf16[1024,256]{1,0:T(8,128)(2,1)}, u32[]{:S(2)}, u32[]{:S(2)}) collective-permute-start(bf16[1024,256]{1,0:T(8,128)(2,1)} %get-tuple-element.35), channel_id=1, source_target_pairs={{4,32},{32,4},{36,64},{64,36},{68,96},{96,68},{100,8},{8,100},{12,... | collective-permute-start | bytes 1572872 | tf_op jit(solution)/shard_map/ppermute | solution.py:304
  72.0 0.8 copy-start.5
  81.5 25.8 %collective-permute-start.12 = (bf16[1024,256]{1,0:T(8,128)(2,1)}, bf16[1024,256]{1,0:T(8,128)(2,1)S(1)}, u32[]{:S(2)}, u32[]{:S(2)}) collective-permute-start(bf16[1024,256]{1,0:T(8,128)(2,1)} %get-tuple-element.28), channel_id=1, source_target_pairs={{0,4},{4,0},{8,12},{12,8},{16,20},{20,16},{24,28},{28,24},{32,36},... | collective-permute-start | bytes 1572872 | tf_op jit(solution)/shard_map/ppermute | solution.py:308
  81.5 4.6 %copy-start.6 = (bf16[1024,256]{1,0:T(8,128)(2,1)}, bf16[1024,256]{1,0:T(8,128)(2,1)S(1)}, u32[]{:S(2)}) copy-start(bf16[1024,256]{1,0:T(8,128)(2,1)S(1)} %collective-permute-done.6.near) | copy-start | bytes 1572868
  81.5 29.7 %collective-permute-start.13 = (bf16[1024,256]{1,0:T(8,128)(2,1)}, bf16[1024,256]{1,0:T(8,128)(2,1)S(1)}, u32[]{:S(2)}, u32[]{:S(2)}) collective-permute-start(bf16[1024,256]{1,0:T(8,128)(2,1)} %get-tuple-element.29), channel_id=1, source_target_pairs={{4,32},{32,4},{36,64},{64,36},{68,96},{96,68},{100,8},{8,100},{12,... | collective-permute-start | bytes 1572872 | tf_op jit(solution)/shard_map/ppermute | solution.py:308
  94.8 16.5 %collective-permute-start.8 = (bf16[1024,256]{1,0:T(8,128)(2,1)}, bf16[1024,256]{1,0:T(8,128)(2,1)S(1)}, u32[]{:S(2)}, u32[]{:S(2)}) collective-permute-start(bf16[1024,256]{1,0:T(8,128)(2,1)} %get-tuple-element.24), channel_id=1, source_target_pairs={{0,4},{4,0},{8,12},{12,8},{16,20},{20,16},{24,28},{28,24},{32,36},... | collective-permute-start | bytes 1572872 | tf_op jit(solution)/shard_map/ppermute | solution.py:308
  94.8 16.5 %collective-permute-start.9 = (bf16[1024,256]{1,0:T(8,128)(2,1)}, bf16[1024,256]{1,0:T(8,128)(2,1)}, u32[]{:S(2)}, u32[]{:S(2)}) collective-permute-start(bf16[1024,256]{1,0:T(8,128)(2,1)} %get-tuple-element.25), channel_id=1, source_target_pairs={{4,32},{32,4},{36,64},{64,36},{68,96},{96,68},{100,8},{8,100},{12,... | collective-permute-start | bytes 1572872 | tf_op jit(solution)/shard_map/ppermute | solution.py:308
  107.3 4.0 %collective-permute-start.4 = (bf16[1024,256]{1,0:T(8,128)(2,1)}, bf16[1024,256]{1,0:T(8,128)(2,1)}, u32[]{:S(2)}, u32[]{:S(2)}) collective-permute-start(bf16[1024,256]{1,0:T(8,128)(2,1)} %get-tuple-element.20), channel_id=1, source_target_pairs={{0,4},{4,0},{8,12},{12,8},{16,20},{20,16},{24,28},{28,24},{32,36},... | collective-permute-start | bytes 1572872 | tf_op jit(solution)/shard_map/ppermute | solution.py:308
  107.3 11.1 %copy-start.1 = (bf16[1024,256]{1,0:T(8,128)(2,1)}, bf16[1024,256]{1,0:T(8,128)(2,1)S(1)}, u32[]{:S(2)}) copy-start(bf16[1024,256]{1,0:T(8,128)(2,1)S(1)} %collective-permute-done.12.refs_10_) | copy-start | bytes 1572868
  107.3 11.1 %collective-permute-start.5 = (bf16[1024,256]{1,0:T(8,128)(2,1)}, bf16[1024,256]{1,0:T(8,128)(2,1)}, u32[]{:S(2)}, u32[]{:S(2)}) collective-permute-start(bf16[1024,256]{1,0:T(8,128)(2,1)} %get-tuple-element.21), channel_id=1, source_target_pairs={{4,32},{32,4},{36,64},{64,36},{68,96},{96,68},{100,8},{8,100},{12,... | collective-permute-start | bytes 1572872 | tf_op jit(solution)/shard_map/ppermute | solution.py:308
  111.3 7.2 %copy-start.2 = (bf16[1024,256]{1,0:T(8,128)(2,1)}, bf16[1024,256]{1,0:T(8,128)(2,1)S(1)}, u32[]{:S(2)}) copy-start(bf16[1024,256]{1,0:T(8,128)(2,1)S(1)} %collective-permute-done.13.refs_11_) | copy-start | bytes 1572868
  111.3 7.1 %copy-start.3 = (bf16[1024,256]{1,0:T(8,128)(2,1)}, bf16[1024,256]{1,0:T(8,128)(2,1)S(1)}, u32[]{:S(2)}) copy-start(bf16[1024,256]{1,0:T(8,128)(2,1)S(1)} %collective-permute-done.8.refs_6_) | copy-start | bytes 1572868

commit v3 on v2

v3 whole, which is shorter than its diff:
```python
import jax
import jax.numpy as jnp
from jax import lax
from jax.experimental import pallas as pl
from jax.experimental.pallas import tpu as pltpu
from jax.sharding import PartitionSpec as P

HEAD_DIM = 128
TILE = 4
ROW_BLOCKS = 2
NEG_FILL = -1e30
SCALE = HEAD_DIM ** (-0.5)
LOG2E = 1.4426950408889634
HEADS_LOCAL = 3
BLOCK = ROW_BLOCKS * TILE**3
STEPS = (-1, 0, 1)

XS, HALVES, STRIPS, CORES = 4, 2, 2, 2


def ctx_of(x, half, strip, core):
    return ((x * HALVES + half) * STRIPS + strip) * CORES + core


def swap_pairs():
    return [(i, i ^ 1) for i in range(32)]


def mask_pairs(flip):
    pairs = []
    for row in range(ROW_BLOCKS):
        for col in range(16):
            pairs.append((row * 16 + col, ctx_of(col % 8 // 2, row ^ flip, col // 8, col % 2)))
    return pairs


def chain_pairs():
    pairs = []
    for half in range(HALVES):
        for link in range(XS * STRIPS - 1):
            a = ctx_of(link % XS, half, link // XS, 1)
            b = ctx_of((link + 1) % XS, half, (link + 1) // XS, 0)
            pairs += [(a, b), (b, a)]
    return pairs


def mask_bias(window_mask):
    place = lax.axis_index("ctx")
    x, strip, core = place // 8, place // 2 % 2, place % 2
    col = strip * 8 + x * 2 + core
    half = place // 4 % 2
    time_blocks = window_mask.shape[1]
    mine = lax.ppermute(window_mask[0], "ctx", mask_pairs(0))
    other = lax.ppermute(window_mask[0], "ctx", mask_pairs(1))
    rows = jnp.stack([jnp.where(half == 0, mine, other), jnp.where(half == 0, other, mine)])
    rows = rows.reshape(ROW_BLOCKS, time_blocks, 3, 3, 3) == 1
    time_pos = jnp.arange(time_blocks)
    has_left = col > 0
    has_right = col < 15
    per_query_row = []
    for rq in range(ROW_BLOCKS):
        per_dt = []
        for dt in range(3):
            inside_t = (time_pos + dt - 1 >= 0) & (time_pos + dt - 1 < time_blocks)
            per_block = []
            for block in range(3):
                per_key_row = []
                for rk in range(ROW_BLOCKS):
                    window = rows[rq, :, dt, rk - rq + 1]
                    left = window[:, 0] & has_left
                    right = window[:, 2] & has_right
                    if block == 0:
                        allowed = window[:, 1]
                        if dt == 1 and rk == rq:
                            allowed = jnp.ones_like(allowed)
                    elif block == 1:
                        allowed = jnp.where(core == 0, right, left)
                    else:
                        allowed = jnp.where(core == 0, left, right)
                    per_key_row.append(allowed & inside_t)
                per_block.append(jnp.stack(per_key_row, axis=1))
            per_dt.append(jnp.stack(per_block, axis=1))
        per_query_row.append(jnp.stack(per_dt, axis=1))
    allowed = jnp.stack(per_query_row, axis=-1).reshape(time_blocks, 18, ROW_BLOCKS)
    bias = jnp.where(allowed, 0.0, NEG_FILL).astype(jnp.float32)
    bias = jnp.broadcast_to(bias[:, :, None, :, None], (time_blocks, 18, TILE, ROW_BLOCKS, TILE * TILE))
    return bias.reshape(time_blocks, 18, BLOCK)


VMEM_LIMIT = 62 * 1024 * 1024


def unpack_kernel(arrived, dk, dv, dq, taken, b0, b1, b2, in_sems, out_sems):
    reads, writes = [], []
    for x in range(XS):
        reads.append(pltpu.make_async_copy(arrived.at[x], taken.at[x], in_sems.at[x]))
        reads[-1].start()
    for x in range(XS):
        reads[x].wait()
        for i, (ref, buf) in enumerate(((dk, b0), (dv, b1), (dq, b2))):
            for strip in range(STRIPS):
                for half in range(HALVES):
                    parts = []
                    for core in range(CORES):
                        lanes = [768 + j * HEAD_DIM if i == 2 else (2 * j + i) * HEAD_DIM for j in range(HEADS_LOCAL)]
                        cells = [taken[x, half, strip, core, :, lane : lane + HEAD_DIM] for lane in lanes]
                        cells = jnp.concatenate(cells, axis=1)
                        parts.append(cells.astype(jnp.float32).reshape(8, TILE, 384))
                    joined = jnp.concatenate(parts, axis=1).astype(jnp.bfloat16)
                    buf[x, :, strip, :, half * 384 : (half + 1) * 384] = joined
            writes.append(pltpu.make_async_copy(buf.at[x], ref.at[:, :, x], out_sems.at[x, i]))
            writes[-1].start()
    for write in writes:
        write.wait()


def unpack(arrived):
    out = jax.ShapeDtypeStruct((8, STRIPS, XS, 8, 768), jnp.bfloat16)
    buf = pltpu.VMEM((XS, 8, STRIPS, 8, 768), jnp.bfloat16)
    lanes = arrived.shape[-1]
    results = pl.pallas_call(
        unpack_kernel,
        in_specs=[pl.BlockSpec(memory_space=pl.ANY)],
        out_specs=[pl.BlockSpec(memory_space=pl.ANY)] * 3,
        out_shape=[out] * 3,
        scratch_shapes=[
            pltpu.VMEM((XS, HALVES, STRIPS, CORES, 32, lanes), jnp.bfloat16),
            buf,
            buf,
            buf,
            pltpu.SemaphoreType.DMA((XS,)),
            pltpu.SemaphoreType.DMA((XS, 3)),
        ],
        compiler_params=pltpu.CompilerParams(vmem_limit_bytes=VMEM_LIMIT),
        cost_estimate=pl.CostEstimate(flops=0, bytes_accessed=4_700_000, transcendentals=0),
        name="unpack",
    )(arrived.reshape(XS, HALVES, STRIPS, CORES, 32, lanes))
    return [r.reshape(1, 8, 64, 768) for r in results]


def block_bias(bias_ref, t, dt, block):
    rows = []
    for rk in range(ROW_BLOCKS):
        row = (dt * 3 + block) * 2 + rk
        rows.append(jnp.broadcast_to(bias_ref[t, row : row + 1, :], (TILE * TILE, BLOCK)))
    return jnp.concatenate(rows * TILE, axis=0)


ANY = pl.BlockSpec(memory_space=pl.ANY)


def pack_kernel(blocks, ins, *refs):
    count = len(ins)
    inputs, out, taken, (packed, in_sems, out_sems) = refs[:count], refs[count], refs[count + 1 : -3], refs[-3:]
    reads, writes = [], []
    for x in range(XS):
        for i, (first, heads) in enumerate(ins):
            for half in range(HALVES):
                lane = (half * HEADS_LOCAL + first) * HEAD_DIM
                source = inputs[i].at[:, :, x, :, lane : lane + heads * HEAD_DIM]
                reads.append(pltpu.make_async_copy(source, taken[i].at[x, half], in_sems.at[x, i, half]))
                reads[-1].start()
    each = count * HALVES
    for x in range(XS):
        for read in reads[x * each : (x + 1) * each]:
            read.wait()
        for half in range(HALVES):
            for strip in range(STRIPS):
                for core in range(CORES):
                    for n, (i, j) in enumerate(blocks):
                        lane = (j - ins[i][0]) * HEAD_DIM
                        cells = taken[i][x, half, :, strip, :, lane : lane + HEAD_DIM].astype(jnp.float32)
                        cells = cells[:, core * TILE : (core + 1) * TILE].reshape(32, HEAD_DIM)
                        to = n * HEAD_DIM
                        packed[x, half, strip, core, :, to : to + HEAD_DIM] = cells.astype(jnp.bfloat16)
            writes.append(pltpu.make_async_copy(packed.at[x, half], out.at[x, half], out_sems.at[x, half]))
            writes[-1].start()
    for write in writes:
        write.wait()


def pack(tensors, ins, blocks, name):
    views = [t.reshape(8, STRIPS, XS, 8, 768) for t in tensors]
    out = (XS, HALVES, STRIPS, CORES, 32, len(blocks) * HEAD_DIM)
    taken = [pltpu.VMEM((XS, HALVES, 8, STRIPS, 8, heads * HEAD_DIM), jnp.bfloat16) for _, heads in ins]
    return pl.pallas_call(
        lambda *refs: pack_kernel(blocks, ins, *refs),
        in_specs=[ANY] * len(views),
        out_specs=ANY,
        out_shape=jax.ShapeDtypeStruct(out, jnp.bfloat16),
        scratch_shapes=taken
        + [
            pltpu.VMEM(out, jnp.bfloat16),
            pltpu.SemaphoreType.DMA((XS, len(ins), HALVES)),
            pltpu.SemaphoreType.DMA((XS, HALVES)),
        ],
        compiler_params=pltpu.CompilerParams(vmem_limit_bytes=VMEM_LIMIT),
        cost_estimate=pl.CostEstimate(flops=0, bytes_accessed=4_000_000, transcendentals=0),
        name=name,
    )(*views).reshape(32, 32, len(blocks) * HEAD_DIM)


def grads_kernel(lanes, *refs):
    qg_lane, own_lane, near_lane, head = lanes
    bias_ref, qg, own, near, far = refs[:5]
    grads, to_near, to_far = refs[-3:]
    time_blocks = bias_ref.shape[0]
    wide = 2 * HEAD_DIM
    sources = ((own, own_lane), (near, near_lane), (far, 0))
    mine, dq_lane = head * wide, 3 * wide + head * HEAD_DIM
    targets = ((grads, mine), (to_near, mine), (to_far, 0))
    weights, pairs = {}, {}

    def finish(tk):
        near_ts = [t for t in (tk - 1, tk, tk + 1) if 0 <= t < time_blocks]
        w = jnp.concatenate([weights[t] for t in near_ts], axis=0)
        x = [
            jnp.concatenate([pairs[t][block][tk - max(t - 1, 0)] for t in near_ts], axis=1)
            for block in range(3)
        ]
        r = jnp.dot(jnp.concatenate(x, axis=0), w, preferred_element_type=jnp.float32)
        for block, (target, lane) in enumerate(targets):
            part = r[block * BLOCK : (block + 1) * BLOCK]
            part = jnp.concatenate([part[:, :HEAD_DIM] * SCALE, part[:, HEAD_DIM:]], axis=1)
            target[pl.ds(tk * BLOCK, BLOCK), lane : lane + wide] = part.astype(jnp.bfloat16)

    for t in range(time_blocks):
        low, high = max(t - 1, 0), min(t + 1, time_blocks - 1)
        here = pl.ds(t * BLOCK, BLOCK)
        q = qg[here, qg_lane : qg_lane + HEAD_DIM]
        g = qg[here, qg_lane + HEAD_DIM : qg_lane + wide]
        zero = jnp.zeros_like(q)
        both = jnp.concatenate(
            [jnp.concatenate([q, zero], axis=1), jnp.concatenate([zero, g], axis=1)], axis=0
        )
        weights[t] = both
        window = pl.ds(low * BLOCK, (high - low + 1) * BLOCK)
        scores, probs = [], []
        top = None
        for block, (source, lane) in enumerate(sources):
            r = lax.dot_general(
                source[window, lane : lane + wide],
                both,
                (((1,), (1,)), ((), ())),
                preferred_element_type=jnp.float32,
            )
            bias = [block_bias(bias_ref, t, near_t - t + 1, block) for near_t in range(low, high + 1)]
            s = r[:, :BLOCK] * (SCALE * LOG2E) + jnp.concatenate(bias, axis=0)
            block_top = jnp.max(s, axis=0, keepdims=True)
            top = block_top if top is None else jnp.maximum(top, block_top)
            scores.append(s)
            probs.append(r[:, BLOCK:])
        total = jnp.zeros((1, BLOCK), jnp.float32)
        dots = jnp.zeros((1, BLOCK), jnp.float32)
        exps = []
        for s, pg in zip(scores, probs):
            e = jnp.exp2(s - top)
            total += jnp.sum(e, axis=0, keepdims=True)
            dots += jnp.sum(e * pg, axis=0, keepdims=True)
            exps.append(e)
        inv = 1.0 / total
        row_dot = dots * inv
        slopes, pairs[t] = [], []
        for e, pg in zip(exps, probs):
            p = e * inv
            ds = (p * (pg - row_dot)).astype(jnp.bfloat16)
            pair = jnp.concatenate([ds, p.astype(jnp.bfloat16)], axis=1)
            pairs[t].append([pair[i * BLOCK : (i + 1) * BLOCK] for i in range(high - low + 1)])
            slopes.append(ds)
        keys = [source[window, lane : lane + HEAD_DIM] for source, lane in sources]
        dq = lax.dot_general(
            jnp.concatenate(slopes, axis=0),
            jnp.concatenate(keys, axis=0),
            (((0,), (0,)), ((), ())),
            preferred_element_type=jnp.float32,
        )
        grads[here, dq_lane : dq_lane + HEAD_DIM] = (dq * SCALE).astype(jnp.bfloat16)
        if t > 0:
            finish(t - 1)
    finish(time_blocks - 1)


VMEM = pl.BlockSpec(memory_space=pltpu.VMEM)
SMALL_LIMIT = 12 * 1024 * 1024


def head_grads(bias, everything, near, far, shared, head, after):
    rows = everything.shape[0]
    wide = 2 * HEAD_DIM
    lanes = ((HEADS_LOCAL + head) * wide, head * wide, head * wide, head)
    return pl.pallas_call(
        lambda *refs: grads_kernel(lanes, *refs),
        in_specs=[VMEM] * (5 + len(shared)) + [ANY] * len(after),
        out_specs=[VMEM] * 3,
        out_shape=[
            jax.ShapeDtypeStruct((rows, 9 * HEAD_DIM), jnp.bfloat16),
            jax.ShapeDtypeStruct((rows, 6 * HEAD_DIM), jnp.bfloat16),
            jax.ShapeDtypeStruct((rows, wide), jnp.bfloat16),
        ],
        input_output_aliases={5: 0, 6: 1} if shared else {},
        compiler_params=pltpu.CompilerParams(vmem_limit_bytes=SMALL_LIMIT),
        cost_estimate=pl.CostEstimate(flops=20_000_000_000, bytes_accessed=4_500_000, transcendentals=1_200_000),
        name="head_grads",
    )(bias, everything, everything, near, far, *shared, *after)


def add_kernel(first, grads, near, *refs):
    fars, out = refs[:-1], refs[-1]
    wide = 2 * HEAD_DIM
    for j, far in enumerate(fars):
        lanes = slice((first + j) * wide, (first + j + 1) * wide)
        total = grads[:, lanes].astype(jnp.float32) + near[:, lanes].astype(jnp.float32)
        out[:, lanes] = (total + far[...].astype(jnp.float32)).astype(jnp.bfloat16)


def add_halos(grads, near, fars, first):
    return pl.pallas_call(
        lambda *refs: add_kernel(first, *refs),
        in_specs=[VMEM] * (2 + len(fars)),
        out_specs=VMEM,
        out_shape=jax.ShapeDtypeStruct(grads.shape, grads.dtype),
        input_output_aliases={0: 0},
        compiler_params=pltpu.CompilerParams(vmem_limit_bytes=SMALL_LIMIT),
        cost_estimate=pl.CostEstimate(flops=0, bytes_accessed=1000, transcendentals=0),
        name="add_halos",
    )(grads, near, *fars)


def split_kernel(arrived, bias, near, *fars):
    wide = 2 * HEAD_DIM
    for j, far in enumerate(fars):
        far[...] = arrived[:, j * wide : (j + 1) * wide]
    near[...] = arrived[:, : len(fars) * wide]


def split(arrived, bias):
    rows, wide = arrived.shape[0], 2 * HEAD_DIM
    far = jax.ShapeDtypeStruct((rows, wide), arrived.dtype)
    near = jax.ShapeDtypeStruct((rows, HEADS_LOCAL * wide), arrived.dtype)
    near, *fars = pl.pallas_call(
        split_kernel,
        in_specs=[VMEM, ANY],
        out_specs=[VMEM] * (1 + HEADS_LOCAL),
        out_shape=[near] + [far] * HEADS_LOCAL,
        compiler_params=pltpu.CompilerParams(vmem_limit_bytes=SMALL_LIMIT),
        cost_estimate=pl.CostEstimate(flops=0, bytes_accessed=1000, transcendentals=0),
        name="split",
    )(arrived, bias)
    return near, fars


def ordered(arrays, after):
    count = len(arrays)
    return pl.pallas_call(
        lambda *refs: None,
        in_specs=[VMEM] * count + [ANY],
        out_specs=[VMEM] * count,
        out_shape=[jax.ShapeDtypeStruct(array.shape, array.dtype) for array in arrays],
        input_output_aliases={i: i for i in range(count)},
        compiler_params=pltpu.CompilerParams(vmem_limit_bytes=SMALL_LIMIT),
        cost_estimate=pl.CostEstimate(flops=0, bytes_accessed=1000, transcendentals=0),
        name="ordered",
    )(*arrays, after)


def shards(queries, keys, values, out_grad, window_mask):
    swap, chain = swap_pairs(), chain_pairs()
    everything = tuple((i, j) for j in range(HEADS_LOCAL) for i in (0, 1))
    everything += tuple((i, j) for j in range(HEADS_LOCAL) for i in (2, 3))
    packed = pack((keys, values, queries, out_grad), ((0, 3),) * 4, everything, "pack")
    packed, window_mask = lax.optimization_barrier((packed, window_mask))
    arrived = lax.all_to_all(packed, "ctx", 0, 0, tiled=True).reshape(1024, 12 * HEAD_DIM)
    bias = mask_bias(window_mask)
    for_near, for_far = split(arrived, bias)
    fars = [lax.ppermute(part, "ctx", chain) for part in for_far]
    near = lax.ppermute(for_near, "ctx", swap)
    shared, back = (), []
    for j in range(HEADS_LOCAL):
        grads, to_near, to_far = head_grads(bias, arrived, near, fars[j], shared, j, back[:1] if j == 2 else [])
        shared = (grads, to_near)
        if j == 2:
            to_far, to_near = ordered((to_far, to_near), back[1])
        back.append(lax.ppermute(to_far, "ctx", chain))
    near_back = lax.ppermute(to_near, "ctx", swap)
    grads = add_halos(grads, near_back, back[:2], 0)
    grads = add_halos(grads, near_back, back[2:], 2)
    grads = lax.all_to_all(grads.reshape(32, 32, 9 * HEAD_DIM), "ctx", 0, 0, tiled=True)
    dk, dv, dq = unpack(grads)
    return dq, dk, dv


def solution(mesh):
    tokens = P("ctx", None, None, "head")
    return jax.shard_map(
        shards,
        mesh=mesh,
        in_specs=(tokens, tokens, tokens, tokens, P("ctx", None, None)),
        out_specs=(tokens, tokens, tokens),
        check_vma=False,
    )
```

time: 167 us -> 154 us (0.922)
  Pallas kernels: 36.7 us -> 26.1 us
  starting transfers between devices: 35.8 us -> 28.1 us
  waiting for transfers between devices: 45.9 us -> 51.3 us
  local copies, waits for them, and re-layouts: 5.85 us -> 3.49 us
  blocking collectives: 40.3 us -> 42.4 us
    pallas_call x5 -> x8, Pallas kernels: 34.1 us -> 23.4 us  [the longest x3 18.3 us: head_grads(): pl.pallas_call(lambda *refs: grads_kernel(lanes, *refs), in_specs=[VMEM]...]
    ppermute x12 -> x8, waiting for transfers between devices: 7.16 us -> 15.8 us  [the longest x3 8.45 us: shards(): back.append(lax.ppermute(to_far, 'ctx', chain))]
    ppermute x12 -> x8, starting transfers between devices: 21.3 us -> 14 us  [the longest x3 7.47 us: shards(): fars = [lax.ppermute(part, 'ctx', chain) for part in for_far]]
    all_to_all x1, starting transfers between devices: 6.27 us -> 9.64 us  [shards(): lax.all_to_all(packed, 'ctx', 0, 0, tiled=True).reshape(1024, 12 * HEAD_DIM)]
    all_to_all x1, waiting for transfers between devices: 38.7 us -> 35.5 us  [shards(): lax.all_to_all(packed, 'ctx', 0, 0, tiled=True).reshape(1024, 12 * HEAD_DIM)]
    ppermute x1, starting transfers between devices: 6.9 us -> 3.81 us  [mask_bias(): other = lax.ppermute(window_mask[0], 'ctx', mask_pairs(1))]
    unnamed x14 -> x2, local copies, waits for them, and re-layouts: 2.45 us -> 0.01 us
    all_to_all x1, blocking collectives: 40.3 us -> 42.4 us  [shards(): lax.all_to_all(grads.reshape(32, 32, 9 * HEAD_DIM), 'ctx', 0, 0, tiled=True)]
  transfers between devices with their start and end apart: 15 -> 11, of which waited for: 2 -> 6; matrix products, arithmetic and copies ran while one was open for 2% -> 3% of each run, Pallas kernels for 18% -> 13%
where the time goes in v3:
time: 154 us; the launch traced here: 153 us
  waiting for transfers between devices  51.3 us (33%)
  blocking collectives  42.4 us (28%)
  starting transfers between devices  28.1 us (18%)
  Pallas kernels  26.1 us (17%)
  local copies, waits for them, and re-layouts  3.49 us (2%)
    all_to_all x1, blocking collectives, shards(): lax.all_to_all(grads.reshape(32, 32, 9 * HEAD_DIM), 'ctx', 0, 0, tiled=True)  42.4 us
    all_to_all x1, waiting for transfers between devices, shards(): lax.all_to_all(packed, 'ctx', 0, 0, tiled=True).reshape(1024, 12 * HEAD_DIM)  35.5 us
    pallas_call x3, Pallas kernels, head_grads(): pl.pallas_call(lambda *refs: grads_kernel(lanes, *refs), in_specs=[VMEM]...  18.3 us
    all_to_all x1, starting transfers between devices, shards(): lax.all_to_all(packed, 'ctx', 0, 0, tiled=True).reshape(1024, 12 * HEAD_DIM)  9.64 us
    ppermute x3, waiting for transfers between devices, shards(): back.append(lax.ppermute(to_far, 'ctx', chain))  8.45 us
    ppermute x3, starting transfers between devices, shards(): fars = [lax.ppermute(part, 'ctx', chain) for part in for_far]  7.47 us
    ppermute x3, starting transfers between devices, shards(): back.append(lax.ppermute(to_far, 'ctx', chain))  6.04 us
    ppermute x3, waiting for transfers between devices, shards(): fars = [lax.ppermute(part, 'ctx', chain) for part in for_far]  6 us
  transfers between devices with their start and end apart: 11, of which 6 were waited for; matrix products, arithmetic and copies ran while one was open for 3% of the time, Pallas kernels for 13%

profile of v3, /device:TPU:1, one launch (start us, length us, event | category | flops | bytes accessed | tf_op | source)
XLA Modules:
  0.0 153.1 jit_solution(3071130509510857422)
XLA Ops:
  0.6 0.0 copy-start
  0.6 3.3 %pack.1 = bf16[4,2,2,2,32,1536]{5,4,3,2,1,0:T(8,128)(2,1)} custom-call(bf16[8,2,4,8,768]{4,3,2,1,0:T(8,128)(2,1)} %bitcast.110, bf16[8,2,4,8,768]{4,3,2,1,0:T(8,128)(2,1)} %bitcast.111, bf16[8,2,4,8,768]{4,3,2,1,0:T(8,128)(2,1)} %bitcast.112, bf16[8,2,4,8,768]{4,3,2,1,0:T(8,128)(2,1)} %bitcast.113), custom_call_target="tpu_custom_call" | custom-call | bytes 4000000 | tf_op jit(solution)/shard_map/pack/pallas_call | solution.py:186
  4.0 0.0 copy-done
  4.0 3.8 %collective-permute-start.1 = (s32[8,27]{1,0:T(8,128)S(1)}, s32[8,27]{1,0:T(8,128)S(1)}, u32[]{:S(2)}, u32[]{:S(2)}) collective-permute-start(s32[8,27]{1,0:T(8,128)S(1)} %bitcast.123), channel_id=1, source_target_pairs={{0,16},{4,20},{8,48},{12,52},{16,80},{20,84},{24,112},{28,116},{32... | collective-permute-start | bytes 2600 | tf_op jit(solution)/shard_map/ppermute | solution.py:54
  7.8 0.6 collective-permute-start
  8.4 9.6 %all-to-all-start = ((bf16[32,32,1536]{2,1,0:T(8,128)(2,1)}), bf16[32,32,1536]{2,1,0:T(8,128)(2,1)S(1)}, u32[]{:S(2)}, u32[]{:S(2)}) async-start(bf16[32,32,1536]{2,1,0:T(8,128)(2,1)} %bitcast.108), calls=%async_computation | async-start | bytes 6291456 | tf_op jit(solution)/shard_map/all_to_all | solution.py:372
  18.2 0.0 collective-permute-done.1
  18.2 0.0 collective-permute-done
  18.2 0.1 copy.39
  18.3 0.1 copy.40
  19.1 0.1 copy.49
  19.3 0.1 copy.50
  19.4 0.1 copy.51
  19.5 1.0 broadcast_in_dim.16
  20.6 1.8 %reshape.148 = f32[8,18,128]{2,0,1:T(8,128)S(1)} reshape(f32[8,18,4,2,16]{4,3,2,0,1:T(2,128)} %broadcast_in_dim.16) | data formatting | bytes 147456 | tf_op jit(solution)/shard_map/reshape | solution.py:87
  22.4 35.5 %all-to-all-done = bf16[32,32,1536]{2,1,0:T(8,128)(2,1)S(1)} async-done(((bf16[32,32,1536]{2,1,0:T(8,128)(2,1)}), bf16[32,32,1536]{2,1,0:T(8,128)(2,1)S(1)}, u32[]{:S(2)}, u32[]{:S(2)}) %all-to-all-start) | async-done | bytes 3145760 | tf_op jit(solution)/shard_map/all_to_all | solution.py:372
  57.8 0.2 split.1
  58.1 0.5 collective-permute-start.2
  58.6 1.9 %collective-permute-start.5 = (bf16[1024,256]{1,0:T(8,128)(2,1)S(1)}, bf16[1024,256]{1,0:T(8,128)(2,1)S(1)}, u32[]{:S(2)}, u32[]{:S(2)}) collective-permute-start(bf16[1024,256]{1,0:T(8,128)(2,1)S(1)} %get-tuple-element.28), channel_id=1, source_target_pairs={{4,32},{32,4},{36,64},{64,36},{68,96},{96,68},{100,8},{8,100},{12,... | collective-permute-start | bytes 1572872 | tf_op jit(solution)/shard_map/ppermute | solution.py:375
  60.5 3.6 %collective-permute-start.3 = (bf16[1024,256]{1,0:T(8,128)(2,1)S(1)}, bf16[1024,256]{1,0:T(8,128)(2,1)S(1)}, u32[]{:S(2)}, u32[]{:S(2)}) collective-permute-start(bf16[1024,256]{1,0:T(8,128)(2,1)S(1)} %get-tuple-element.26), channel_id=1, source_target_pairs={{4,32},{32,4},{36,64},{64,36},{68,96},{96,68},{100,8},{8,100},{12,... | collective-permute-start | bytes 1572872 | tf_op jit(solution)/shard_map/ppermute | solution.py:375
  64.1 1.9 %collective-permute-start.4 = (bf16[1024,256]{1,0:T(8,128)(2,1)S(1)}, bf16[1024,256]{1,0:T(8,128)(2,1)S(1)}, u32[]{:S(2)}, u32[]{:S(2)}) collective-permute-start(bf16[1024,256]{1,0:T(8,128)(2,1)S(1)} %get-tuple-element.27), channel_id=1, source_target_pairs={{4,32},{32,4},{36,64},{64,36},{68,96},{96,68},{100,8},{8,100},{12,... | collective-permute-start | bytes 1572872 | tf_op jit(solution)/shard_map/ppermute | solution.py:375
  66.0 3.0 %collective-permute-done.5.refs_4_ = bf16[1024,256]{1,0:T(8,128)(2,1)S(1)} collective-permute-done((bf16[1024,256]{1,0:T(8,128)(2,1)S(1)}, bf16[1024,256]{1,0:T(8,128)(2,1)S(1)}, u32[]{:S(2)}, u32[]{:S(2)}) %collective-permute-start.5) | collective-permute-done | bytes 524320 | tf_op jit(solution)/shard_map/ppermute | solution.py:375
  69.0 0.0 collective-permute-done.2.refs_3_
  69.0 6.1 %head_grads.3 = (bf16[1024,1152]{1,0:T(8,128)(2,1)S(1)}, bf16[1024,768]{1,0:T(8,128)(2,1)S(1)}, bf16[1024,256]{1,0:T(8,128)(2,1)S(1)}) custom-call(f32[8,18,128]{2,1,0:T(8,128)S(1)} %copy.55.bias.refs_0_, bf16[1024,1536]{1,0:T(8,128)(2,1)S(1)} %bitcast.102, bf16[1024,1536]{1,0:T(8,128)(2,1)S(1)} %bitcast.103, ...), custom_call_target="tpu_custom_call" | custom-call | flops 20000000000 | bytes 4500000 | tf_op jit(solution)/shard_map/head_grads/pallas_call | solution.py:291
  75.2 2.1 %collective-permute-start.6 = (bf16[1024,256]{1,0:T(8,128)(2,1)S(1)}, bf16[1024,256]{1,0:T(8,128)(2,1)S(1)}, u32[]{:S(2)}, u32[]{:S(2)}) collective-permute-start(bf16[1024,256]{1,0:T(8,128)(2,1)S(1)} %get-tuple-element.33), channel_id=1, source_target_pairs={{4,32},{32,4},{36,64},{64,36},{68,96},{96,68},{100,8},{8,100},{12,... | collective-permute-start | bytes 1572872 | tf_op jit(solution)/shard_map/ppermute | solution.py:383
  77.3 3.0 %collective-permute-done.4.refs_4_ = bf16[1024,256]{1,0:T(8,128)(2,1)S(1)} collective-permute-done((bf16[1024,256]{1,0:T(8,128)(2,1)S(1)}, bf16[1024,256]{1,0:T(8,128)(2,1)S(1)}, u32[]{:S(2)}, u32[]{:S(2)}) %collective-permute-start.4) | collective-permute-done | bytes 524320 | tf_op jit(solution)/shard_map/ppermute | solution.py:375
  80.3 6.1 %head_grads.4 = (bf16[1024,1152]{1,0:T(8,128)(2,1)S(1)}, bf16[1024,768]{1,0:T(8,128)(2,1)S(1)}, bf16[1024,256]{1,0:T(8,128)(2,1)S(1)}) custom-call(f32[8,18,128]{2,1,0:T(8,128)S(1)} %copy.55.bias.refs_0_, bf16[1024,1536]{1,0:T(8,128)(2,1)S(1)} %bitcast.104, bf16[1024,1536]{1,0:T(8,128)(2,1)S(1)} %bitcast.105, ...), custom_call_target="tpu_custom_call", output_to_operand_aliasing={{0}: (5, {}), {1}: (6, {})} | custom-call | flops 20000000000 | bytes 4500000 | tf_op jit(solution)/shard_map/head_grads/pallas_call | solution.py:291
  86.4 1.9 %collective-permute-start.7 = (bf16[1024,256]{1,0:T(8,128)(2,1)S(1)}, bf16[1024,256]{1,0:T(8,128)(2,1)S(1)}, u32[]{:S(2)}, u32[]{:S(2)}) collective-permute-start(bf16[1024,256]{1,0:T(8,128)(2,1)S(1)} %get-tuple-element.37), channel_id=1, source_target_pairs={{4,32},{32,4},{36,64},{64,36},{68,96},{96,68},{100,8},{8,100},{12,... | collective-permute-start | bytes 1572872 | tf_op jit(solution)/shard_map/ppermute | solution.py:383
  88.3 0.0 collective-permute-done.3.refs_4_
  88.3 0.0 collective-permute-done.6.refs_7_.refs_2_
  88.3 6.1 %head_grads.5 = (bf16[1024,1152]{1,0:T(8,128)(2,1)S(1)}, bf16[1024,768]{1,0:T(8,128)(2,1)S(1)}, bf16[1024,256]{1,0:T(8,128)(2,1)S(1)}) custom-call(f32[8,18,128]{2,1,0:T(8,128)S(1)} %copy.55.bias.refs_0_, bf16[1024,1536]{1,0:T(8,128)(2,1)S(1)} %bitcast.106, bf16[1024,1536]{1,0:T(8,128)(2,1)S(1)} %bitcast.107, ...), custom_call_target="tpu_custom_call", output_to_operand_aliasing={{0}: (5, {}), {1}: (6, {})} | custom-call | flops 20000000000 | bytes 4500000 | tf_op jit(solution)/shard_map/head_grads/pallas_call | solution.py:291
  94.5 2.4 %collective-permute-done.7.refs_2_.refs_3_ = bf16[1024,256]{1,0:T(8,128)(2,1)S(1)} collective-permute-done((bf16[1024,256]{1,0:T(8,128)(2,1)S(1)}, bf16[1024,256]{1,0:T(8,128)(2,1)S(1)}, u32[]{:S(2)}, u32[]{:S(2)}) %collective-permute-start.7) | collective-permute-done | bytes 524320 | tf_op jit(solution)/shard_map/ppermute | solution.py:383
  96.9 0.0 collective-permute-start.8
  96.9 2.0 %collective-permute-start.9 = (bf16[1024,256]{1,0:T(8,128)(2,1)S(1)}, bf16[1024,256]{1,0:T(8,128)(2,1)S(1)}, u32[]{:S(2)}, u32[]{:S(2)}) collective-permute-start(bf16[1024,256]{1,0:T(8,128)(2,1)S(1)} %get-tuple-element.39), channel_id=1, source_target_pairs={{4,32},{32,4},{36,64},{64,36},{68,96},{96,68},{100,8},{8,100},{12,... | collective-permute-start | bytes 1572872 | tf_op jit(solution)/shard_map/ppermute | solution.py:383
  98.9 1.4 collective-permute-done.8.refs_1_
  100.3 1.1 add_halos.2.refs_0_
  101.4 6.0 %collective-permute-done.9.refs_2_ = bf16[1024,256]{1,0:T(8,128)(2,1)S(1)} collective-permute-done((bf16[1024,256]{1,0:T(8,128)(2,1)S(1)}, bf16[1024,256]{1,0:T(8,128)(2,1)S(1)}, u32[]{:S(2)}, u32[]{:S(2)}) %collective-permute-start.9) | collective-permute-done | bytes 524320 | tf_op jit(solution)/shard_map/ppermute | solution.py:383
  107.4 0.5 add_halos.3
  107.9 42.4 %all_to_all.10 = bf16[32,32,1152]{2,1,0:T(8,128)(2,1)} all-to-all(bf16[32,32,1152]{2,1,0:T(8,128)(2,1)S(1)} %bitcast.100), channel_id=1, replica_groups=mesh['ctx'=32,'head'=4] {'ctx'}, dimensions={0} | all-to-all | bytes 4718592 | tf_op jit(solution)/shard_map/all_to_all | solution.py:387
  150.3 2.6 %unpack.1 = (bf16[8,2,4,8,768]{4,3,2,1,0:T(8,128)(2,1)}, bf16[8,2,4,8,768]{4,3,2,1,0:T(8,128)(2,1)}, bf16[8,2,4,8,768]{4,3,2,1,0:T(8,128)(2,1)}) custom-call(bf16[4,2,2,2,32,1152]{5,4,3,2,1,0:T(8,128)(2,1)} %bitcast.109), custom_call_target="tpu_custom_call" | custom-call | bytes 4700000 | tf_op jit(solution)/shard_map/unpack/pallas_call | solution.py:121
  (50 shorter events, 0.5 us)
Async XLA Ops:
  0.6 3.3 %copy-start = (s32[1,8,27]{2,1,0:T(8,128)S(1)}, s32[1,8,27]{2,1,0:T(8,128)}, u32[]{:S(2)}) copy-start(s32[1,8,27]{2,1,0:T(8,128)} %param.9) | copy-start | bytes 2596
  4.0 14.2 %collective-permute-start.1 = (s32[8,27]{1,0:T(8,128)S(1)}, s32[8,27]{1,0:T(8,128)S(1)}, u32[]{:S(2)}, u32[]{:S(2)}) collective-permute-start(s32[8,27]{1,0:T(8,128)S(1)} %bitcast.123), channel_id=1, source_target_pairs={{0,16},{4,20},{8,48},{12,52},{16,80},{20,84},{24,112},{28,116},{32... | collective-permute-start | bytes 2600 | tf_op jit(solution)/shard_map/ppermute | solution.py:54
  7.8 10.4 %collective-permute-start = (s32[8,27]{1,0:T(8,128)S(1)}, s32[8,27]{1,0:T(8,128)S(1)}, u32[]{:S(2)}, u32[]{:S(2)}) collective-permute-start(s32[8,27]{1,0:T(8,128)S(1)} %bitcast.124), channel_id=1, source_target_pairs={{0,0},{4,4},{8,32},{12,36},{16,64},{20,68},{24,96},{28,100},{32,8}... | collective-permute-start | bytes 2600 | tf_op jit(solution)/shard_map/ppermute | solution.py:53
  8.4 49.4 %all-to-all-start = ((bf16[32,32,1536]{2,1,0:T(8,128)(2,1)}), bf16[32,32,1536]{2,1,0:T(8,128)(2,1)S(1)}, u32[]{:S(2)}, u32[]{:S(2)}) async-start(bf16[32,32,1536]{2,1,0:T(8,128)(2,1)} %bitcast.108), calls=%async_computation | async-start | bytes 6291456 | tf_op jit(solution)/shard_map/all_to_all | solution.py:372
  58.1 11.0 %collective-permute-start.2 = (bf16[1024,768]{1,0:T(8,128)(2,1)S(1)}, bf16[1024,768]{1,0:T(8,128)(2,1)S(1)}, u32[]{:S(2)}, u32[]{:S(2)}) collective-permute-start(bf16[1024,768]{1,0:T(8,128)(2,1)S(1)} %get-tuple-element.25), channel_id=1, source_target_pairs={{0,4},{4,0},{8,12},{12,8},{16,20},{20,16},{24,28},{28,24},{32,36},... | collective-permute-start | bytes 4718600 | tf_op jit(solution)/shard_map/ppermute | solution.py:376
  58.6 10.5 %collective-permute-start.5 = (bf16[1024,256]{1,0:T(8,128)(2,1)S(1)}, bf16[1024,256]{1,0:T(8,128)(2,1)S(1)}, u32[]{:S(2)}, u32[]{:S(2)}) collective-permute-start(bf16[1024,256]{1,0:T(8,128)(2,1)S(1)} %get-tuple-element.28), channel_id=1, source_target_pairs={{4,32},{32,4},{36,64},{64,36},{68,96},{96,68},{100,8},{8,100},{12,... | collective-permute-start | bytes 1572872 | tf_op jit(solution)/shard_map/ppermute | solution.py:375
  60.5 27.9 %collective-permute-start.3 = (bf16[1024,256]{1,0:T(8,128)(2,1)S(1)}, bf16[1024,256]{1,0:T(8,128)(2,1)S(1)}, u32[]{:S(2)}, u32[]{:S(2)}) collective-permute-start(bf16[1024,256]{1,0:T(8,128)(2,1)S(1)} %get-tuple-element.26), channel_id=1, source_target_pairs={{4,32},{32,4},{36,64},{64,36},{68,96},{96,68},{100,8},{8,100},{12,... | collective-permute-start | bytes 1572872 | tf_op jit(solution)/shard_map/ppermute | solution.py:375
  64.1 16.2 %collective-permute-start.4 = (bf16[1024,256]{1,0:T(8,128)(2,1)S(1)}, bf16[1024,256]{1,0:T(8,128)(2,1)S(1)}, u32[]{:S(2)}, u32[]{:S(2)}) collective-permute-start(bf16[1024,256]{1,0:T(8,128)(2,1)S(1)} %get-tuple-element.27), channel_id=1, source_target_pairs={{4,32},{32,4},{36,64},{64,36},{68,96},{96,68},{100,8},{8,100},{12,... | collective-permute-start | bytes 1572872 | tf_op jit(solution)/shard_map/ppermute | solution.py:375
  75.2 13.2 %collective-permute-start.6 = (bf16[1024,256]{1,0:T(8,128)(2,1)S(1)}, bf16[1024,256]{1,0:T(8,128)(2,1)S(1)}, u32[]{:S(2)}, u32[]{:S(2)}) collective-permute-start(bf16[1024,256]{1,0:T(8,128)(2,1)S(1)} %get-tuple-element.33), channel_id=1, source_target_pairs={{4,32},{32,4},{36,64},{64,36},{68,96},{96,68},{100,8},{8,100},{12,... | collective-permute-start | bytes 1572872 | tf_op jit(solution)/shard_map/ppermute | solution.py:383
  86.4 10.5 %collective-permute-start.7 = (bf16[1024,256]{1,0:T(8,128)(2,1)S(1)}, bf16[1024,256]{1,0:T(8,128)(2,1)S(1)}, u32[]{:S(2)}, u32[]{:S(2)}) collective-permute-start(bf16[1024,256]{1,0:T(8,128)(2,1)S(1)} %get-tuple-element.37), channel_id=1, source_target_pairs={{4,32},{32,4},{36,64},{64,36},{68,96},{96,68},{100,8},{8,100},{12,... | collective-permute-start | bytes 1572872 | tf_op jit(solution)/shard_map/ppermute | solution.py:383
  96.9 3.4 %collective-permute-start.8 = (bf16[1024,768]{1,0:T(8,128)(2,1)S(1)}, bf16[1024,768]{1,0:T(8,128)(2,1)S(1)}, u32[]{:S(2)}, u32[]{:S(2)}) collective-permute-start(bf16[1024,768]{1,0:T(8,128)(2,1)S(1)} %get-tuple-element.38), channel_id=1, source_target_pairs={{0,4},{4,0},{8,12},{12,8},{16,20},{20,16},{24,28},{28,24},{32,36},... | collective-permute-start | bytes 4718600 | tf_op jit(solution)/shard_map/ppermute | solution.py:384
  96.9 10.5 %collective-permute-start.9 = (bf16[1024,256]{1,0:T(8,128)(2,1)S(1)}, bf16[1024,256]{1,0:T(8,128)(2,1)S(1)}, u32[]{:S(2)}, u32[]{:S(2)}) collective-permute-start(bf16[1024,256]{1,0:T(8,128)(2,1)S(1)} %get-tuple-element.39), channel_id=1, source_target_pairs={{4,32},{32,4},{36,64},{64,36},{68,96},{96,68},{100,8},{8,100},{12,... | collective-permute-start | bytes 1572872 | tf_op jit(solution)/shard_map/ppermute | solution.py:383

commit v4 on v3

v4 whole, which is shorter than its diff:
```python
import jax
import jax.numpy as jnp
from jax import lax
from jax.experimental import pallas as pl
from jax.experimental.pallas import tpu as pltpu
from jax.sharding import PartitionSpec as P

HEAD_DIM = 128
TILE = 4
ROW_BLOCKS = 2
NEG_FILL = -1e30
SCALE = HEAD_DIM ** (-0.5)
LOG2E = 1.4426950408889634
HEADS_LOCAL = 3
BLOCK = ROW_BLOCKS * TILE**3
STEPS = (-1, 0, 1)

XS, HALVES, STRIPS, CORES = 4, 2, 2, 2
ORDER = (0, 3, 1, 2)


def ctx_of(x, half, strip, core):
    return ((x * HALVES + half) * STRIPS + strip) * CORES + core


def run_of(x, strip):
    return x if strip == 0 else XS - 1 - x


def swap_pairs():
    return [(i, i ^ 1) for i in range(32)]


def mask_pairs(flip):
    pairs = []
    for row in range(ROW_BLOCKS):
        for col in range(16):
            pairs.append((row * 16 + col, ctx_of(run_of(col % 8 // 2, col // 8), row ^ flip, col // 8, col % 2)))
    return pairs


def chain_pairs():
    pairs = []
    for half in range(HALVES):
        for link in range(XS * STRIPS - 1):
            a = ctx_of(run_of(link % XS, link // XS), half, link // XS, 1)
            b = ctx_of(run_of((link + 1) % XS, (link + 1) // XS), half, (link + 1) // XS, 0)
            pairs += [(a, b), (b, a)]
    return pairs


def mask_bias(window_mask):
    place = lax.axis_index("ctx")
    x, strip, core = place // 8, place // 2 % 2, place % 2
    col = strip * 8 + jnp.where(strip == 0, x, XS - 1 - x) * 2 + core
    half = place // 4 % 2
    time_blocks = window_mask.shape[1]
    mine = lax.ppermute(window_mask[0], "ctx", mask_pairs(0))
    other = lax.ppermute(window_mask[0], "ctx", mask_pairs(1))
    rows = jnp.stack([jnp.where(half == 0, mine, other), jnp.where(half == 0, other, mine)])
    rows = rows.reshape(ROW_BLOCKS, time_blocks, 3, 3, 3) == 1
    time_pos = jnp.arange(time_blocks)
    has_left = col > 0
    has_right = col < 15
    per_query_row = []
    for rq in range(ROW_BLOCKS):
        per_dt = []
        for dt in range(3):
            inside_t = (time_pos + dt - 1 >= 0) & (time_pos + dt - 1 < time_blocks)
            per_block = []
            for block in range(3):
                per_key_row = []
                for rk in range(ROW_BLOCKS):
                    window = rows[rq, :, dt, rk - rq + 1]
                    left = window[:, 0] & has_left
                    right = window[:, 2] & has_right
                    if block == 0:
                        allowed = window[:, 1]
                        if dt == 1 and rk == rq:
                            allowed = jnp.ones_like(allowed)
                    elif block == 1:
                        allowed = jnp.where(core == 0, right, left)
                    else:
                        allowed = jnp.where(core == 0, left, right)
                    per_key_row.append(allowed & inside_t)
                per_block.append(jnp.stack(per_key_row, axis=1))
            per_dt.append(jnp.stack(per_block, axis=1))
        per_query_row.append(jnp.stack(per_dt, axis=1))
    allowed = jnp.stack(per_query_row, axis=-1).reshape(time_blocks, 18, ROW_BLOCKS)
    bias = jnp.where(allowed, 0.0, NEG_FILL).astype(jnp.float32)
    bias = jnp.broadcast_to(bias[:, :, None, :, None], (time_blocks, 18, TILE, ROW_BLOCKS, TILE * TILE))
    return bias.reshape(time_blocks, 18, BLOCK)


def unpack_kernel(taken, dk, dv, dq, b0, b1, b2, out_sems):
    writes = []
    for run in ORDER:
        for i, (ref, buf) in enumerate(((dk, b0), (dv, b1), (dq, b2))):
            for strip in range(STRIPS):
                for half in range(HALVES):
                    parts = []
                    for core in range(CORES):
                        lanes = [768 + j * HEAD_DIM if i == 2 else (2 * j + i) * HEAD_DIM for j in range(HEADS_LOCAL)]
                        x = run_of(run, strip)
                        cells = [taken[x, half, strip, core, :, lane : lane + HEAD_DIM] for lane in lanes]
                        cells = jnp.concatenate(cells, axis=1)
                        parts.append(cells.astype(jnp.float32).reshape(8, TILE, 384))
                    joined = jnp.concatenate(parts, axis=1).astype(jnp.bfloat16)
                    buf[run, :, strip, :, half * 384 : (half + 1) * 384] = joined
            writes.append(pltpu.make_async_copy(buf.at[run], ref.at[:, :, run], out_sems.at[run, i]))
            writes[-1].start()
    for write in writes:
        write.wait()


def unpack(arrived):
    out = jax.ShapeDtypeStruct((8, STRIPS, XS, 8, 768), jnp.bfloat16)
    buf = pltpu.VMEM((XS, 8, STRIPS, 8, 768), jnp.bfloat16)
    lanes = arrived.shape[-1]
    results = pl.pallas_call(
        unpack_kernel,
        in_specs=[VMEM],
        out_specs=[ANY] * 3,
        out_shape=[out] * 3,
        scratch_shapes=[buf, buf, buf, pltpu.SemaphoreType.DMA((XS, 3))],
        compiler_params=pltpu.CompilerParams(vmem_limit_bytes=SMALL_LIMIT),
        cost_estimate=pl.CostEstimate(flops=0, bytes_accessed=4_700_000, transcendentals=0),
        name="unpack",
    )(arrived.reshape(XS, HALVES, STRIPS, CORES, 32, lanes))
    return [r.reshape(1, 8, 64, 768) for r in results]


def block_bias(bias_ref, t, dt, block):
    rows = []
    for rk in range(ROW_BLOCKS):
        row = (dt * 3 + block) * 2 + rk
        rows.append(jnp.broadcast_to(bias_ref[t, row : row + 1, :], (TILE * TILE, BLOCK)))
    return jnp.concatenate(rows * TILE, axis=0)


ANY = pl.BlockSpec(memory_space=pl.ANY)
VMEM = pl.BlockSpec(memory_space=pltpu.VMEM)
SMALL_LIMIT = 12 * 1024 * 1024
VMEM_LIMIT = 62 * 1024 * 1024


def pack_kernel(blocks, ins, *refs):
    count = len(ins)
    inputs, out, taken, (packed, in_sems, out_sems) = refs[:count], refs[count], refs[count + 1 : -3], refs[-3:]
    reads, writes = [], []
    for x in ORDER:
        for i, (first, heads) in enumerate(ins):
            for half in range(HALVES):
                lane = (half * HEADS_LOCAL + first) * HEAD_DIM
                source = inputs[i].at[:, :, x, :, lane : lane + heads * HEAD_DIM]
                reads.append(pltpu.make_async_copy(source, taken[i].at[x, half], in_sems.at[x, i, half]))
                reads[-1].start()
    each = count * HALVES
    for n, x in enumerate(ORDER):
        if n % 2 == 0:
            for read in reads[n * each : (n + 2) * each]:
                read.wait()
        for half in range(HALVES):
            for strip in range(STRIPS):
                for core in range(CORES):
                    for n, (i, j) in enumerate(blocks):
                        lane = (j - ins[i][0]) * HEAD_DIM
                        cells = taken[i][run_of(x, strip), half, :, strip, :, lane : lane + HEAD_DIM]
                        cells = cells.astype(jnp.float32)[:, core * TILE : (core + 1) * TILE].reshape(32, HEAD_DIM)
                        to = n * HEAD_DIM
                        packed[x, half, strip, core, :, to : to + HEAD_DIM] = cells.astype(jnp.bfloat16)
            writes.append(pltpu.make_async_copy(packed.at[x, half], out.at[x, half], out_sems.at[x, half]))
            writes[-1].start()
    for write in writes:
        write.wait()


def pack(tensors, ins, blocks, name):
    views = [t.reshape(8, STRIPS, XS, 8, 768) for t in tensors]
    out = (XS, HALVES, STRIPS, CORES, 32, len(blocks) * HEAD_DIM)
    taken = [pltpu.VMEM((XS, HALVES, 8, STRIPS, 8, heads * HEAD_DIM), jnp.bfloat16) for _, heads in ins]
    return pl.pallas_call(
        lambda *refs: pack_kernel(blocks, ins, *refs),
        in_specs=[ANY] * len(views),
        out_specs=ANY,
        out_shape=jax.ShapeDtypeStruct(out, jnp.bfloat16),
        scratch_shapes=taken
        + [
            pltpu.VMEM(out, jnp.bfloat16),
            pltpu.SemaphoreType.DMA((XS, len(ins), HALVES)),
            pltpu.SemaphoreType.DMA((XS, HALVES)),
        ],
        compiler_params=pltpu.CompilerParams(vmem_limit_bytes=VMEM_LIMIT),
        cost_estimate=pl.CostEstimate(flops=0, bytes_accessed=4_000_000, transcendentals=0),
        name=name,
    )(*views).reshape(32, 32, len(blocks) * HEAD_DIM)


def grads_kernel(lanes, onward, *refs):
    qg_lane, own_lane, near_lane, head, far_lane = lanes
    bias_ref, qg, own, near, far = refs[:5]
    grads, to_near, to_far = refs[-3 - len(onward) :][:3]
    if onward:
        refs[-1][...] = own[:, onward[0]]
    time_blocks = bias_ref.shape[0]
    wide = 2 * HEAD_DIM
    sources = ((own, own_lane), (near, near_lane), (far, 0))
    mine, dq_lane = head * wide, 3 * wide + head * HEAD_DIM
    targets = ((grads, mine), (to_near, mine), (to_far, far_lane))
    both, raw, pairs, slopes = {}, {}, {}, {}
    over_channels = (((1,), (1,)), ((), ()))

    def rows(t):
        return pl.ds(t * BLOCK, BLOCK)

    def window(t):
        low, high = max(t - 1, 0), min(t + 1, time_blocks - 1)
        return low, high, pl.ds(low * BLOCK, (high - low + 1) * BLOCK)

    def products(t):
        q = qg[rows(t), qg_lane : qg_lane + HEAD_DIM]
        g = qg[rows(t), qg_lane + HEAD_DIM : qg_lane + wide]
        zero = jnp.zeros_like(q)
        both[t] = jnp.concatenate(
            [jnp.concatenate([q, zero], axis=1), jnp.concatenate([zero, g], axis=1)], axis=0
        )
        low, high, span = window(t)
        scores, probs = [], []
        top = None
        for block, (source, lane) in enumerate(sources):
            k = source[span, lane : lane + HEAD_DIM]
            v = source[span, lane + HEAD_DIM : lane + wide]
            s = lax.dot_general(k, q, over_channels, preferred_element_type=jnp.float32)
            probs.append(lax.dot_general(v, g, over_channels, preferred_element_type=jnp.float32))
            bias = [block_bias(bias_ref, t, near_t - t + 1, block) for near_t in range(low, high + 1)]
            s = s * (SCALE * LOG2E) + jnp.concatenate(bias, axis=0)
            block_top = jnp.max(s, axis=0, keepdims=True)
            top = block_top if top is None else jnp.maximum(top, block_top)
            scores.append(s)
        raw[t] = (scores, probs, top)

    def softmax(t):
        scores, probs, top = raw.pop(t)
        low, high, _ = window(t)
        total = jnp.zeros((1, BLOCK), jnp.float32)
        dots = jnp.zeros((1, BLOCK), jnp.float32)
        exps = []
        for s, pg in zip(scores, probs):
            e = jnp.exp2(s - top)
            total += jnp.sum(e, axis=0, keepdims=True)
            dots += jnp.sum(e * pg, axis=0, keepdims=True)
            exps.append(e)
        return low, high, exps, probs, 1.0 / total, dots

    def slope(t, low, high, exps, probs, inv, dots):
        row_dot = dots * inv
        slopes[t], pairs[t] = [], []
        for e, pg in zip(exps, probs):
            p = e * inv
            ds = (p * (pg - row_dot)).astype(jnp.bfloat16)
            pair = jnp.concatenate([ds, p.astype(jnp.bfloat16)], axis=1)
            pairs[t].append([pair[i * BLOCK : (i + 1) * BLOCK] for i in range(high - low + 1)])
            slopes[t].append(ds)

    def to_query(t):
        _, _, span = window(t)
        keys = jnp.concatenate([source[span, lane : lane + HEAD_DIM] for source, lane in sources], axis=0)
        ds = jnp.concatenate(slopes.pop(t), axis=0)
        dq = lax.dot_general(ds, keys, (((0,), (0,)), ((), ())), preferred_element_type=jnp.float32)
        grads[rows(t), dq_lane : dq_lane + HEAD_DIM] = (dq * SCALE).astype(jnp.bfloat16)

    def to_keys(t):
        near_ts = [n for n in (t - 1, t, t + 1) if 0 <= n < time_blocks]
        w = jnp.concatenate([both[n] for n in near_ts], axis=0)
        x = [
            jnp.concatenate([pairs[n][block][t - max(n - 1, 0)] for n in near_ts], axis=1)
            for block in range(3)
        ]
        r = jnp.dot(jnp.concatenate(x, axis=0), w, preferred_element_type=jnp.float32)
        for block, (target, lane) in enumerate(targets):
            part = r[block * BLOCK : (block + 1) * BLOCK]
            part = jnp.concatenate([part[:, :HEAD_DIM] * SCALE, part[:, HEAD_DIM:]], axis=1)
            target[rows(t), lane : lane + wide] = part.astype(jnp.bfloat16)

    products(0)
    for t in range(time_blocks):
        if t + 1 < time_blocks:
            products(t + 1)
        if t > 1:
            to_keys(t - 2)
        state = softmax(t)
        if t > 0:
            to_query(t - 1)
        slope(t, *state)
    to_query(time_blocks - 1)
    to_keys(time_blocks - 2)
    to_keys(time_blocks - 1)


def head_grads(bias, everything, near, far, shared, head, far_lane, far_lanes, onward=()):
    rows = everything.shape[0]
    wide = 2 * HEAD_DIM
    lanes = ((HEADS_LOCAL + head) * wide, head * wide, head * wide, head, far_lane)
    return pl.pallas_call(
        lambda *refs: grads_kernel(lanes, onward, *refs),
        in_specs=[VMEM] * (5 + len(shared)),
        out_specs=[VMEM] * (3 + len(onward)),
        out_shape=[
            jax.ShapeDtypeStruct((rows, lanes_out), jnp.bfloat16)
            for lanes_out in (9 * HEAD_DIM, 6 * HEAD_DIM, far_lanes) + (wide,) * len(onward)
        ],
        input_output_aliases={5 + i: i for i in range(len(shared))},
        compiler_params=pltpu.CompilerParams(vmem_limit_bytes=SMALL_LIMIT),
        cost_estimate=pl.CostEstimate(flops=100_000_000_000, bytes_accessed=4_500_000, transcendentals=1_200_000),
        name="head_grads",
    )(bias, everything, everything, near, far, *shared)


def add_halo(grads, halo, first, flops):
    lanes = slice(first * 2 * HEAD_DIM, first * 2 * HEAD_DIM + halo.shape[1])

    def kernel(grads, halo, out):
        total = grads[:, lanes].astype(jnp.float32) + halo[...].astype(jnp.float32)
        out[:, lanes] = total.astype(jnp.bfloat16)

    return pl.pallas_call(
        kernel,
        in_specs=[VMEM] * 2,
        out_specs=VMEM,
        out_shape=jax.ShapeDtypeStruct(grads.shape, grads.dtype),
        input_output_aliases={0: 0},
        compiler_params=pltpu.CompilerParams(vmem_limit_bytes=SMALL_LIMIT),
        cost_estimate=pl.CostEstimate(flops=flops, bytes_accessed=1000, transcendentals=0),
        name="add_halo",
    )(grads, halo)


def split_kernel(arrived, bias, near, *fars):
    wide = 2 * HEAD_DIM
    for j, far in enumerate(fars):
        far[...] = arrived[:, j * wide : (j + 1) * wide]
    near[...] = arrived[:, : HEADS_LOCAL * wide]


def split(arrived, bias):
    rows, wide = arrived.shape[0], 2 * HEAD_DIM
    far = jax.ShapeDtypeStruct((rows, wide), arrived.dtype)
    near = jax.ShapeDtypeStruct((rows, HEADS_LOCAL * wide), arrived.dtype)
    near, *fars = pl.pallas_call(
        split_kernel,
        in_specs=[VMEM, ANY],
        out_specs=[VMEM] * HEADS_LOCAL,
        out_shape=[near] + [far] * (HEADS_LOCAL - 1),
        compiler_params=pltpu.CompilerParams(vmem_limit_bytes=SMALL_LIMIT),
        cost_estimate=pl.CostEstimate(flops=0, bytes_accessed=1000, transcendentals=0),
        name="split",
    )(arrived, bias)
    return near, fars


def shards(queries, keys, values, out_grad, window_mask):
    swap, chain = swap_pairs(), chain_pairs()
    wide = 2 * HEAD_DIM
    everything = tuple((i, j) for j in range(HEADS_LOCAL) for i in (0, 1))
    everything += tuple((i, j) for j in range(HEADS_LOCAL) for i in (2, 3))
    packed = pack((keys, values, queries, out_grad), ((0, 3),) * 4, everything, "pack")
    packed, window_mask = lax.optimization_barrier((packed, window_mask))
    arrived = lax.all_to_all(packed, "ctx", 0, 0, tiled=True).reshape(1024, 12 * HEAD_DIM)
    bias = mask_bias(window_mask)
    for_near, for_far = split(arrived, bias)
    fars = [lax.ppermute(part, "ctx", chain) for part in for_far]
    near = lax.ppermute(for_near, "ctx", swap)
    last = slice(2 * wide, 3 * wide)
    *shared, for_last = head_grads(bias, arrived, near, fars[0], (), 0, 0, 2 * wide, (last,))
    far = lax.ppermute(for_last, "ctx", chain)
    grads, to_near, to_far = head_grads(bias, arrived, near, fars[1], shared, 1, wide, 2 * wide)
    back = lax.ppermute(to_far, "ctx", chain)
    grads, to_near, to_far = head_grads(bias, arrived, near, far, (grads, to_near), 2, 0, wide)
    near_back = lax.ppermute(to_near, "ctx", swap)
    last_back = lax.ppermute(to_far, "ctx", chain)
    grads = add_halo(grads, back, 0, 100_000_000_000)
    grads = add_halo(grads, near_back, 0, 1000)
    grads = add_halo(grads, last_back, 2, 1000)
    grads = lax.all_to_all(grads.reshape(32, 32, 9 * HEAD_DIM), "ctx", 0, 0, tiled=True)
    dk, dv, dq = unpack(grads)
    return dq, dk, dv


def solution(mesh):
    tokens = P("ctx", None, None, "head")
    return jax.shard_map(
        shards,
        mesh=mesh,
        in_specs=(tokens, tokens, tokens, tokens, P("ctx", None, None)),
        out_specs=(tokens, tokens, tokens),
        check_vma=False,
    )
```

time: 154 us -> 142 us (0.922)
  Pallas kernels: 26.1 us -> 19.9 us
  blocking collectives: 42.4 us -> 38.1 us
    pallas_call x8, Pallas kernels: 22.8 us -> 16.3 us  [the longest x3 12.1 us: head_grads(): pl.pallas_call(lambda *refs: grads_kernel(lanes, onward, *refs), in_specs...]
    all_to_all x1, blocking collectives: 42.4 us -> 38.1 us  [shards(): lax.all_to_all(grads.reshape(32, 32, 9 * HEAD_DIM), 'ctx', 0, 0, tiled=True)]
    ppermute x3 -> x2, starting transfers between devices: 7.47 us -> 5.55 us  [shards(): fars = [lax.ppermute(part, 'ctx', chain) for part in for_far]]
    ppermute x3, starting transfers between devices: 6.04 us -> 7.66 us  [the longest x1 3.64 us: shards(): back = lax.ppermute(to_far, 'ctx', chain)]
    ppermute x3 -> x2, waiting for transfers between devices: 6 us -> 4.92 us  [shards(): fars = [lax.ppermute(part, 'ctx', chain) for part in for_far]]
  transfers between devices with their start and end apart: 11 -> 10, of which waited for: 6 -> 5; matrix products, arithmetic and copies ran while one was open for 3% -> 3% of each run, Pallas kernels for 13% -> 10%
where the time goes in v4:
time: 142 us; the launch traced here: 141 us
  waiting for transfers between devices  50.3 us (35%)
  blocking collectives  38.1 us (27%)
  starting transfers between devices  27.9 us (20%)
  Pallas kernels  19.9 us (14%)
  local copies, waits for them, and re-layouts  3.49 us (2%)
    all_to_all x1, blocking collectives, shards(): lax.all_to_all(grads.reshape(32, 32, 9 * HEAD_DIM), 'ctx', 0, 0, tiled=True)  38.1 us
    all_to_all x1, waiting for transfers between devices, shards(): lax.all_to_all(packed, 'ctx', 0, 0, tiled=True).reshape(1024, 12 * HEAD_DIM)  35.5 us
    pallas_call x3, Pallas kernels, head_grads(): pl.pallas_call(lambda *refs: grads_kernel(lanes, onward, *refs), in_specs...  12.1 us
    all_to_all x1, starting transfers between devices, shards(): lax.all_to_all(packed, 'ctx', 0, 0, tiled=True).reshape(1024, 12 * HEAD_DIM)  9.64 us
    ppermute x1, waiting for transfers between devices, shards(): back = lax.ppermute(to_far, 'ctx', chain)  5.72 us
    ppermute x2, starting transfers between devices, shards(): fars = [lax.ppermute(part, 'ctx', chain) for part in for_far]  5.55 us
    ppermute x2, waiting for transfers between devices, shards(): fars = [lax.ppermute(part, 'ctx', chain) for part in for_far]  4.92 us
    ppermute x1, starting transfers between devices, mask_bias(): other = lax.ppermute(window_mask[0], 'ctx', mask_pairs(1))  3.81 us
  transfers between devices with their start and end apart: 10, of which 5 were waited for; matrix products, arithmetic and copies ran while one was open for 3% of the time, Pallas kernels for 10%

profile of v4, /device:TPU:1, one launch (start us, length us, event | category | flops | bytes accessed | tf_op | source)
XLA Modules:
  0.0 141.5 jit_solution(14763772820936303638)
XLA Ops:
  0.6 0.0 copy-start
  0.6 3.6 %pack.1 = bf16[4,2,2,2,32,1536]{5,4,3,2,1,0:T(8,128)(2,1)} custom-call(bf16[8,2,4,8,768]{4,3,2,1,0:T(8,128)(2,1)} %bitcast.110, bf16[8,2,4,8,768]{4,3,2,1,0:T(8,128)(2,1)} %bitcast.111, bf16[8,2,4,8,768]{4,3,2,1,0:T(8,128)(2,1)} %bitcast.112, bf16[8,2,4,8,768]{4,3,2,1,0:T(8,128)(2,1)} %bitcast.113), custom_call_target="tpu_custom_call" | custom-call | bytes 4000000 | tf_op jit(solution)/shard_map/pack/pallas_call | solution.py:182
  4.2 0.0 copy-done
  4.2 3.8 %collective-permute-start.1 = (s32[8,27]{1,0:T(8,128)S(1)}, s32[8,27]{1,0:T(8,128)S(1)}, u32[]{:S(2)}, u32[]{:S(2)}) collective-permute-start(s32[8,27]{1,0:T(8,128)S(1)} %bitcast.123), channel_id=1, source_target_pairs={{0,16},{4,20},{8,48},{12,52},{16,80},{20,84},{24,112},{28,116},{32... | collective-permute-start | bytes 2600 | tf_op jit(solution)/shard_map/ppermute | solution.py:59
  8.1 0.6 collective-permute-start
  8.7 9.6 %all-to-all-start = ((bf16[32,32,1536]{2,1,0:T(8,128)(2,1)}), bf16[32,32,1536]{2,1,0:T(8,128)(2,1)S(1)}, u32[]{:S(2)}, u32[]{:S(2)}) async-start(bf16[32,32,1536]{2,1,0:T(8,128)(2,1)} %bitcast.109), calls=%async_computation | async-start | bytes 6291456 | tf_op jit(solution)/shard_map/all_to_all | solution.py:368
  18.5 0.0 collective-permute-done.1
  18.5 0.0 collective-permute-done
  18.5 0.1 copy.39
  18.6 0.1 copy.40
  19.4 0.1 copy.49
  19.6 0.1 copy.50
  19.7 0.1 copy.51
  19.8 1.0 broadcast_in_dim.16
  20.8 1.8 %reshape.148 = f32[8,18,128]{2,0,1:T(8,128)S(1)} reshape(f32[8,18,4,2,16]{4,3,2,0,1:T(2,128)} %broadcast_in_dim.16) | data formatting | bytes 147456 | tf_op jit(solution)/shard_map/reshape | solution.py:92
  22.7 35.5 %all-to-all-done = bf16[32,32,1536]{2,1,0:T(8,128)(2,1)S(1)} async-done(((bf16[32,32,1536]{2,1,0:T(8,128)(2,1)}), bf16[32,32,1536]{2,1,0:T(8,128)(2,1)S(1)}, u32[]{:S(2)}, u32[]{:S(2)}) %all-to-all-start) | async-done | bytes 3145760 | tf_op jit(solution)/shard_map/all_to_all | solution.py:368
  58.1 0.2 split.1
  58.3 0.5 collective-permute-start.2
  58.8 1.9 %collective-permute-start.3 = (bf16[1024,256]{1,0:T(8,128)(2,1)S(1)}, bf16[1024,256]{1,0:T(8,128)(2,1)S(1)}, u32[]{:S(2)}, u32[]{:S(2)}) collective-permute-start(bf16[1024,256]{1,0:T(8,128)(2,1)S(1)} %get-tuple-element.24), channel_id=1, source_target_pairs={{4,32},{32,4},{36,64},{64,36},{68,96},{96,68},{100,104},{104,100},... | collective-permute-start | bytes 1572872 | tf_op jit(solution)/shard_map/ppermute | solution.py:371
  60.7 3.6 %collective-permute-start.5 = (bf16[1024,256]{1,0:T(8,128)(2,1)S(1)}, bf16[1024,256]{1,0:T(8,128)(2,1)S(1)}, u32[]{:S(2)}, u32[]{:S(2)}) collective-permute-start(bf16[1024,256]{1,0:T(8,128)(2,1)S(1)} %get-tuple-element.26), channel_id=1, source_target_pairs={{4,32},{32,4},{36,64},{64,36},{68,96},{96,68},{100,104},{104,100},... | collective-permute-start | bytes 1572872 | tf_op jit(solution)/shard_map/ppermute | solution.py:371
  64.4 4.9 %collective-permute-done.3.refs_4_ = bf16[1024,256]{1,0:T(8,128)(2,1)S(1)} collective-permute-done((bf16[1024,256]{1,0:T(8,128)(2,1)S(1)}, bf16[1024,256]{1,0:T(8,128)(2,1)S(1)}, u32[]{:S(2)}, u32[]{:S(2)}) %collective-permute-start.3) | collective-permute-done | bytes 524320 | tf_op jit(solution)/shard_map/ppermute | solution.py:371
  69.3 0.0 collective-permute-done.2.refs_3_
  69.3 4.0 %head_grads.3 = (bf16[1024,1152]{1,0:T(8,128)(2,1)S(1)}, bf16[1024,768]{1,0:T(8,128)(2,1)S(1)}, bf16[1024,512]{1,0:T(8,128)(2,1)S(1)}, bf16[1024,256]{1,0:T(8,128)(2,1)S(1)}) custom-call(f32[8,18,128]{2,1,0:T(8,128)S(1)} %copy.55.bias.refs_0_, bf16[1024,1536]{1,0:T(8,128)(2,1)S(1)} %bitcast.102, bf16[1024,1536]{1,0:T(8,128)(2,1)S(1)} %bitcast.103, ...), custom_call_target="tpu_custom_call" | custom-call | flops 99999997952 | bytes 4500000 | tf_op jit(solution)/shard_map/head_grads/pallas_call | solution.py:304
  73.3 2.1 %collective-permute-start.4 = (bf16[1024,256]{1,0:T(8,128)(2,1)S(1)}, bf16[1024,256]{1,0:T(8,128)(2,1)S(1)}, u32[]{:S(2)}, u32[]{:S(2)}) collective-permute-start(bf16[1024,256]{1,0:T(8,128)(2,1)S(1)} %get-tuple-element.25), channel_id=1, source_target_pairs={{4,32},{32,4},{36,64},{64,36},{68,96},{96,68},{100,104},{104,100},... | collective-permute-start | bytes 1572872 | tf_op jit(solution)/shard_map/ppermute | solution.py:375
  75.4 0.0 collective-permute-done.5.refs_4_
  75.5 4.0 %head_grads.4 = (bf16[1024,1152]{1,0:T(8,128)(2,1)S(1)}, bf16[1024,768]{1,0:T(8,128)(2,1)S(1)}, bf16[1024,512]{1,0:T(8,128)(2,1)S(1)}) custom-call(f32[8,18,128]{2,1,0:T(8,128)S(1)} %copy.55.bias.refs_0_, bf16[1024,1536]{1,0:T(8,128)(2,1)S(1)} %bitcast.104, ...), custom_call_target="tpu_custom_call", output_to_operand_aliasing={{0}: (5, {}), {1}: (6, {}), {2}: (7, {})} | custom-call | flops 99999997952 | bytes 4500000 | tf_op jit(solution)/shard_map/head_grads/pallas_call | solution.py:304
  79.5 3.6 %collective-permute-start.6 = (bf16[1024,512]{1,0:T(8,128)(2,1)S(1)}, bf16[1024,512]{1,0:T(8,128)(2,1)S(1)}, u32[]{:S(2)}, u32[]{:S(2)}) collective-permute-start(bf16[1024,512]{1,0:T(8,128)(2,1)S(1)} %get-tuple-element.33), channel_id=1, source_target_pairs={{4,32},{32,4},{36,64},{64,36},{68,96},{96,68},{100,104},{104,100},... | collective-permute-start | bytes 3145736 | tf_op jit(solution)/shard_map/ppermute | solution.py:377
  83.1 0.7 collective-permute-done.4.refs_4_
  83.8 4.0 %head_grads.5 = (bf16[1024,1152]{1,0:T(8,128)(2,1)S(1)}, bf16[1024,768]{1,0:T(8,128)(2,1)S(1)}, bf16[1024,256]{1,0:T(8,128)(2,1)S(1)}) custom-call(f32[8,18,128]{2,1,0:T(8,128)S(1)} %copy.55.bias.refs_0_, bf16[1024,1536]{1,0:T(8,128)(2,1)S(1)} %bitcast.106, bf16[1024,1536]{1,0:T(8,128)(2,1)S(1)} %bitcast.107, ...), custom_call_target="tpu_custom_call", output_to_operand_aliasing={{0}: (5, {}), {1}: (6, {})} | custom-call | flops 99999997952 | bytes 4500000 | tf_op jit(solution)/shard_map/head_grads/pallas_call | solution.py:304
  87.9 1.9 %collective-permute-start.8 = (bf16[1024,256]{1,0:T(8,128)(2,1)S(1)}, bf16[1024,256]{1,0:T(8,128)(2,1)S(1)}, u32[]{:S(2)}, u32[]{:S(2)}) collective-permute-start(bf16[1024,256]{1,0:T(8,128)(2,1)S(1)} %get-tuple-element.35), channel_id=1, source_target_pairs={{4,32},{32,4},{36,64},{64,36},{68,96},{96,68},{100,104},{104,100},... | collective-permute-start | bytes 1572872 | tf_op jit(solution)/shard_map/ppermute | solution.py:380
  89.8 0.1 collective-permute-start.7
  89.9 5.7 %collective-permute-done.6.halo = bf16[1024,512]{1,0:T(8,128)(2,1)S(1)} collective-permute-done((bf16[1024,512]{1,0:T(8,128)(2,1)S(1)}, bf16[1024,512]{1,0:T(8,128)(2,1)S(1)}, u32[]{:S(2)}, u32[]{:S(2)}) %collective-permute-start.6) | collective-permute-done | bytes 1048608 | tf_op jit(solution)/shard_map/ppermute | solution.py:377
  95.6 0.8 add_halo.3.grads
  96.4 0.0 collective-permute-done.7.halo
  96.5 1.3 add_halo.4.grads
  97.7 3.5 %collective-permute-done.8.halo = bf16[1024,256]{1,0:T(8,128)(2,1)S(1)} collective-permute-done((bf16[1024,256]{1,0:T(8,128)(2,1)S(1)}, bf16[1024,256]{1,0:T(8,128)(2,1)S(1)}, u32[]{:S(2)}, u32[]{:S(2)}) %collective-permute-start.8) | collective-permute-done | bytes 524320 | tf_op jit(solution)/shard_map/ppermute | solution.py:380
  101.2 0.4 add_halo.5
  101.6 38.1 %all_to_all.10 = bf16[32,32,1152]{2,1,0:T(8,128)(2,1)S(1)} all-to-all(bf16[32,32,1152]{2,1,0:T(8,128)(2,1)S(1)} %bitcast.100), channel_id=1, replica_groups=mesh['ctx'=32,'head'=4] {'ctx'}, dimensions={0} | all-to-all | bytes 4718592 | tf_op jit(solution)/shard_map/all_to_all | solution.py:384
  139.8 1.5 %unpack.1 = (bf16[8,2,4,8,768]{4,3,2,1,0:T(8,128)(2,1)}, bf16[8,2,4,8,768]{4,3,2,1,0:T(8,128)(2,1)}, bf16[8,2,4,8,768]{4,3,2,1,0:T(8,128)(2,1)}) custom-call(bf16[4,2,2,2,32,1152]{5,4,3,2,1,0:T(8,128)(2,1)S(1)} %bitcast.108), custom_call_target="tpu_custom_call" | custom-call | bytes 4700000 | tf_op jit(solution)/shard_map/unpack/pallas_call | solution.py:120
  (49 shorter events, 0.5 us)
Async XLA Ops:
  0.6 3.6 %copy-start = (s32[1,8,27]{2,1,0:T(8,128)S(1)}, s32[1,8,27]{2,1,0:T(8,128)}, u32[]{:S(2)}) copy-start(s32[1,8,27]{2,1,0:T(8,128)} %param.9) | copy-start | bytes 2596
  4.2 14.2 %collective-permute-start.1 = (s32[8,27]{1,0:T(8,128)S(1)}, s32[8,27]{1,0:T(8,128)S(1)}, u32[]{:S(2)}, u32[]{:S(2)}) collective-permute-start(s32[8,27]{1,0:T(8,128)S(1)} %bitcast.123), channel_id=1, source_target_pairs={{0,16},{4,20},{8,48},{12,52},{16,80},{20,84},{24,112},{28,116},{32... | collective-permute-start | bytes 2600 | tf_op jit(solution)/shard_map/ppermute | solution.py:59
  8.1 10.4 %collective-permute-start = (s32[8,27]{1,0:T(8,128)S(1)}, s32[8,27]{1,0:T(8,128)S(1)}, u32[]{:S(2)}, u32[]{:S(2)}) collective-permute-start(s32[8,27]{1,0:T(8,128)S(1)} %bitcast.124), channel_id=1, source_target_pairs={{0,0},{4,4},{8,32},{12,36},{16,64},{20,68},{24,96},{28,100},{32,10... | collective-permute-start | bytes 2600 | tf_op jit(solution)/shard_map/ppermute | solution.py:58
  8.7 49.4 %all-to-all-start = ((bf16[32,32,1536]{2,1,0:T(8,128)(2,1)}), bf16[32,32,1536]{2,1,0:T(8,128)(2,1)S(1)}, u32[]{:S(2)}, u32[]{:S(2)}) async-start(bf16[32,32,1536]{2,1,0:T(8,128)(2,1)} %bitcast.109), calls=%async_computation | async-start | bytes 6291456 | tf_op jit(solution)/shard_map/all_to_all | solution.py:368
  58.3 11.0 %collective-permute-start.2 = (bf16[1024,768]{1,0:T(8,128)(2,1)S(1)}, bf16[1024,768]{1,0:T(8,128)(2,1)S(1)}, u32[]{:S(2)}, u32[]{:S(2)}) collective-permute-start(bf16[1024,768]{1,0:T(8,128)(2,1)S(1)} %get-tuple-element.23), channel_id=1, source_target_pairs={{0,4},{4,0},{8,12},{12,8},{16,20},{20,16},{24,28},{28,24},{32,36},... | collective-permute-start | bytes 4718600 | tf_op jit(solution)/shard_map/ppermute | solution.py:372
  58.8 10.5 %collective-permute-start.3 = (bf16[1024,256]{1,0:T(8,128)(2,1)S(1)}, bf16[1024,256]{1,0:T(8,128)(2,1)S(1)}, u32[]{:S(2)}, u32[]{:S(2)}) collective-permute-start(bf16[1024,256]{1,0:T(8,128)(2,1)S(1)} %get-tuple-element.24), channel_id=1, source_target_pairs={{4,32},{32,4},{36,64},{64,36},{68,96},{96,68},{100,104},{104,100},... | collective-permute-start | bytes 1572872 | tf_op jit(solution)/shard_map/ppermute | solution.py:371
  60.7 14.7 %collective-permute-start.5 = (bf16[1024,256]{1,0:T(8,128)(2,1)S(1)}, bf16[1024,256]{1,0:T(8,128)(2,1)S(1)}, u32[]{:S(2)}, u32[]{:S(2)}) collective-permute-start(bf16[1024,256]{1,0:T(8,128)(2,1)S(1)} %get-tuple-element.26), channel_id=1, source_target_pairs={{4,32},{32,4},{36,64},{64,36},{68,96},{96,68},{100,104},{104,100},... | collective-permute-start | bytes 1572872 | tf_op jit(solution)/shard_map/ppermute | solution.py:371
  73.3 10.5 %collective-permute-start.4 = (bf16[1024,256]{1,0:T(8,128)(2,1)S(1)}, bf16[1024,256]{1,0:T(8,128)(2,1)S(1)}, u32[]{:S(2)}, u32[]{:S(2)}) collective-permute-start(bf16[1024,256]{1,0:T(8,128)(2,1)S(1)} %get-tuple-element.25), channel_id=1, source_target_pairs={{4,32},{32,4},{36,64},{64,36},{68,96},{96,68},{100,104},{104,100},... | collective-permute-start | bytes 1572872 | tf_op jit(solution)/shard_map/ppermute | solution.py:375
  79.5 16.1 %collective-permute-start.6 = (bf16[1024,512]{1,0:T(8,128)(2,1)S(1)}, bf16[1024,512]{1,0:T(8,128)(2,1)S(1)}, u32[]{:S(2)}, u32[]{:S(2)}) collective-permute-start(bf16[1024,512]{1,0:T(8,128)(2,1)S(1)} %get-tuple-element.33), channel_id=1, source_target_pairs={{4,32},{32,4},{36,64},{64,36},{68,96},{96,68},{100,104},{104,100},... | collective-permute-start | bytes 3145736 | tf_op jit(solution)/shard_map/ppermute | solution.py:377
  87.9 13.4 %collective-permute-start.8 = (bf16[1024,256]{1,0:T(8,128)(2,1)S(1)}, bf16[1024,256]{1,0:T(8,128)(2,1)S(1)}, u32[]{:S(2)}, u32[]{:S(2)}) collective-permute-start(bf16[1024,256]{1,0:T(8,128)(2,1)S(1)} %get-tuple-element.35), channel_id=1, source_target_pairs={{4,32},{32,4},{36,64},{64,36},{68,96},{96,68},{100,104},{104,100},... | collective-permute-start | bytes 1572872 | tf_op jit(solution)/shard_map/ppermute | solution.py:380
  89.8 6.6 %collective-permute-start.7 = (bf16[1024,768]{1,0:T(8,128)(2,1)S(1)}, bf16[1024,768]{1,0:T(8,128)(2,1)S(1)}, u32[]{:S(2)}, u32[]{:S(2)}) collective-permute-start(bf16[1024,768]{1,0:T(8,128)(2,1)S(1)} %get-tuple-element.34), channel_id=1, source_target_pairs={{0,4},{4,0},{8,12},{12,8},{16,20},{20,16},{24,28},{28,24},{32,36},... | collective-permute-start | bytes 4718600 | tf_op jit(solution)/shard_map/ppermute | solution.py:379

commit v5 on v4

--- a/solution.py
+++ b/solution.py
@@ -196,12 +196,10 @@
     )(*views).reshape(32, 32, len(blocks) * HEAD_DIM)
 
 
-def grads_kernel(lanes, onward, *refs):
+def grads_kernel(lanes, *refs):
     qg_lane, own_lane, near_lane, head, far_lane = lanes
     bias_ref, qg, own, near, far = refs[:5]
-    grads, to_near, to_far = refs[-3 - len(onward) :][:3]
-    if onward:
-        refs[-1][...] = own[:, onward[0]]
+    grads, to_near, to_far = refs[-3:]
     time_blocks = bias_ref.shape[0]
     wide = 2 * HEAD_DIM
     sources = ((own, own_lane), (near, near_lane), (far, 0))
@@ -297,21 +295,21 @@
     to_keys(time_blocks - 1)
 
 
-def head_grads(bias, everything, near, far, shared, head, far_lane, far_lanes, onward=()):
+def head_grads(bias, everything, near, far, shared, head, far_lane, far_lanes, flops):
     rows = everything.shape[0]
     wide = 2 * HEAD_DIM
     lanes = ((HEADS_LOCAL + head) * wide, head * wide, head * wide, head, far_lane)
     return pl.pallas_call(
-        lambda *refs: grads_kernel(lanes, onward, *refs),
+        lambda *refs: grads_kernel(lanes, *refs),
         in_specs=[VMEM] * (5 + len(shared)),
-        out_specs=[VMEM] * (3 + len(onward)),
+        out_specs=[VMEM] * 3,
         out_shape=[
             jax.ShapeDtypeStruct((rows, lanes_out), jnp.bfloat16)
-            for lanes_out in (9 * HEAD_DIM, 6 * HEAD_DIM, far_lanes) + (wide,) * len(onward)
+            for lanes_out in (9 * HEAD_DIM, 6 * HEAD_DIM, far_lanes)
         ],
         input_output_aliases={5 + i: i for i in range(len(shared))},
         compiler_params=pltpu.CompilerParams(vmem_limit_bytes=SMALL_LIMIT),
-        cost_estimate=pl.CostEstimate(flops=100_000_000_000, bytes_accessed=4_500_000, transcendentals=1_200_000),
+        cost_estimate=pl.CostEstimate(flops=flops, bytes_accessed=4_500_000, transcendentals=1_200_000),
         name="head_grads",
     )(bias, everything, everything, near, far, *shared)
 
@@ -358,6 +356,23 @@
     return near, fars
 
 
+def take_last(arrived, after):
+    rows, wide = arrived.shape[0], 2 * HEAD_DIM
+
+    def kernel(arrived, _, out):
+        out[...] = arrived[:, (HEADS_LOCAL - 1) * wide : HEADS_LOCAL * wide]
+
+    return pl.pallas_call(
+        kernel,
+        in_specs=[VMEM, ANY],
+        out_specs=VMEM,
+        out_shape=jax.ShapeDtypeStruct((rows, wide), arrived.dtype),
+        compiler_params=pltpu.CompilerParams(vmem_limit_bytes=SMALL_LIMIT),
+        cost_estimate=pl.CostEstimate(flops=0, bytes_accessed=1000, transcendentals=0),
+        name="take_last",
+    )(arrived, after)
+
+
 def shards(queries, keys, values, out_grad, window_mask):
     swap, chain = swap_pairs(), chain_pairs()
     wide = 2 * HEAD_DIM
@@ -370,12 +385,11 @@
     for_near, for_far = split(arrived, bias)
     fars = [lax.ppermute(part, "ctx", chain) for part in for_far]
     near = lax.ppermute(for_near, "ctx", swap)
-    last = slice(2 * wide, 3 * wide)
-    *shared, for_last = head_grads(bias, arrived, near, fars[0], (), 0, 0, 2 * wide, (last,))
-    far = lax.ppermute(for_last, "ctx", chain)
-    grads, to_near, to_far = head_grads(bias, arrived, near, fars[1], shared, 1, wide, 2 * wide)
+    fars.append(lax.ppermute(take_last(arrived, near), "ctx", chain))
+    shared = head_grads(bias, arrived, near, fars[0], (), 0, 0, 2 * wide, 1_000_000_000)
+    grads, to_near, to_far = head_grads(bias, arrived, near, fars[1], shared, 1, wide, 2 * wide, 1_000_000_000)
     back = lax.ppermute(to_far, "ctx", chain)
-    grads, to_near, to_far = head_grads(bias, arrived, near, far, (grads, to_near), 2, 0, wide)
+    grads, to_near, to_far = head_grads(bias, arrived, near, fars[2], (grads, to_near), 2, 0, wide, 100_000_000_000)
     near_back = lax.ppermute(to_near, "ctx", swap)
     last_back = lax.ppermute(to_far, "ctx", chain)
     grads = add_halo(grads, back, 0, 100_000_000_000)

time: 142 us -> 140 us (0.986)
  blocking collectives: 38.1 us -> 36.4 us
    ppermute x1, starting transfers between devices: 3.81 us -> 7.58 us  [mask_bias(): other = lax.ppermute(window_mask[0], 'ctx', mask_pairs(1))]
    all_to_all x1, starting transfers between devices: 9.64 us -> 6.02 us  [shards(): lax.all_to_all(packed, 'ctx', 0, 0, tiled=True).reshape(1024, 12 * HEAD_DIM)]
    ppermute x1, starting transfers between devices: 3.64 us -> 1.93 us  [shards(): back = lax.ppermute(to_far, 'ctx', chain)]
    ppermute x1, starting transfers between devices: 1.92 us -> 3.63 us  [shards(): last_back = lax.ppermute(to_far, 'ctx', chain)]
    all_to_all x1, blocking collectives: 38.1 us -> 36.4 us  [shards(): lax.all_to_all(grads.reshape(32, 32, 9 * HEAD_DIM), 'ctx', 0, 0, tiled=True)]
    pallas_call x3 -> x4, Pallas kernels: 12.1 us -> 12.2 us  [the longest x3 12.1 us: head_grads(): pl.pallas_call(lambda *refs: grads_kernel(lanes, *refs), in_specs=[VMEM]...]
where the time goes in v5:
time: 140 us; the launch traced here: 139 us
  waiting for transfers between devices  49.5 us (35%)
  blocking collectives  36.4 us (26%)
  starting transfers between devices  28.3 us (20%)
  Pallas kernels  20 us (14%)
  local copies, waits for them, and re-layouts  3.49 us (2%)
    all_to_all x1, blocking collectives, shards(): lax.all_to_all(grads.reshape(32, 32, 9 * HEAD_DIM), 'ctx', 0, 0, tiled=True)  36.4 us
    all_to_all x1, waiting for transfers between devices, shards(): lax.all_to_all(packed, 'ctx', 0, 0, tiled=True).reshape(1024, 12 * HEAD_DIM)  35.5 us
    pallas_call x3, Pallas kernels, head_grads(): pl.pallas_call(lambda *refs: grads_kernel(lanes, *refs), in_specs=[VMEM]...  12.1 us
    ppermute x1, starting transfers between devices, mask_bias(): other = lax.ppermute(window_mask[0], 'ctx', mask_pairs(1))  7.58 us
    ppermute x1, waiting for transfers between devices, shards(): back = lax.ppermute(to_far, 'ctx', chain)  6.16 us
    all_to_all x1, starting transfers between devices, shards(): lax.all_to_all(packed, 'ctx', 0, 0, tiled=True).reshape(1024, 12 * HEAD_DIM)  6.02 us
    ppermute x2, starting transfers between devices, shards(): fars = [lax.ppermute(part, 'ctx', chain) for part in for_far]  5.55 us
    ppermute x2, waiting for transfers between devices, shards(): fars = [lax.ppermute(part, 'ctx', chain) for part in for_far]  4.33 us
  transfers between devices with their start and end apart: 10, of which 5 were waited for; matrix products, arithmetic and copies ran while one was open for 3% of the time, Pallas kernels for 10%

profile of v5, /device:TPU:1, one launch (start us, length us, event | category | flops | bytes accessed | tf_op | source)
XLA Modules:
  0.0 139.4 jit_solution(2946725540651080996)
XLA Ops:
  0.6 0.0 copy-start
  0.6 3.6 %pack.1 = bf16[4,2,2,2,32,1536]{5,4,3,2,1,0:T(8,128)(2,1)} custom-call(bf16[8,2,4,8,768]{4,3,2,1,0:T(8,128)(2,1)} %bitcast.111, bf16[8,2,4,8,768]{4,3,2,1,0:T(8,128)(2,1)} %bitcast.112, bf16[8,2,4,8,768]{4,3,2,1,0:T(8,128)(2,1)} %bitcast.113, bf16[8,2,4,8,768]{4,3,2,1,0:T(8,128)(2,1)} %bitcast.114), custom_call_target="tpu_custom_call" | custom-call | bytes 4000000 | tf_op jit(solution)/shard_map/pack/pallas_call | solution.py:182
  4.2 0.0 copy-done
  4.2 0.7 collective-permute-start
  4.9 7.6 %collective-permute-start.1 = (s32[8,27]{1,0:T(8,128)S(1)}, s32[8,27]{1,0:T(8,128)S(1)}, u32[]{:S(2)}, u32[]{:S(2)}) collective-permute-start(s32[8,27]{1,0:T(8,128)S(1)} %bitcast.125), channel_id=1, source_target_pairs={{0,16},{4,20},{8,48},{12,52},{16,80},{20,84},{24,112},{28,116},{32... | collective-permute-start | bytes 2600 | tf_op jit(solution)/shard_map/ppermute | solution.py:59
  12.5 6.0 %all-to-all-start = ((bf16[32,32,1536]{2,1,0:T(8,128)(2,1)}), bf16[32,32,1536]{2,1,0:T(8,128)(2,1)S(1)}, u32[]{:S(2)}, u32[]{:S(2)}) async-start(bf16[32,32,1536]{2,1,0:T(8,128)(2,1)} %bitcast.110), calls=%async_computation | async-start | bytes 6291456 | tf_op jit(solution)/shard_map/all_to_all | solution.py:383
  18.6 0.0 collective-permute-done
  18.6 0.0 collective-permute-done.1
  18.7 0.1 copy.39
  18.8 0.1 copy.40
  19.3 0.1 copy.49
  19.7 0.1 copy.50
  19.8 0.1 copy.51
  20.0 1.0 broadcast_in_dim.16
  21.0 1.8 %reshape.148 = f32[8,18,128]{2,0,1:T(8,128)S(1)} reshape(f32[8,18,4,2,16]{4,3,2,0,1:T(2,128)} %broadcast_in_dim.16) | data formatting | bytes 147456 | tf_op jit(solution)/shard_map/reshape | solution.py:92
  22.8 35.5 %all-to-all-done = bf16[32,32,1536]{2,1,0:T(8,128)(2,1)S(1)} async-done(((bf16[32,32,1536]{2,1,0:T(8,128)(2,1)}), bf16[32,32,1536]{2,1,0:T(8,128)(2,1)S(1)}, u32[]{:S(2)}, u32[]{:S(2)}) %all-to-all-start) | async-done | bytes 3145760 | tf_op jit(solution)/shard_map/all_to_all | solution.py:383
  58.3 0.2 split.1
  58.5 0.5 collective-permute-start.2
  59.0 1.9 %collective-permute-start.5 = (bf16[1024,256]{1,0:T(8,128)(2,1)S(1)}, bf16[1024,256]{1,0:T(8,128)(2,1)S(1)}, u32[]{:S(2)}, u32[]{:S(2)}) collective-permute-start(bf16[1024,256]{1,0:T(8,128)(2,1)S(1)} %get-tuple-element.24), channel_id=1, source_target_pairs={{4,32},{32,4},{36,64},{64,36},{68,96},{96,68},{100,104},{104,100},... | collective-permute-start | bytes 1572872 | tf_op jit(solution)/shard_map/ppermute | solution.py:386
  60.9 3.6 %collective-permute-start.4 = (bf16[1024,256]{1,0:T(8,128)(2,1)S(1)}, bf16[1024,256]{1,0:T(8,128)(2,1)S(1)}, u32[]{:S(2)}, u32[]{:S(2)}) collective-permute-start(bf16[1024,256]{1,0:T(8,128)(2,1)S(1)} %get-tuple-element.23), channel_id=1, source_target_pairs={{4,32},{32,4},{36,64},{64,36},{68,96},{96,68},{100,104},{104,100},... | collective-permute-start | bytes 1572872 | tf_op jit(solution)/shard_map/ppermute | solution.py:386
  64.5 0.0 collective-permute-done.2._.refs_3_
  64.6 2.1 %collective-permute-start.3 = (bf16[1024,256]{1,0:T(8,128)(2,1)S(1)}, bf16[1024,256]{1,0:T(8,128)(2,1)S(1)}, u32[]{:S(2)}, u32[]{:S(2)}) collective-permute-start(bf16[1024,256]{1,0:T(8,128)(2,1)S(1)} %take_last.1), channel_id=1, source_target_pairs={{4,32},{32,4},{36,64},{64,36},{68,96},{96,68},{100,104},{104,100},... | collective-permute-start | bytes 1572872 | tf_op jit(solution)/shard_map/ppermute | solution.py:388
  66.7 2.8 %collective-permute-done.5.refs_4_ = bf16[1024,256]{1,0:T(8,128)(2,1)S(1)} collective-permute-done((bf16[1024,256]{1,0:T(8,128)(2,1)S(1)}, bf16[1024,256]{1,0:T(8,128)(2,1)S(1)}, u32[]{:S(2)}, u32[]{:S(2)}) %collective-permute-start.5) | collective-permute-done | bytes 524320 | tf_op jit(solution)/shard_map/ppermute | solution.py:386
  69.4 4.0 %head_grads.3 = (bf16[1024,1152]{1,0:T(8,128)(2,1)S(1)}, bf16[1024,768]{1,0:T(8,128)(2,1)S(1)}, bf16[1024,512]{1,0:T(8,128)(2,1)S(1)}) custom-call(f32[8,18,128]{2,1,0:T(8,128)S(1)} %copy.55.bias.refs_0_, bf16[1024,1536]{1,0:T(8,128)(2,1)S(1)} %bitcast.102, bf16[1024,1536]{1,0:T(8,128)(2,1)S(1)} %bitcast.103, ...), custom_call_target="tpu_custom_call" | custom-call | flops 1000000000 | bytes 4500000 | tf_op jit(solution)/shard_map/head_grads/pallas_call | solution.py:302
  73.5 1.6 %collective-permute-done.4.refs_4_ = bf16[1024,256]{1,0:T(8,128)(2,1)S(1)} collective-permute-done((bf16[1024,256]{1,0:T(8,128)(2,1)S(1)}, bf16[1024,256]{1,0:T(8,128)(2,1)S(1)}, u32[]{:S(2)}, u32[]{:S(2)}) %collective-permute-start.4) | collective-permute-done | bytes 524320 | tf_op jit(solution)/shard_map/ppermute | solution.py:386
  75.1 4.0 %head_grads.4 = (bf16[1024,1152]{1,0:T(8,128)(2,1)S(1)}, bf16[1024,768]{1,0:T(8,128)(2,1)S(1)}, bf16[1024,512]{1,0:T(8,128)(2,1)S(1)}) custom-call(f32[8,18,128]{2,1,0:T(8,128)S(1)} %copy.55.bias.refs_0_, bf16[1024,1536]{1,0:T(8,128)(2,1)S(1)} %bitcast.104, ...), custom_call_target="tpu_custom_call", output_to_operand_aliasing={{0}: (5, {}), {1}: (6, {}), {2}: (7, {})} | custom-call | flops 1000000000 | bytes 4500000 | tf_op jit(solution)/shard_map/head_grads/pallas_call | solution.py:302
  79.1 1.9 %collective-permute-start.6 = (bf16[1024,512]{1,0:T(8,128)(2,1)S(1)}, bf16[1024,512]{1,0:T(8,128)(2,1)S(1)}, u32[]{:S(2)}, u32[]{:S(2)}) collective-permute-start(bf16[1024,512]{1,0:T(8,128)(2,1)S(1)} %get-tuple-element.31), channel_id=1, source_target_pairs={{4,32},{32,4},{36,64},{64,36},{68,96},{96,68},{100,104},{104,100},... | collective-permute-start | bytes 3145736 | tf_op jit(solution)/shard_map/ppermute | solution.py:391
  81.0 0.0 collective-permute-done.3.refs_4_
  81.0 4.0 %head_grads.5 = (bf16[1024,1152]{1,0:T(8,128)(2,1)S(1)}, bf16[1024,768]{1,0:T(8,128)(2,1)S(1)}, bf16[1024,256]{1,0:T(8,128)(2,1)S(1)}) custom-call(f32[8,18,128]{2,1,0:T(8,128)S(1)} %copy.55.bias.refs_0_, bf16[1024,1536]{1,0:T(8,128)(2,1)S(1)} %bitcast.106, bf16[1024,1536]{1,0:T(8,128)(2,1)S(1)} %bitcast.107, ...), custom_call_target="tpu_custom_call", output_to_operand_aliasing={{0}: (5, {}), {1}: (6, {})} | custom-call | flops 99999997952 | bytes 4500000 | tf_op jit(solution)/shard_map/head_grads/pallas_call | solution.py:302
  85.1 0.3 collective-permute-start.7
  85.4 3.6 %collective-permute-start.8 = (bf16[1024,256]{1,0:T(8,128)(2,1)S(1)}, bf16[1024,256]{1,0:T(8,128)(2,1)S(1)}, u32[]{:S(2)}, u32[]{:S(2)}) collective-permute-start(bf16[1024,256]{1,0:T(8,128)(2,1)S(1)} %get-tuple-element.33), channel_id=1, source_target_pairs={{4,32},{32,4},{36,64},{64,36},{68,96},{96,68},{100,104},{104,100},... | collective-permute-start | bytes 1572872 | tf_op jit(solution)/shard_map/ppermute | solution.py:394
  89.1 6.2 %collective-permute-done.6.halo = bf16[1024,512]{1,0:T(8,128)(2,1)S(1)} collective-permute-done((bf16[1024,512]{1,0:T(8,128)(2,1)S(1)}, bf16[1024,512]{1,0:T(8,128)(2,1)S(1)}, u32[]{:S(2)}, u32[]{:S(2)}) %collective-permute-start.6) | collective-permute-done | bytes 1048608 | tf_op jit(solution)/shard_map/ppermute | solution.py:391
  95.2 0.8 add_halo.3.grads
  96.1 0.0 collective-permute-done.7.halo
  96.1 1.3 add_halo.4.grads
  97.3 3.5 %collective-permute-done.8.halo = bf16[1024,256]{1,0:T(8,128)(2,1)S(1)} collective-permute-done((bf16[1024,256]{1,0:T(8,128)(2,1)S(1)}, bf16[1024,256]{1,0:T(8,128)(2,1)S(1)}, u32[]{:S(2)}, u32[]{:S(2)}) %collective-permute-start.8) | collective-permute-done | bytes 524320 | tf_op jit(solution)/shard_map/ppermute | solution.py:394
  100.8 0.4 add_halo.5
  101.2 36.4 %all_to_all.10 = bf16[32,32,1152]{2,1,0:T(8,128)(2,1)S(1)} all-to-all(bf16[32,32,1152]{2,1,0:T(8,128)(2,1)S(1)} %bitcast.108), channel_id=1, replica_groups=mesh['ctx'=32,'head'=4] {'ctx'}, dimensions={0} | all-to-all | bytes 4718592 | tf_op jit(solution)/shard_map/all_to_all | solution.py:398
  137.6 1.5 %unpack.1 = (bf16[8,2,4,8,768]{4,3,2,1,0:T(8,128)(2,1)}, bf16[8,2,4,8,768]{4,3,2,1,0:T(8,128)(2,1)}, bf16[8,2,4,8,768]{4,3,2,1,0:T(8,128)(2,1)}) custom-call(bf16[4,2,2,2,32,1152]{5,4,3,2,1,0:T(8,128)(2,1)S(1)} %bitcast.109), custom_call_target="tpu_custom_call" | custom-call | bytes 4700000 | tf_op jit(solution)/shard_map/unpack/pallas_call | solution.py:120
  (50 shorter events, 0.6 us)
Async XLA Ops:
  0.6 3.6 %copy-start = (s32[1,8,27]{2,1,0:T(8,128)S(1)}, s32[1,8,27]{2,1,0:T(8,128)}, u32[]{:S(2)}) copy-start(s32[1,8,27]{2,1,0:T(8,128)} %param.9) | copy-start | bytes 2596
  4.2 14.4 %collective-permute-start = (s32[8,27]{1,0:T(8,128)S(1)}, s32[8,27]{1,0:T(8,128)S(1)}, u32[]{:S(2)}, u32[]{:S(2)}) collective-permute-start(s32[8,27]{1,0:T(8,128)S(1)} %bitcast.124), channel_id=1, source_target_pairs={{0,0},{4,4},{8,32},{12,36},{16,64},{20,68},{24,96},{28,100},{32,10... | collective-permute-start | bytes 2600 | tf_op jit(solution)/shard_map/ppermute | solution.py:58
  4.9 13.7 %collective-permute-start.1 = (s32[8,27]{1,0:T(8,128)S(1)}, s32[8,27]{1,0:T(8,128)S(1)}, u32[]{:S(2)}, u32[]{:S(2)}) collective-permute-start(s32[8,27]{1,0:T(8,128)S(1)} %bitcast.125), channel_id=1, source_target_pairs={{0,16},{4,20},{8,48},{12,52},{16,80},{20,84},{24,112},{28,116},{32... | collective-permute-start | bytes 2600 | tf_op jit(solution)/shard_map/ppermute | solution.py:59
  12.5 45.8 %all-to-all-start = ((bf16[32,32,1536]{2,1,0:T(8,128)(2,1)}), bf16[32,32,1536]{2,1,0:T(8,128)(2,1)S(1)}, u32[]{:S(2)}, u32[]{:S(2)}) async-start(bf16[32,32,1536]{2,1,0:T(8,128)(2,1)} %bitcast.110), calls=%async_computation | async-start | bytes 6291456 | tf_op jit(solution)/shard_map/all_to_all | solution.py:383
  58.5 6.1 %collective-permute-start.2 = (bf16[1024,768]{1,0:T(8,128)(2,1)S(1)}, bf16[1024,768]{1,0:T(8,128)(2,1)S(1)}, u32[]{:S(2)}, u32[]{:S(2)}) collective-permute-start(bf16[1024,768]{1,0:T(8,128)(2,1)S(1)} %get-tuple-element.22), channel_id=1, source_target_pairs={{0,4},{4,0},{8,12},{12,8},{16,20},{20,16},{24,28},{28,24},{32,36},... | collective-permute-start | bytes 4718600 | tf_op jit(solution)/shard_map/ppermute | solution.py:387
  59.0 10.5 %collective-permute-start.5 = (bf16[1024,256]{1,0:T(8,128)(2,1)S(1)}, bf16[1024,256]{1,0:T(8,128)(2,1)S(1)}, u32[]{:S(2)}, u32[]{:S(2)}) collective-permute-start(bf16[1024,256]{1,0:T(8,128)(2,1)S(1)} %get-tuple-element.24), channel_id=1, source_target_pairs={{4,32},{32,4},{36,64},{64,36},{68,96},{96,68},{100,104},{104,100},... | collective-permute-start | bytes 1572872 | tf_op jit(solution)/shard_map/ppermute | solution.py:386
  60.9 14.2 %collective-permute-start.4 = (bf16[1024,256]{1,0:T(8,128)(2,1)S(1)}, bf16[1024,256]{1,0:T(8,128)(2,1)S(1)}, u32[]{:S(2)}, u32[]{:S(2)}) collective-permute-start(bf16[1024,256]{1,0:T(8,128)(2,1)S(1)} %get-tuple-element.23), channel_id=1, source_target_pairs={{4,32},{32,4},{36,64},{64,36},{68,96},{96,68},{100,104},{104,100},... | collective-permute-start | bytes 1572872 | tf_op jit(solution)/shard_map/ppermute | solution.py:386
  64.6 16.5 %collective-permute-start.3 = (bf16[1024,256]{1,0:T(8,128)(2,1)S(1)}, bf16[1024,256]{1,0:T(8,128)(2,1)S(1)}, u32[]{:S(2)}, u32[]{:S(2)}) collective-permute-start(bf16[1024,256]{1,0:T(8,128)(2,1)S(1)} %take_last.1), channel_id=1, source_target_pairs={{4,32},{32,4},{36,64},{64,36},{68,96},{96,68},{100,104},{104,100},... | collective-permute-start | bytes 1572872 | tf_op jit(solution)/shard_map/ppermute | solution.py:388
  79.1 16.1 %collective-permute-start.6 = (bf16[1024,512]{1,0:T(8,128)(2,1)S(1)}, bf16[1024,512]{1,0:T(8,128)(2,1)S(1)}, u32[]{:S(2)}, u32[]{:S(2)}) collective-permute-start(bf16[1024,512]{1,0:T(8,128)(2,1)S(1)} %get-tuple-element.31), channel_id=1, source_target_pairs={{4,32},{32,4},{36,64},{64,36},{68,96},{96,68},{100,104},{104,100},... | collective-permute-start | bytes 3145736 | tf_op jit(solution)/shard_map/ppermute | solution.py:391
  85.1 11.0 %collective-permute-start.7 = (bf16[1024,768]{1,0:T(8,128)(2,1)S(1)}, bf16[1024,768]{1,0:T(8,128)(2,1)S(1)}, u32[]{:S(2)}, u32[]{:S(2)}) collective-permute-start(bf16[1024,768]{1,0:T(8,128)(2,1)S(1)} %get-tuple-element.32), channel_id=1, source_target_pairs={{0,4},{4,0},{8,12},{12,8},{16,20},{20,16},{24,28},{28,24},{32,36},... | collective-permute-start | bytes 4718600 | tf_op jit(solution)/shard_map/ppermute | solution.py:393
  85.4 15.4 %collective-permute-start.8 = (bf16[1024,256]{1,0:T(8,128)(2,1)S(1)}, bf16[1024,256]{1,0:T(8,128)(2,1)S(1)}, u32[]{:S(2)}, u32[]{:S(2)}) collective-permute-start(bf16[1024,256]{1,0:T(8,128)(2,1)S(1)} %get-tuple-element.33), channel_id=1, source_target_pairs={{4,32},{32,4},{36,64},{64,36},{68,96},{96,68},{100,104},{104,100},... | collective-permute-start | bytes 1572872 | tf_op jit(solution)/shard_map/ppermute | solution.py:394

commit v6 on v5

--- a/solution.py
+++ b/solution.py
@@ -144,30 +144,28 @@
 VMEM_LIMIT = 62 * 1024 * 1024
 
 
-def pack_kernel(blocks, ins, *refs):
-    count = len(ins)
-    inputs, out, taken, (packed, in_sems, out_sems) = refs[:count], refs[count], refs[count + 1 : -3], refs[-3:]
+def pack_kernel(blocks, *refs):
+    inputs, out, (taken, packed, in_sems, out_sems) = refs[:-5], refs[-5], refs[-4:]
+    count = len(inputs)
     reads, writes = [], []
-    for x in ORDER:
-        for i, (first, heads) in enumerate(ins):
-            for half in range(HALVES):
-                lane = (half * HEADS_LOCAL + first) * HEAD_DIM
-                source = inputs[i].at[:, :, x, :, lane : lane + heads * HEAD_DIM]
-                reads.append(pltpu.make_async_copy(source, taken[i].at[x, half], in_sems.at[x, i, half]))
-                reads[-1].start()
-    each = count * HALVES
-    for n, x in enumerate(ORDER):
-        if n % 2 == 0:
-            for read in reads[n * each : (n + 2) * each]:
-                read.wait()
+    for x in range(XS):
+        for strip in range(STRIPS):
+            run = run_of(x, strip)
+            for i, ref in enumerate(inputs):
+                read = pltpu.make_async_copy(ref.at[:, strip, run], taken.at[i, strip, run], in_sems.at[x, strip, i])
+                reads.append(read)
+                read.start()
+    each = count * STRIPS
+    for x in range(XS):
+        for read in reads[x * each : (x + 1) * each]:
+            read.wait()
         for half in range(HALVES):
             for strip in range(STRIPS):
                 for core in range(CORES):
                     for n, (i, j) in enumerate(blocks):
-                        lane = (j - ins[i][0]) * HEAD_DIM
-                        cells = taken[i][run_of(x, strip), half, :, strip, :, lane : lane + HEAD_DIM]
-                        cells = cells.astype(jnp.float32)[:, core * TILE : (core + 1) * TILE].reshape(32, HEAD_DIM)
-                        to = n * HEAD_DIM
+                        lane, to = (half * HEADS_LOCAL + j) * HEAD_DIM, n * HEAD_DIM
+                        cells = taken[i, strip, run_of(x, strip), :, :, lane : lane + HEAD_DIM].astype(jnp.float32)
+                        cells = cells[:, core * TILE : (core + 1) * TILE].reshape(32, HEAD_DIM)
                         packed[x, half, strip, core, :, to : to + HEAD_DIM] = cells.astype(jnp.bfloat16)
             writes.append(pltpu.make_async_copy(packed.at[x, half], out.at[x, half], out_sems.at[x, half]))
             writes[-1].start()
@@ -175,36 +173,35 @@
         write.wait()
 
 
-def pack(tensors, ins, blocks, name):
+def pack(tensors, blocks):
     views = [t.reshape(8, STRIPS, XS, 8, 768) for t in tensors]
     out = (XS, HALVES, STRIPS, CORES, 32, len(blocks) * HEAD_DIM)
-    taken = [pltpu.VMEM((XS, HALVES, 8, STRIPS, 8, heads * HEAD_DIM), jnp.bfloat16) for _, heads in ins]
     return pl.pallas_call(
-        lambda *refs: pack_kernel(blocks, ins, *refs),
+        lambda *refs: pack_kernel(blocks, *refs),
         in_specs=[ANY] * len(views),
         out_specs=ANY,
         out_shape=jax.ShapeDtypeStruct(out, jnp.bfloat16),
-        scratch_shapes=taken
-        + [
+        scratch_shapes=[
+            pltpu.VMEM((len(views), STRIPS, XS, 8, 8, 768), jnp.bfloat16),
             pltpu.VMEM(out, jnp.bfloat16),
-            pltpu.SemaphoreType.DMA((XS, len(ins), HALVES)),
+            pltpu.SemaphoreType.DMA((XS, STRIPS, len(views))),
             pltpu.SemaphoreType.DMA((XS, HALVES)),
         ],
         compiler_params=pltpu.CompilerParams(vmem_limit_bytes=VMEM_LIMIT),
         cost_estimate=pl.CostEstimate(flops=0, bytes_accessed=4_000_000, transcendentals=0),
-        name=name,
+        name="pack",
     )(*views).reshape(32, 32, len(blocks) * HEAD_DIM)
 
 
 def grads_kernel(lanes, *refs):
-    qg_lane, own_lane, near_lane, head, far_lane = lanes
+    qg_lane, own_lane, near_lane, head = lanes
     bias_ref, qg, own, near, far = refs[:5]
     grads, to_near, to_far = refs[-3:]
     time_blocks = bias_ref.shape[0]
     wide = 2 * HEAD_DIM
     sources = ((own, own_lane), (near, near_lane), (far, 0))
     mine, dq_lane = head * wide, 3 * wide + head * HEAD_DIM
-    targets = ((grads, mine), (to_near, mine), (to_far, far_lane))
+    targets = ((grads, mine), (to_near, mine), (to_far, 0))
     both, raw, pairs, slopes = {}, {}, {}, {}
     over_channels = (((1,), (1,)), ((), ()))
 
@@ -295,23 +292,23 @@
     to_keys(time_blocks - 1)
 
 
-def head_grads(bias, everything, near, far, shared, head, far_lane, far_lanes, flops):
+def head_grads(bias, everything, near, far, shared, head, flops, after=()):
     rows = everything.shape[0]
     wide = 2 * HEAD_DIM
-    lanes = ((HEADS_LOCAL + head) * wide, head * wide, head * wide, head, far_lane)
+    lanes = ((HEADS_LOCAL + head) * wide, head * wide, head * wide, head)
     return pl.pallas_call(
         lambda *refs: grads_kernel(lanes, *refs),
-        in_specs=[VMEM] * (5 + len(shared)),
+        in_specs=[VMEM] * (5 + len(shared)) + [ANY] * len(after),
         out_specs=[VMEM] * 3,
         out_shape=[
             jax.ShapeDtypeStruct((rows, lanes_out), jnp.bfloat16)
-            for lanes_out in (9 * HEAD_DIM, 6 * HEAD_DIM, far_lanes)
+            for lanes_out in (9 * HEAD_DIM, 6 * HEAD_DIM, wide)
         ],
         input_output_aliases={5 + i: i for i in range(len(shared))},
         compiler_params=pltpu.CompilerParams(vmem_limit_bytes=SMALL_LIMIT),
         cost_estimate=pl.CostEstimate(flops=flops, bytes_accessed=4_500_000, transcendentals=1_200_000),
         name="head_grads",
-    )(bias, everything, everything, near, far, *shared)
+    )(bias, everything, everything, near, far, *shared, *after)
 
 
 def add_halo(grads, halo, first, flops):
@@ -378,7 +375,7 @@
     wide = 2 * HEAD_DIM
     everything = tuple((i, j) for j in range(HEADS_LOCAL) for i in (0, 1))
     everything += tuple((i, j) for j in range(HEADS_LOCAL) for i in (2, 3))
-    packed = pack((keys, values, queries, out_grad), ((0, 3),) * 4, everything, "pack")
+    packed = pack((keys, values, queries, out_grad), everything)
     packed, window_mask = lax.optimization_barrier((packed, window_mask))
     arrived = lax.all_to_all(packed, "ctx", 0, 0, tiled=True).reshape(1024, 12 * HEAD_DIM)
     bias = mask_bias(window_mask)
@@ -386,13 +383,16 @@
     fars = [lax.ppermute(part, "ctx", chain) for part in for_far]
     near = lax.ppermute(for_near, "ctx", swap)
     fars.append(lax.ppermute(take_last(arrived, near), "ctx", chain))
-    shared = head_grads(bias, arrived, near, fars[0], (), 0, 0, 2 * wide, 1_000_000_000)
-    grads, to_near, to_far = head_grads(bias, arrived, near, fars[1], shared, 1, wide, 2 * wide, 1_000_000_000)
+    grads, to_near, to_far = head_grads(bias, arrived, near, fars[0], (), 0, 1_000_000_000)
     back = lax.ppermute(to_far, "ctx", chain)
-    grads, to_near, to_far = head_grads(bias, arrived, near, fars[2], (grads, to_near), 2, 0, wide, 100_000_000_000)
+    grads, to_near, to_far = head_grads(bias, arrived, near, fars[1], (grads, to_near), 1, 1_000_000_000)
+    next_back = lax.ppermute(to_far, "ctx", chain)
+    shared = (grads, to_near)
+    grads, to_near, to_far = head_grads(bias, arrived, near, fars[2], shared, 2, 3_000_000_000)
     near_back = lax.ppermute(to_near, "ctx", swap)
     last_back = lax.ppermute(to_far, "ctx", chain)
-    grads = add_halo(grads, back, 0, 100_000_000_000)
+    grads = add_halo(grads, back, 0, 3_000_000_000)
+    grads = add_halo(grads, next_back, 1, 100_000_000_000)
     grads = add_halo(grads, near_back, 0, 1000)
     grads = add_halo(grads, last_back, 2, 1000)
     grads = lax.all_to_all(grads.reshape(32, 32, 9 * HEAD_DIM), "ctx", 0, 0, tiled=True)

time: 140 us -> 136 us (0.971)
  waiting for transfers between devices: 49.5 us -> 44.8 us
  starting transfers between devices: 28.3 us -> 29.8 us
    ppermute x1, waiting for transfers between devices: 6.16 us -> 0.01 us  [shards(): back = lax.ppermute(to_far, 'ctx', chain)]
    ppermute x1, starting transfers between devices: 7.58 us -> 3.81 us  [mask_bias(): other = lax.ppermute(window_mask[0], 'ctx', mask_pairs(1))]
    ppermute x0 -> x1, starting transfers between devices: none -> 3.64 us  [shards(): next_back = lax.ppermute(to_far, 'ctx', chain)]
    all_to_all x1, starting transfers between devices: 6.02 us -> 9.64 us  [shards(): lax.all_to_all(packed, 'ctx', 0, 0, tiled=True).reshape(1024, 12 * HEAD_DIM)]
    ppermute x0 -> x1, waiting for transfers between devices: none -> 2.1 us  [shards(): next_back = lax.ppermute(to_far, 'ctx', chain)]
    ppermute x1, starting transfers between devices: 3.63 us -> 1.93 us  [shards(): last_back = lax.ppermute(to_far, 'ctx', chain)]
  transfers between devices with their start and end apart: 10 -> 11, of which waited for: 5 -> 5; matrix products, arithmetic and copies ran while one was open for 3% -> 3% of each run, Pallas kernels for 10% -> 10%
where the time goes in v6:
time: 136 us
  waiting for transfers between devices  44.8 us (33%)
  blocking collectives  36.4 us (27%)
  starting transfers between devices  29.8 us (22%)
  Pallas kernels  19.7 us (14%)
  local copies, waits for them, and re-layouts  3.49 us (3%)
  between operations  1.37 us (1%)
    all_to_all x1, blocking collectives, shards(): lax.all_to_all(grads.reshape(32, 32, 9 * HEAD_DIM), 'ctx', 0, 0, tiled=True)  36.4 us
    all_to_all x1, waiting for transfers between devices, shards(): lax.all_to_all(packed, 'ctx', 0, 0, tiled=True).reshape(1024, 12 * HEAD_DIM)  35.5 us
    pallas_call x3, Pallas kernels, head_grads(): pl.pallas_call(lambda *refs: grads_kernel(lanes, *refs), in_specs=[VMEM]...  12.1 us
    all_to_all x1, starting transfers between devices, shards(): lax.all_to_all(packed, 'ctx', 0, 0, tiled=True).reshape(1024, 12 * HEAD_DIM)  9.64 us
    ppermute x2, starting transfers between devices, shards(): fars = [lax.ppermute(part, 'ctx', chain) for part in for_far]  5.55 us
    ppermute x1, waiting for transfers between devices, shards(): last_back = lax.ppermute(to_far, 'ctx', chain)  3.82 us
    ppermute x1, starting transfers between devices, mask_bias(): other = lax.ppermute(window_mask[0], 'ctx', mask_pairs(1))  3.81 us
    ppermute x1, starting transfers between devices, shards(): next_back = lax.ppermute(to_far, 'ctx', chain)  3.64 us
  transfers between devices with their start and end apart: 11, of which 5 were waited for; matrix products, arithmetic and copies ran while one was open for 3% of the time, Pallas kernels for 10%

profile of v6, /device:TPU:1, one launch (start us, length us, event | category | flops | bytes accessed | tf_op | source)
XLA Modules:
  0.0 135.9 jit_solution(8616153830516498691)
XLA Ops:
  0.6 0.0 copy-start
  0.6 3.3 %pack.1 = bf16[4,2,2,2,32,1536]{5,4,3,2,1,0:T(8,128)(2,1)} custom-call(bf16[8,2,4,8,768]{4,3,2,1,0:T(8,128)(2,1)} %bitcast.111, bf16[8,2,4,8,768]{4,3,2,1,0:T(8,128)(2,1)} %bitcast.112, bf16[8,2,4,8,768]{4,3,2,1,0:T(8,128)(2,1)} %bitcast.113, bf16[8,2,4,8,768]{4,3,2,1,0:T(8,128)(2,1)} %bitcast.114), custom_call_target="tpu_custom_call" | custom-call | bytes 4000000 | tf_op jit(solution)/shard_map/pack/pallas_call | solution.py:179
  3.9 0.0 copy-done
  4.0 3.8 %collective-permute-start.1 = (s32[8,27]{1,0:T(8,128)S(1)}, s32[8,27]{1,0:T(8,128)S(1)}, u32[]{:S(2)}, u32[]{:S(2)}) collective-permute-start(s32[8,27]{1,0:T(8,128)S(1)} %bitcast.124), channel_id=1, source_target_pairs={{0,16},{4,20},{8,48},{12,52},{16,80},{20,84},{24,112},{28,116},{32... | collective-permute-start | bytes 2600 | tf_op jit(solution)/shard_map/ppermute | solution.py:59
  7.8 0.6 collective-permute-start
  8.4 9.6 %all-to-all-start = ((bf16[32,32,1536]{2,1,0:T(8,128)(2,1)}), bf16[32,32,1536]{2,1,0:T(8,128)(2,1)S(1)}, u32[]{:S(2)}, u32[]{:S(2)}) async-start(bf16[32,32,1536]{2,1,0:T(8,128)(2,1)} %bitcast.110), calls=%async_computation | async-start | bytes 6291456 | tf_op jit(solution)/shard_map/all_to_all | solution.py:380
  18.2 0.0 collective-permute-done.1
  18.2 0.0 collective-permute-done
  18.2 0.1 copy.39
  18.3 0.1 copy.40
  19.1 0.1 copy.49
  19.3 0.1 copy.50
  19.4 0.1 copy.51
  19.5 1.0 broadcast_in_dim.16
  20.6 1.8 %reshape.148 = f32[8,18,128]{2,0,1:T(8,128)S(1)} reshape(f32[8,18,4,2,16]{4,3,2,0,1:T(2,128)} %broadcast_in_dim.16) | data formatting | bytes 147456 | tf_op jit(solution)/shard_map/reshape | solution.py:92
  22.4 35.5 %all-to-all-done = bf16[32,32,1536]{2,1,0:T(8,128)(2,1)S(1)} async-done(((bf16[32,32,1536]{2,1,0:T(8,128)(2,1)}), bf16[32,32,1536]{2,1,0:T(8,128)(2,1)S(1)}, u32[]{:S(2)}, u32[]{:S(2)}) %all-to-all-start) | async-done | bytes 3145760 | tf_op jit(solution)/shard_map/all_to_all | solution.py:380
  57.8 0.2 split.1
  58.0 0.5 collective-permute-start.2
  58.5 1.9 %collective-permute-start.5 = (bf16[1024,256]{1,0:T(8,128)(2,1)S(1)}, bf16[1024,256]{1,0:T(8,128)(2,1)S(1)}, u32[]{:S(2)}, u32[]{:S(2)}) collective-permute-start(bf16[1024,256]{1,0:T(8,128)(2,1)S(1)} %get-tuple-element.24), channel_id=1, source_target_pairs={{4,32},{32,4},{36,64},{64,36},{68,96},{96,68},{100,104},{104,100},... | collective-permute-start | bytes 1572872 | tf_op jit(solution)/shard_map/ppermute | solution.py:383
  60.4 3.6 %collective-permute-start.4 = (bf16[1024,256]{1,0:T(8,128)(2,1)S(1)}, bf16[1024,256]{1,0:T(8,128)(2,1)S(1)}, u32[]{:S(2)}, u32[]{:S(2)}) collective-permute-start(bf16[1024,256]{1,0:T(8,128)(2,1)S(1)} %get-tuple-element.23), channel_id=1, source_target_pairs={{4,32},{32,4},{36,64},{64,36},{68,96},{96,68},{100,104},{104,100},... | collective-permute-start | bytes 1572872 | tf_op jit(solution)/shard_map/ppermute | solution.py:383
  64.1 0.0 collective-permute-done.2._.refs_3_
  64.1 1.9 %collective-permute-start.3 = (bf16[1024,256]{1,0:T(8,128)(2,1)S(1)}, bf16[1024,256]{1,0:T(8,128)(2,1)S(1)}, u32[]{:S(2)}, u32[]{:S(2)}) collective-permute-start(bf16[1024,256]{1,0:T(8,128)(2,1)S(1)} %take_last.1), channel_id=1, source_target_pairs={{4,32},{32,4},{36,64},{64,36},{68,96},{96,68},{100,104},{104,100},... | collective-permute-start | bytes 1572872 | tf_op jit(solution)/shard_map/ppermute | solution.py:385
  66.1 2.9 %collective-permute-done.5.refs_4_ = bf16[1024,256]{1,0:T(8,128)(2,1)S(1)} collective-permute-done((bf16[1024,256]{1,0:T(8,128)(2,1)S(1)}, bf16[1024,256]{1,0:T(8,128)(2,1)S(1)}, u32[]{:S(2)}, u32[]{:S(2)}) %collective-permute-start.5) | collective-permute-done | bytes 524320 | tf_op jit(solution)/shard_map/ppermute | solution.py:383
  69.0 4.0 %head_grads.3 = (bf16[1024,1152]{1,0:T(8,128)(2,1)S(1)}, bf16[1024,768]{1,0:T(8,128)(2,1)S(1)}, bf16[1024,256]{1,0:T(8,128)(2,1)S(1)}) custom-call(f32[8,18,128]{2,1,0:T(8,128)S(1)} %copy.55.bias.refs_0_, bf16[1024,1536]{1,0:T(8,128)(2,1)S(1)} %bitcast.102, bf16[1024,1536]{1,0:T(8,128)(2,1)S(1)} %bitcast.103, ...), custom_call_target="tpu_custom_call" | custom-call | flops 1000000000 | bytes 4500000 | tf_op jit(solution)/shard_map/head_grads/pallas_call | solution.py:299
  73.0 2.1 %collective-permute-start.6 = (bf16[1024,256]{1,0:T(8,128)(2,1)S(1)}, bf16[1024,256]{1,0:T(8,128)(2,1)S(1)}, u32[]{:S(2)}, u32[]{:S(2)}) collective-permute-start(bf16[1024,256]{1,0:T(8,128)(2,1)S(1)} %get-tuple-element.30), channel_id=1, source_target_pairs={{4,32},{32,4},{36,64},{64,36},{68,96},{96,68},{100,104},{104,100},... | collective-permute-start | bytes 1572872 | tf_op jit(solution)/shard_map/ppermute | solution.py:387
  75.1 0.0 collective-permute-done.4.refs_4_
  75.2 4.0 %head_grads.4 = (bf16[1024,1152]{1,0:T(8,128)(2,1)S(1)}, bf16[1024,768]{1,0:T(8,128)(2,1)S(1)}, bf16[1024,256]{1,0:T(8,128)(2,1)S(1)}) custom-call(f32[8,18,128]{2,1,0:T(8,128)S(1)} %copy.55.bias.refs_0_, bf16[1024,1536]{1,0:T(8,128)(2,1)S(1)} %bitcast.104, bf16[1024,1536]{1,0:T(8,128)(2,1)S(1)} %bitcast.105, ...), custom_call_target="tpu_custom_call", output_to_operand_aliasing={{0}: (5, {}), {1}: (6, {})} | custom-call | flops 1000000000 | bytes 4500000 | tf_op jit(solution)/shard_map/head_grads/pallas_call | solution.py:299
  79.2 3.6 %collective-permute-start.7 = (bf16[1024,256]{1,0:T(8,128)(2,1)S(1)}, bf16[1024,256]{1,0:T(8,128)(2,1)S(1)}, u32[]{:S(2)}, u32[]{:S(2)}) collective-permute-start(bf16[1024,256]{1,0:T(8,128)(2,1)S(1)} %get-tuple-element.31), channel_id=1, source_target_pairs={{4,32},{32,4},{36,64},{64,36},{68,96},{96,68},{100,104},{104,100},... | collective-permute-start | bytes 1572872 | tf_op jit(solution)/shard_map/ppermute | solution.py:389
  82.9 0.0 collective-permute-done.3.refs_4_
  82.9 4.0 %head_grads.5 = (bf16[1024,1152]{1,0:T(8,128)(2,1)S(1)}, bf16[1024,768]{1,0:T(8,128)(2,1)S(1)}, bf16[1024,256]{1,0:T(8,128)(2,1)S(1)}) custom-call(f32[8,18,128]{2,1,0:T(8,128)S(1)} %copy.55.bias.refs_0_, bf16[1024,1536]{1,0:T(8,128)(2,1)S(1)} %bitcast.106, bf16[1024,1536]{1,0:T(8,128)(2,1)S(1)} %bitcast.107, ...), custom_call_target="tpu_custom_call", output_to_operand_aliasing={{0}: (5, {}), {1}: (6, {})} | custom-call | flops 3000000000 | bytes 4500000 | tf_op jit(solution)/shard_map/head_grads/pallas_call | solution.py:299
  86.9 1.9 %collective-permute-start.9 = (bf16[1024,256]{1,0:T(8,128)(2,1)S(1)}, bf16[1024,256]{1,0:T(8,128)(2,1)S(1)}, u32[]{:S(2)}, u32[]{:S(2)}) collective-permute-start(bf16[1024,256]{1,0:T(8,128)(2,1)S(1)} %get-tuple-element.33), channel_id=1, source_target_pairs={{4,32},{32,4},{36,64},{64,36},{68,96},{96,68},{100,104},{104,100},... | collective-permute-start | bytes 1572872 | tf_op jit(solution)/shard_map/ppermute | solution.py:393
  88.9 0.1 collective-permute-start.8
  88.9 0.0 collective-permute-done.6.halo
  89.0 0.4 add_halo.4.grads
  89.4 2.1 %collective-permute-done.7.halo = bf16[1024,256]{1,0:T(8,128)(2,1)S(1)} collective-permute-done((bf16[1024,256]{1,0:T(8,128)(2,1)S(1)}, bf16[1024,256]{1,0:T(8,128)(2,1)S(1)}, u32[]{:S(2)}, u32[]{:S(2)}) %collective-permute-start.7) | collective-permute-done | bytes 524320 | tf_op jit(solution)/shard_map/ppermute | solution.py:389
  91.5 0.4 add_halo.5.grads
  91.9 0.5 collective-permute-done.8.halo
  92.3 1.3 add_halo.6.grads
  93.6 3.8 %collective-permute-done.9.halo = bf16[1024,256]{1,0:T(8,128)(2,1)S(1)} collective-permute-done((bf16[1024,256]{1,0:T(8,128)(2,1)S(1)}, bf16[1024,256]{1,0:T(8,128)(2,1)S(1)}, u32[]{:S(2)}, u32[]{:S(2)}) %collective-permute-start.9) | collective-permute-done | bytes 524320 | tf_op jit(solution)/shard_map/ppermute | solution.py:393
  97.4 0.4 add_halo.7
  97.8 36.4 %all_to_all.10 = bf16[32,32,1152]{2,1,0:T(8,128)(2,1)S(1)} all-to-all(bf16[32,32,1152]{2,1,0:T(8,128)(2,1)S(1)} %bitcast.108), channel_id=1, replica_groups=mesh['ctx'=32,'head'=4] {'ctx'}, dimensions={0} | all-to-all | bytes 4718592 | tf_op jit(solution)/shard_map/all_to_all | solution.py:398
  134.2 1.5 %unpack.1 = (bf16[8,2,4,8,768]{4,3,2,1,0:T(8,128)(2,1)}, bf16[8,2,4,8,768]{4,3,2,1,0:T(8,128)(2,1)}, bf16[8,2,4,8,768]{4,3,2,1,0:T(8,128)(2,1)}) custom-call(bf16[4,2,2,2,32,1152]{5,4,3,2,1,0:T(8,128)(2,1)S(1)} %bitcast.109), custom_call_target="tpu_custom_call" | custom-call | bytes 4700000 | tf_op jit(solution)/shard_map/unpack/pallas_call | solution.py:120
  (50 shorter events, 0.6 us)
Async XLA Ops:
  0.6 3.3 %copy-start = (s32[1,8,27]{2,1,0:T(8,128)S(1)}, s32[1,8,27]{2,1,0:T(8,128)}, u32[]{:S(2)}) copy-start(s32[1,8,27]{2,1,0:T(8,128)} %param.9) | copy-start | bytes 2596
  4.0 14.2 %collective-permute-start.1 = (s32[8,27]{1,0:T(8,128)S(1)}, s32[8,27]{1,0:T(8,128)S(1)}, u32[]{:S(2)}, u32[]{:S(2)}) collective-permute-start(s32[8,27]{1,0:T(8,128)S(1)} %bitcast.124), channel_id=1, source_target_pairs={{0,16},{4,20},{8,48},{12,52},{16,80},{20,84},{24,112},{28,116},{32... | collective-permute-start | bytes 2600 | tf_op jit(solution)/shard_map/ppermute | solution.py:59
  7.8 10.4 %collective-permute-start = (s32[8,27]{1,0:T(8,128)S(1)}, s32[8,27]{1,0:T(8,128)S(1)}, u32[]{:S(2)}, u32[]{:S(2)}) collective-permute-start(s32[8,27]{1,0:T(8,128)S(1)} %bitcast.125), channel_id=1, source_target_pairs={{0,0},{4,4},{8,32},{12,36},{16,64},{20,68},{24,96},{28,100},{32,10... | collective-permute-start | bytes 2600 | tf_op jit(solution)/shard_map/ppermute | solution.py:58
  8.4 49.4 %all-to-all-start = ((bf16[32,32,1536]{2,1,0:T(8,128)(2,1)}), bf16[32,32,1536]{2,1,0:T(8,128)(2,1)S(1)}, u32[]{:S(2)}, u32[]{:S(2)}) async-start(bf16[32,32,1536]{2,1,0:T(8,128)(2,1)} %bitcast.110), calls=%async_computation | async-start | bytes 6291456 | tf_op jit(solution)/shard_map/all_to_all | solution.py:380
  58.0 6.1 %collective-permute-start.2 = (bf16[1024,768]{1,0:T(8,128)(2,1)S(1)}, bf16[1024,768]{1,0:T(8,128)(2,1)S(1)}, u32[]{:S(2)}, u32[]{:S(2)}) collective-permute-start(bf16[1024,768]{1,0:T(8,128)(2,1)S(1)} %get-tuple-element.22), channel_id=1, source_target_pairs={{0,4},{4,0},{8,12},{12,8},{16,20},{20,16},{24,28},{28,24},{32,36},... | collective-permute-start | bytes 4718600 | tf_op jit(solution)/shard_map/ppermute | solution.py:384
  58.5 10.5 %collective-permute-start.5 = (bf16[1024,256]{1,0:T(8,128)(2,1)S(1)}, bf16[1024,256]{1,0:T(8,128)(2,1)S(1)}, u32[]{:S(2)}, u32[]{:S(2)}) collective-permute-start(bf16[1024,256]{1,0:T(8,128)(2,1)S(1)} %get-tuple-element.24), channel_id=1, source_target_pairs={{4,32},{32,4},{36,64},{64,36},{68,96},{96,68},{100,104},{104,100},... | collective-permute-start | bytes 1572872 | tf_op jit(solution)/shard_map/ppermute | solution.py:383
  60.4 14.7 %collective-permute-start.4 = (bf16[1024,256]{1,0:T(8,128)(2,1)S(1)}, bf16[1024,256]{1,0:T(8,128)(2,1)S(1)}, u32[]{:S(2)}, u32[]{:S(2)}) collective-permute-start(bf16[1024,256]{1,0:T(8,128)(2,1)S(1)} %get-tuple-element.23), channel_id=1, source_target_pairs={{4,32},{32,4},{36,64},{64,36},{68,96},{96,68},{100,104},{104,100},... | collective-permute-start | bytes 1572872 | tf_op jit(solution)/shard_map/ppermute | solution.py:383
  64.1 18.7 %collective-permute-start.3 = (bf16[1024,256]{1,0:T(8,128)(2,1)S(1)}, bf16[1024,256]{1,0:T(8,128)(2,1)S(1)}, u32[]{:S(2)}, u32[]{:S(2)}) collective-permute-start(bf16[1024,256]{1,0:T(8,128)(2,1)S(1)} %take_last.1), channel_id=1, source_target_pairs={{4,32},{32,4},{36,64},{64,36},{68,96},{96,68},{100,104},{104,100},... | collective-permute-start | bytes 1572872 | tf_op jit(solution)/shard_map/ppermute | solution.py:385
  73.0 15.9 %collective-permute-start.6 = (bf16[1024,256]{1,0:T(8,128)(2,1)S(1)}, bf16[1024,256]{1,0:T(8,128)(2,1)S(1)}, u32[]{:S(2)}, u32[]{:S(2)}) collective-permute-start(bf16[1024,256]{1,0:T(8,128)(2,1)S(1)} %get-tuple-element.30), channel_id=1, source_target_pairs={{4,32},{32,4},{36,64},{64,36},{68,96},{96,68},{100,104},{104,100},... | collective-permute-start | bytes 1572872 | tf_op jit(solution)/shard_map/ppermute | solution.py:387
  79.2 12.3 %collective-permute-start.7 = (bf16[1024,256]{1,0:T(8,128)(2,1)S(1)}, bf16[1024,256]{1,0:T(8,128)(2,1)S(1)}, u32[]{:S(2)}, u32[]{:S(2)}) collective-permute-start(bf16[1024,256]{1,0:T(8,128)(2,1)S(1)} %get-tuple-element.31), channel_id=1, source_target_pairs={{4,32},{32,4},{36,64},{64,36},{68,96},{96,68},{100,104},{104,100},... | collective-permute-start | bytes 1572872 | tf_op jit(solution)/shard_map/ppermute | solution.py:389
  86.9 10.5 %collective-permute-start.9 = (bf16[1024,256]{1,0:T(8,128)(2,1)S(1)}, bf16[1024,256]{1,0:T(8,128)(2,1)S(1)}, u32[]{:S(2)}, u32[]{:S(2)}) collective-permute-start(bf16[1024,256]{1,0:T(8,128)(2,1)S(1)} %get-tuple-element.33), channel_id=1, source_target_pairs={{4,32},{32,4},{36,64},{64,36},{68,96},{96,68},{100,104},{104,100},... | collective-permute-start | bytes 1572872 | tf_op jit(solution)/shard_map/ppermute | solution.py:393
  88.9 3.5 %collective-permute-start.8 = (bf16[1024,768]{1,0:T(8,128)(2,1)S(1)}, bf16[1024,768]{1,0:T(8,128)(2,1)S(1)}, u32[]{:S(2)}, u32[]{:S(2)}) collective-permute-start(bf16[1024,768]{1,0:T(8,128)(2,1)S(1)} %get-tuple-element.32), channel_id=1, source_target_pairs={{0,4},{4,0},{8,12},{12,8},{16,20},{20,16},{24,28},{28,24},{32,36},... | collective-permute-start | bytes 4718600 | tf_op jit(solution)/shard_map/ppermute | solution.py:392

commit v7 on v6

--- a/solution.py
+++ b/solution.py
@@ -10,7 +10,6 @@
 ROW_BLOCKS = 2
 NEG_FILL = -1e30
 SCALE = HEAD_DIM ** (-0.5)
-LOG2E = 1.4426950408889634
 HEADS_LOCAL = 3
 BLOCK = ROW_BLOCKS * TILE**3
 STEPS = (-1, 0, 1)
@@ -228,7 +227,7 @@
             s = lax.dot_general(k, q, over_channels, preferred_element_type=jnp.float32)
             probs.append(lax.dot_general(v, g, over_channels, preferred_element_type=jnp.float32))
             bias = [block_bias(bias_ref, t, near_t - t + 1, block) for near_t in range(low, high + 1)]
-            s = s * (SCALE * LOG2E) + jnp.concatenate(bias, axis=0)
+            s = s * SCALE + jnp.concatenate(bias, axis=0)
             block_top = jnp.max(s, axis=0, keepdims=True)
             top = block_top if top is None else jnp.maximum(top, block_top)
             scores.append(s)
@@ -238,22 +237,24 @@
         scores, probs, top = raw.pop(t)
         low, high, _ = window(t)
         total = jnp.zeros((1, BLOCK), jnp.float32)
-        dots = jnp.zeros((1, BLOCK), jnp.float32)
         exps = []
-        for s, pg in zip(scores, probs):
-            e = jnp.exp2(s - top)
+        for s in scores:
+            e = jnp.exp(s - top)
             total += jnp.sum(e, axis=0, keepdims=True)
-            dots += jnp.sum(e * pg, axis=0, keepdims=True)
             exps.append(e)
-        return low, high, exps, probs, 1.0 / total, dots
-
-    def slope(t, low, high, exps, probs, inv, dots):
-        row_dot = dots * inv
+        inv = 1.0 / total
+        row_dot = jnp.zeros((1, BLOCK), jnp.float32)
+        lows = []
+        for e, pg in zip(exps, probs):
+            lows.append((e * inv).astype(jnp.bfloat16))
+            row_dot += jnp.sum(lows[-1].astype(jnp.float32) * pg, axis=0, keepdims=True)
+        return low, high, exps, probs, inv, row_dot, lows
+
+    def slope(t, low, high, exps, probs, inv, row_dot, lows):
         slopes[t], pairs[t] = [], []
-        for e, pg in zip(exps, probs):
-            p = e * inv
-            ds = (p * (pg - row_dot)).astype(jnp.bfloat16)
-            pair = jnp.concatenate([ds, p.astype(jnp.bfloat16)], axis=1)
+        for e, pg, p in zip(exps, probs, lows):
+            ds = ((e * inv) * (pg - row_dot) * SCALE).astype(jnp.bfloat16)
+            pair = jnp.concatenate([ds, p], axis=1)
             pairs[t].append([pair[i * BLOCK : (i + 1) * BLOCK] for i in range(high - low + 1)])
             slopes[t].append(ds)
 
@@ -262,7 +263,7 @@
         keys = jnp.concatenate([source[span, lane : lane + HEAD_DIM] for source, lane in sources], axis=0)
         ds = jnp.concatenate(slopes.pop(t), axis=0)
         dq = lax.dot_general(ds, keys, (((0,), (0,)), ((), ())), preferred_element_type=jnp.float32)
-        grads[rows(t), dq_lane : dq_lane + HEAD_DIM] = (dq * SCALE).astype(jnp.bfloat16)
+        grads[rows(t), dq_lane : dq_lane + HEAD_DIM] = dq.astype(jnp.bfloat16)
 
     def to_keys(t):
         near_ts = [n for n in (t - 1, t, t + 1) if 0 <= n < time_blocks]
@@ -274,7 +275,6 @@
         r = jnp.dot(jnp.concatenate(x, axis=0), w, preferred_element_type=jnp.float32)
         for block, (target, lane) in enumerate(targets):
             part = r[block * BLOCK : (block + 1) * BLOCK]
-            part = jnp.concatenate([part[:, :HEAD_DIM] * SCALE, part[:, HEAD_DIM:]], axis=1)
             target[rows(t), lane : lane + wide] = part.astype(jnp.bfloat16)
 
     products(0)

time: 136 us -> 138 us (1.015)
  transfers between devices with their start and end apart: 11 -> 11, of which waited for: 5 -> 5; matrix products, arithmetic and copies ran while one was open for 3% -> 3% of each run, Pallas kernels for 10% -> 11%
where the time goes in v7:
time: 138 us; the launch traced here: 137 us
  waiting for transfers between devices  44.8 us (32%)
  blocking collectives  36.4 us (26%)
  starting transfers between devices  29.8 us (22%)
  Pallas kernels  20.8 us (15%)
  local copies, waits for them, and re-layouts  3.49 us (3%)
    all_to_all x1, blocking collectives, shards(): lax.all_to_all(grads.reshape(32, 32, 9 * HEAD_DIM), 'ctx', 0, 0, tiled=True)  36.4 us
    all_to_all x1, waiting for transfers between devices, shards(): lax.all_to_all(packed, 'ctx', 0, 0, tiled=True).reshape(1024, 12 * HEAD_DIM)  35.5 us
    pallas_call x3, Pallas kernels, head_grads(): pl.pallas_call(lambda *refs: grads_kernel(lanes, *refs), in_specs=[VMEM]...  13.3 us
    all_to_all x1, starting transfers between devices, shards(): lax.all_to_all(packed, 'ctx', 0, 0, tiled=True).reshape(1024, 12 * HEAD_DIM)  9.64 us
    ppermute x2, starting transfers between devices, shards(): fars = [lax.ppermute(part, 'ctx', chain) for part in for_far]  5.55 us
    ppermute x1, waiting for transfers between devices, shards(): last_back = lax.ppermute(to_far, 'ctx', chain)  3.82 us
    ppermute x1, starting transfers between devices, mask_bias(): other = lax.ppermute(window_mask[0], 'ctx', mask_pairs(1))  3.81 us
    ppermute x1, starting transfers between devices, shards(): next_back = lax.ppermute(to_far, 'ctx', chain)  3.64 us
  transfers between devices with their start and end apart: 11, of which 5 were waited for; matrix products, arithmetic and copies ran while one was open for 3% of the time, Pallas kernels for 11%

profile of v7, /device:TPU:1, one launch (start us, length us, event | category | flops | bytes accessed | tf_op | source)
XLA Modules:
  0.0 137.1 jit_solution(8082691886328170976)
XLA Ops:
  0.6 0.0 copy-start
  0.6 3.3 %pack.1 = bf16[4,2,2,2,32,1536]{5,4,3,2,1,0:T(8,128)(2,1)} custom-call(bf16[8,2,4,8,768]{4,3,2,1,0:T(8,128)(2,1)} %bitcast.111, bf16[8,2,4,8,768]{4,3,2,1,0:T(8,128)(2,1)} %bitcast.112, bf16[8,2,4,8,768]{4,3,2,1,0:T(8,128)(2,1)} %bitcast.113, bf16[8,2,4,8,768]{4,3,2,1,0:T(8,128)(2,1)} %bitcast.114), custom_call_target="tpu_custom_call" | custom-call | bytes 4000000 | tf_op jit(solution)/shard_map/pack/pallas_call | solution.py:178
  3.9 0.0 copy-done
  4.0 3.8 %collective-permute-start.1 = (s32[8,27]{1,0:T(8,128)S(1)}, s32[8,27]{1,0:T(8,128)S(1)}, u32[]{:S(2)}, u32[]{:S(2)}) collective-permute-start(s32[8,27]{1,0:T(8,128)S(1)} %bitcast.124), channel_id=1, source_target_pairs={{0,16},{4,20},{8,48},{12,52},{16,80},{20,84},{24,112},{28,116},{32... | collective-permute-start | bytes 2600 | tf_op jit(solution)/shard_map/ppermute | solution.py:58
  7.8 0.6 collective-permute-start
  8.4 9.6 %all-to-all-start = ((bf16[32,32,1536]{2,1,0:T(8,128)(2,1)}), bf16[32,32,1536]{2,1,0:T(8,128)(2,1)S(1)}, u32[]{:S(2)}, u32[]{:S(2)}) async-start(bf16[32,32,1536]{2,1,0:T(8,128)(2,1)} %bitcast.110), calls=%async_computation | async-start | bytes 6291456 | tf_op jit(solution)/shard_map/all_to_all | solution.py:380
  18.2 0.0 collective-permute-done.1
  18.2 0.0 collective-permute-done
  18.2 0.1 copy.39
  18.3 0.1 copy.40
  19.1 0.1 copy.49
  19.3 0.1 copy.50
  19.4 0.1 copy.51
  19.5 1.0 broadcast_in_dim.16
  20.6 1.8 %reshape.148 = f32[8,18,128]{2,0,1:T(8,128)S(1)} reshape(f32[8,18,4,2,16]{4,3,2,0,1:T(2,128)} %broadcast_in_dim.16) | data formatting | bytes 147456 | tf_op jit(solution)/shard_map/reshape | solution.py:91
  22.4 35.5 %all-to-all-done = bf16[32,32,1536]{2,1,0:T(8,128)(2,1)S(1)} async-done(((bf16[32,32,1536]{2,1,0:T(8,128)(2,1)}), bf16[32,32,1536]{2,1,0:T(8,128)(2,1)S(1)}, u32[]{:S(2)}, u32[]{:S(2)}) %all-to-all-start) | async-done | bytes 3145760 | tf_op jit(solution)/shard_map/all_to_all | solution.py:380
  57.8 0.2 split.1
  58.0 0.5 collective-permute-start.2
  58.5 1.9 %collective-permute-start.5 = (bf16[1024,256]{1,0:T(8,128)(2,1)S(1)}, bf16[1024,256]{1,0:T(8,128)(2,1)S(1)}, u32[]{:S(2)}, u32[]{:S(2)}) collective-permute-start(bf16[1024,256]{1,0:T(8,128)(2,1)S(1)} %get-tuple-element.24), channel_id=1, source_target_pairs={{4,32},{32,4},{36,64},{64,36},{68,96},{96,68},{100,104},{104,100},... | collective-permute-start | bytes 1572872 | tf_op jit(solution)/shard_map/ppermute | solution.py:383
  60.4 3.6 %collective-permute-start.4 = (bf16[1024,256]{1,0:T(8,128)(2,1)S(1)}, bf16[1024,256]{1,0:T(8,128)(2,1)S(1)}, u32[]{:S(2)}, u32[]{:S(2)}) collective-permute-start(bf16[1024,256]{1,0:T(8,128)(2,1)S(1)} %get-tuple-element.23), channel_id=1, source_target_pairs={{4,32},{32,4},{36,64},{64,36},{68,96},{96,68},{100,104},{104,100},... | collective-permute-start | bytes 1572872 | tf_op jit(solution)/shard_map/ppermute | solution.py:383
  64.1 0.0 collective-permute-done.2._.refs_3_
  64.1 1.9 %collective-permute-start.3 = (bf16[1024,256]{1,0:T(8,128)(2,1)S(1)}, bf16[1024,256]{1,0:T(8,128)(2,1)S(1)}, u32[]{:S(2)}, u32[]{:S(2)}) collective-permute-start(bf16[1024,256]{1,0:T(8,128)(2,1)S(1)} %take_last.1), channel_id=1, source_target_pairs={{4,32},{32,4},{36,64},{64,36},{68,96},{96,68},{100,104},{104,100},... | collective-permute-start | bytes 1572872 | tf_op jit(solution)/shard_map/ppermute | solution.py:385
  66.1 2.9 %collective-permute-done.5.refs_4_ = bf16[1024,256]{1,0:T(8,128)(2,1)S(1)} collective-permute-done((bf16[1024,256]{1,0:T(8,128)(2,1)S(1)}, bf16[1024,256]{1,0:T(8,128)(2,1)S(1)}, u32[]{:S(2)}, u32[]{:S(2)}) %collective-permute-start.5) | collective-permute-done | bytes 524320 | tf_op jit(solution)/shard_map/ppermute | solution.py:383
  69.0 4.4 %head_grads.3 = (bf16[1024,1152]{1,0:T(8,128)(2,1)S(1)}, bf16[1024,768]{1,0:T(8,128)(2,1)S(1)}, bf16[1024,256]{1,0:T(8,128)(2,1)S(1)}) custom-call(f32[8,18,128]{2,1,0:T(8,128)S(1)} %copy.55.bias.refs_0_, bf16[1024,1536]{1,0:T(8,128)(2,1)S(1)} %bitcast.102, bf16[1024,1536]{1,0:T(8,128)(2,1)S(1)} %bitcast.103, ...), custom_call_target="tpu_custom_call" | custom-call | flops 1000000000 | bytes 4500000 | tf_op jit(solution)/shard_map/head_grads/pallas_call | solution.py:299
  73.4 2.1 %collective-permute-start.6 = (bf16[1024,256]{1,0:T(8,128)(2,1)S(1)}, bf16[1024,256]{1,0:T(8,128)(2,1)S(1)}, u32[]{:S(2)}, u32[]{:S(2)}) collective-permute-start(bf16[1024,256]{1,0:T(8,128)(2,1)S(1)} %get-tuple-element.30), channel_id=1, source_target_pairs={{4,32},{32,4},{36,64},{64,36},{68,96},{96,68},{100,104},{104,100},... | collective-permute-start | bytes 1572872 | tf_op jit(solution)/shard_map/ppermute | solution.py:387
  75.5 0.0 collective-permute-done.4.refs_4_
  75.6 4.4 %head_grads.4 = (bf16[1024,1152]{1,0:T(8,128)(2,1)S(1)}, bf16[1024,768]{1,0:T(8,128)(2,1)S(1)}, bf16[1024,256]{1,0:T(8,128)(2,1)S(1)}) custom-call(f32[8,18,128]{2,1,0:T(8,128)S(1)} %copy.55.bias.refs_0_, bf16[1024,1536]{1,0:T(8,128)(2,1)S(1)} %bitcast.104, bf16[1024,1536]{1,0:T(8,128)(2,1)S(1)} %bitcast.105, ...), custom_call_target="tpu_custom_call", output_to_operand_aliasing={{0}: (5, {}), {1}: (6, {})} | custom-call | flops 1000000000 | bytes 4500000 | tf_op jit(solution)/shard_map/head_grads/pallas_call | solution.py:299
  80.0 3.6 %collective-permute-start.7 = (bf16[1024,256]{1,0:T(8,128)(2,1)S(1)}, bf16[1024,256]{1,0:T(8,128)(2,1)S(1)}, u32[]{:S(2)}, u32[]{:S(2)}) collective-permute-start(bf16[1024,256]{1,0:T(8,128)(2,1)S(1)} %get-tuple-element.31), channel_id=1, source_target_pairs={{4,32},{32,4},{36,64},{64,36},{68,96},{96,68},{100,104},{104,100},... | collective-permute-start | bytes 1572872 | tf_op jit(solution)/shard_map/ppermute | solution.py:389
  83.6 0.0 collective-permute-done.3.refs_4_
  83.7 4.4 %head_grads.5 = (bf16[1024,1152]{1,0:T(8,128)(2,1)S(1)}, bf16[1024,768]{1,0:T(8,128)(2,1)S(1)}, bf16[1024,256]{1,0:T(8,128)(2,1)S(1)}) custom-call(f32[8,18,128]{2,1,0:T(8,128)S(1)} %copy.55.bias.refs_0_, bf16[1024,1536]{1,0:T(8,128)(2,1)S(1)} %bitcast.106, bf16[1024,1536]{1,0:T(8,128)(2,1)S(1)} %bitcast.107, ...), custom_call_target="tpu_custom_call", output_to_operand_aliasing={{0}: (5, {}), {1}: (6, {})} | custom-call | flops 3000000000 | bytes 4500000 | tf_op jit(solution)/shard_map/head_grads/pallas_call | solution.py:299
  88.1 1.9 %collective-permute-start.9 = (bf16[1024,256]{1,0:T(8,128)(2,1)S(1)}, bf16[1024,256]{1,0:T(8,128)(2,1)S(1)}, u32[]{:S(2)}, u32[]{:S(2)}) collective-permute-start(bf16[1024,256]{1,0:T(8,128)(2,1)S(1)} %get-tuple-element.33), channel_id=1, source_target_pairs={{4,32},{32,4},{36,64},{64,36},{68,96},{96,68},{100,104},{104,100},... | collective-permute-start | bytes 1572872 | tf_op jit(solution)/shard_map/ppermute | solution.py:393
  90.0 0.1 collective-permute-start.8
  90.1 0.0 collective-permute-done.6.halo
  90.1 0.4 add_halo.4.grads
  90.6 0.9 collective-permute-done.7.halo
  91.5 0.4 add_halo.5.grads
  91.9 1.7 %collective-permute-done.8.halo = bf16[1024,768]{1,0:T(8,128)(2,1)S(1)} collective-permute-done((bf16[1024,768]{1,0:T(8,128)(2,1)S(1)}, bf16[1024,768]{1,0:T(8,128)(2,1)S(1)}, u32[]{:S(2)}, u32[]{:S(2)}) %collective-permute-start.8) | collective-permute-done | bytes 1572896 | tf_op jit(solution)/shard_map/ppermute | solution.py:392
  93.5 1.3 add_halo.6.grads
  94.8 3.8 %collective-permute-done.9.halo = bf16[1024,256]{1,0:T(8,128)(2,1)S(1)} collective-permute-done((bf16[1024,256]{1,0:T(8,128)(2,1)S(1)}, bf16[1024,256]{1,0:T(8,128)(2,1)S(1)}, u32[]{:S(2)}, u32[]{:S(2)}) %collective-permute-start.9) | collective-permute-done | bytes 524320 | tf_op jit(solution)/shard_map/ppermute | solution.py:393
  98.6 0.4 add_halo.7
  99.0 36.4 %all_to_all.10 = bf16[32,32,1152]{2,1,0:T(8,128)(2,1)S(1)} all-to-all(bf16[32,32,1152]{2,1,0:T(8,128)(2,1)S(1)} %bitcast.108), channel_id=1, replica_groups=mesh['ctx'=32,'head'=4] {'ctx'}, dimensions={0} | all-to-all | bytes 4718592 | tf_op jit(solution)/shard_map/all_to_all | solution.py:398
  135.4 1.5 %unpack.1 = (bf16[8,2,4,8,768]{4,3,2,1,0:T(8,128)(2,1)}, bf16[8,2,4,8,768]{4,3,2,1,0:T(8,128)(2,1)}, bf16[8,2,4,8,768]{4,3,2,1,0:T(8,128)(2,1)}) custom-call(bf16[4,2,2,2,32,1152]{5,4,3,2,1,0:T(8,128)(2,1)S(1)} %bitcast.109), custom_call_target="tpu_custom_call" | custom-call | bytes 4700000 | tf_op jit(solution)/shard_map/unpack/pallas_call | solution.py:119
  (50 shorter events, 0.6 us)
Async XLA Ops:
  0.6 3.3 %copy-start = (s32[1,8,27]{2,1,0:T(8,128)S(1)}, s32[1,8,27]{2,1,0:T(8,128)}, u32[]{:S(2)}) copy-start(s32[1,8,27]{2,1,0:T(8,128)} %param.9) | copy-start | bytes 2596
  4.0 14.2 %collective-permute-start.1 = (s32[8,27]{1,0:T(8,128)S(1)}, s32[8,27]{1,0:T(8,128)S(1)}, u32[]{:S(2)}, u32[]{:S(2)}) collective-permute-start(s32[8,27]{1,0:T(8,128)S(1)} %bitcast.124), channel_id=1, source_target_pairs={{0,16},{4,20},{8,48},{12,52},{16,80},{20,84},{24,112},{28,116},{32... | collective-permute-start | bytes 2600 | tf_op jit(solution)/shard_map/ppermute | solution.py:58
  7.8 10.4 %collective-permute-start = (s32[8,27]{1,0:T(8,128)S(1)}, s32[8,27]{1,0:T(8,128)S(1)}, u32[]{:S(2)}, u32[]{:S(2)}) collective-permute-start(s32[8,27]{1,0:T(8,128)S(1)} %bitcast.125), channel_id=1, source_target_pairs={{0,0},{4,4},{8,32},{12,36},{16,64},{20,68},{24,96},{28,100},{32,10... | collective-permute-start | bytes 2600 | tf_op jit(solution)/shard_map/ppermute | solution.py:57
  8.4 49.4 %all-to-all-start = ((bf16[32,32,1536]{2,1,0:T(8,128)(2,1)}), bf16[32,32,1536]{2,1,0:T(8,128)(2,1)S(1)}, u32[]{:S(2)}, u32[]{:S(2)}) async-start(bf16[32,32,1536]{2,1,0:T(8,128)(2,1)} %bitcast.110), calls=%async_computation | async-start | bytes 6291456 | tf_op jit(solution)/shard_map/all_to_all | solution.py:380
  58.0 6.1 %collective-permute-start.2 = (bf16[1024,768]{1,0:T(8,128)(2,1)S(1)}, bf16[1024,768]{1,0:T(8,128)(2,1)S(1)}, u32[]{:S(2)}, u32[]{:S(2)}) collective-permute-start(bf16[1024,768]{1,0:T(8,128)(2,1)S(1)} %get-tuple-element.22), channel_id=1, source_target_pairs={{0,4},{4,0},{8,12},{12,8},{16,20},{20,16},{24,28},{28,24},{32,36},... | collective-permute-start | bytes 4718600 | tf_op jit(solution)/shard_map/ppermute | solution.py:384
  58.5 10.5 %collective-permute-start.5 = (bf16[1024,256]{1,0:T(8,128)(2,1)S(1)}, bf16[1024,256]{1,0:T(8,128)(2,1)S(1)}, u32[]{:S(2)}, u32[]{:S(2)}) collective-permute-start(bf16[1024,256]{1,0:T(8,128)(2,1)S(1)} %get-tuple-element.24), channel_id=1, source_target_pairs={{4,32},{32,4},{36,64},{64,36},{68,96},{96,68},{100,104},{104,100},... | collective-permute-start | bytes 1572872 | tf_op jit(solution)/shard_map/ppermute | solution.py:383
  60.4 15.1 %collective-permute-start.4 = (bf16[1024,256]{1,0:T(8,128)(2,1)S(1)}, bf16[1024,256]{1,0:T(8,128)(2,1)S(1)}, u32[]{:S(2)}, u32[]{:S(2)}) collective-permute-start(bf16[1024,256]{1,0:T(8,128)(2,1)S(1)} %get-tuple-element.23), channel_id=1, source_target_pairs={{4,32},{32,4},{36,64},{64,36},{68,96},{96,68},{100,104},{104,100},... | collective-permute-start | bytes 1572872 | tf_op jit(solution)/shard_map/ppermute | solution.py:383
  64.1 19.5 %collective-permute-start.3 = (bf16[1024,256]{1,0:T(8,128)(2,1)S(1)}, bf16[1024,256]{1,0:T(8,128)(2,1)S(1)}, u32[]{:S(2)}, u32[]{:S(2)}) collective-permute-start(bf16[1024,256]{1,0:T(8,128)(2,1)S(1)} %take_last.1), channel_id=1, source_target_pairs={{4,32},{32,4},{36,64},{64,36},{68,96},{96,68},{100,104},{104,100},... | collective-permute-start | bytes 1572872 | tf_op jit(solution)/shard_map/ppermute | solution.py:385
  73.4 16.7 %collective-permute-start.6 = (bf16[1024,256]{1,0:T(8,128)(2,1)S(1)}, bf16[1024,256]{1,0:T(8,128)(2,1)S(1)}, u32[]{:S(2)}, u32[]{:S(2)}) collective-permute-start(bf16[1024,256]{1,0:T(8,128)(2,1)S(1)} %get-tuple-element.30), channel_id=1, source_target_pairs={{4,32},{32,4},{36,64},{64,36},{68,96},{96,68},{100,104},{104,100},... | collective-permute-start | bytes 1572872 | tf_op jit(solution)/shard_map/ppermute | solution.py:387
  80.0 11.5 %collective-permute-start.7 = (bf16[1024,256]{1,0:T(8,128)(2,1)S(1)}, bf16[1024,256]{1,0:T(8,128)(2,1)S(1)}, u32[]{:S(2)}, u32[]{:S(2)}) collective-permute-start(bf16[1024,256]{1,0:T(8,128)(2,1)S(1)} %get-tuple-element.31), channel_id=1, source_target_pairs={{4,32},{32,4},{36,64},{64,36},{68,96},{96,68},{100,104},{104,100},... | collective-permute-start | bytes 1572872 | tf_op jit(solution)/shard_map/ppermute | solution.py:389
  88.1 10.5 %collective-permute-start.9 = (bf16[1024,256]{1,0:T(8,128)(2,1)S(1)}, bf16[1024,256]{1,0:T(8,128)(2,1)S(1)}, u32[]{:S(2)}, u32[]{:S(2)}) collective-permute-start(bf16[1024,256]{1,0:T(8,128)(2,1)S(1)} %get-tuple-element.33), channel_id=1, source_target_pairs={{4,32},{32,4},{36,64},{64,36},{68,96},{96,68},{100,104},{104,100},... | collective-permute-start | bytes 1572872 | tf_op jit(solution)/shard_map/ppermute | solution.py:393
  90.0 3.5 %collective-permute-start.8 = (bf16[1024,768]{1,0:T(8,128)(2,1)S(1)}, bf16[1024,768]{1,0:T(8,128)(2,1)S(1)}, u32[]{:S(2)}, u32[]{:S(2)}) collective-permute-start(bf16[1024,768]{1,0:T(8,128)(2,1)S(1)} %get-tuple-element.32), channel_id=1, source_target_pairs={{0,4},{4,0},{8,12},{12,8},{16,20},{20,16},{24,28},{28,24},{32,36},... | collective-permute-start | bytes 4718600 | tf_op jit(solution)/shard_map/ppermute | solution.py:392

commit v8 on v7

--- a/solution.py
+++ b/solution.py
@@ -244,17 +244,16 @@
             exps.append(e)
         inv = 1.0 / total
         row_dot = jnp.zeros((1, BLOCK), jnp.float32)
-        lows = []
-        for e, pg in zip(exps, probs):
-            lows.append((e * inv).astype(jnp.bfloat16))
-            row_dot += jnp.sum(lows[-1].astype(jnp.float32) * pg, axis=0, keepdims=True)
-        return low, high, exps, probs, inv, row_dot, lows
-
-    def slope(t, low, high, exps, probs, inv, row_dot, lows):
+        attention = [e * inv for e in exps]
+        for p, pg in zip(attention, probs):
+            row_dot += jnp.sum(p.astype(jnp.bfloat16).astype(jnp.float32) * pg, axis=0, keepdims=True)
+        return low, high, attention, probs, row_dot
+
+    def slope(t, low, high, attention, probs, row_dot):
         slopes[t], pairs[t] = [], []
-        for e, pg, p in zip(exps, probs, lows):
-            ds = ((e * inv) * (pg - row_dot) * SCALE).astype(jnp.bfloat16)
-            pair = jnp.concatenate([ds, p], axis=1)
+        for p, pg in zip(attention, probs):
+            ds = (p * (pg - row_dot) * SCALE).astype(jnp.bfloat16)
+            pair = jnp.concatenate([ds, p.astype(jnp.bfloat16)], axis=1)
             pairs[t].append([pair[i * BLOCK : (i + 1) * BLOCK] for i in range(high - low + 1)])
             slopes[t].append(ds)
 

time: 138 us -> 138 us (level)
  no operation moved by 1% of the time
where the time goes in v8:
time: 138 us; the launch traced here: 137 us
  waiting for transfers between devices  44.8 us (32%)
  blocking collectives  36.4 us (26%)
  starting transfers between devices  29.8 us (22%)
  Pallas kernels  20.8 us (15%)
  local copies, waits for them, and re-layouts  3.49 us (3%)
    all_to_all x1, blocking collectives, shards(): lax.all_to_all(grads.reshape(32, 32, 9 * HEAD_DIM), 'ctx', 0, 0, tiled=True)  36.4 us
    all_to_all x1, waiting for transfers between devices, shards(): lax.all_to_all(packed, 'ctx', 0, 0, tiled=True).reshape(1024, 12 * HEAD_DIM)  35.5 us
    pallas_call x3, Pallas kernels, head_grads(): pl.pallas_call(lambda *refs: grads_kernel(lanes, *refs), in_specs=[VMEM]...  13.3 us
    all_to_all x1, starting transfers between devices, shards(): lax.all_to_all(packed, 'ctx', 0, 0, tiled=True).reshape(1024, 12 * HEAD_DIM)  9.64 us
    ppermute x2, starting transfers between devices, shards(): fars = [lax.ppermute(part, 'ctx', chain) for part in for_far]  5.55 us
    ppermute x1, waiting for transfers between devices, shards(): last_back = lax.ppermute(to_far, 'ctx', chain)  3.83 us
    ppermute x1, starting transfers between devices, mask_bias(): other = lax.ppermute(window_mask[0], 'ctx', mask_pairs(1))  3.81 us
    ppermute x1, starting transfers between devices, shards(): next_back = lax.ppermute(to_far, 'ctx', chain)  3.64 us
  transfers between devices with their start and end apart: 11, of which 5 were waited for; matrix products, arithmetic and copies ran while one was open for 3% of the time, Pallas kernels for 11%

profile of v8, /device:TPU:1, one launch (start us, length us, event | category | flops | bytes accessed | tf_op | source)
XLA Modules:
  0.0 137.1 jit_solution(5665904955059180437)
XLA Ops:
  0.6 0.0 copy-start
  0.6 3.3 %pack.1 = bf16[4,2,2,2,32,1536]{5,4,3,2,1,0:T(8,128)(2,1)} custom-call(bf16[8,2,4,8,768]{4,3,2,1,0:T(8,128)(2,1)} %bitcast.111, bf16[8,2,4,8,768]{4,3,2,1,0:T(8,128)(2,1)} %bitcast.112, bf16[8,2,4,8,768]{4,3,2,1,0:T(8,128)(2,1)} %bitcast.113, bf16[8,2,4,8,768]{4,3,2,1,0:T(8,128)(2,1)} %bitcast.114), custom_call_target="tpu_custom_call" | custom-call | bytes 4000000 | tf_op jit(solution)/shard_map/pack/pallas_call | solution.py:178
  3.9 0.0 copy-done
  4.0 3.8 %collective-permute-start.1 = (s32[8,27]{1,0:T(8,128)S(1)}, s32[8,27]{1,0:T(8,128)S(1)}, u32[]{:S(2)}, u32[]{:S(2)}) collective-permute-start(s32[8,27]{1,0:T(8,128)S(1)} %bitcast.124), channel_id=1, source_target_pairs={{0,16},{4,20},{8,48},{12,52},{16,80},{20,84},{24,112},{28,116},{32... | collective-permute-start | bytes 2600 | tf_op jit(solution)/shard_map/ppermute | solution.py:58
  7.8 0.6 collective-permute-start
  8.4 9.6 %all-to-all-start = ((bf16[32,32,1536]{2,1,0:T(8,128)(2,1)}), bf16[32,32,1536]{2,1,0:T(8,128)(2,1)S(1)}, u32[]{:S(2)}, u32[]{:S(2)}) async-start(bf16[32,32,1536]{2,1,0:T(8,128)(2,1)} %bitcast.110), calls=%async_computation | async-start | bytes 6291456 | tf_op jit(solution)/shard_map/all_to_all | solution.py:379
  18.2 0.0 collective-permute-done.1
  18.2 0.0 collective-permute-done
  18.2 0.1 copy.39
  18.3 0.1 copy.40
  19.1 0.1 copy.49
  19.3 0.1 copy.50
  19.4 0.1 copy.51
  19.5 1.0 broadcast_in_dim.16
  20.6 1.8 %reshape.148 = f32[8,18,128]{2,0,1:T(8,128)S(1)} reshape(f32[8,18,4,2,16]{4,3,2,0,1:T(2,128)} %broadcast_in_dim.16) | data formatting | bytes 147456 | tf_op jit(solution)/shard_map/reshape | solution.py:91
  22.4 35.5 %all-to-all-done = bf16[32,32,1536]{2,1,0:T(8,128)(2,1)S(1)} async-done(((bf16[32,32,1536]{2,1,0:T(8,128)(2,1)}), bf16[32,32,1536]{2,1,0:T(8,128)(2,1)S(1)}, u32[]{:S(2)}, u32[]{:S(2)}) %all-to-all-start) | async-done | bytes 3145760 | tf_op jit(solution)/shard_map/all_to_all | solution.py:379
  57.8 0.2 split.1
  58.0 0.5 collective-permute-start.2
  58.5 1.9 %collective-permute-start.5 = (bf16[1024,256]{1,0:T(8,128)(2,1)S(1)}, bf16[1024,256]{1,0:T(8,128)(2,1)S(1)}, u32[]{:S(2)}, u32[]{:S(2)}) collective-permute-start(bf16[1024,256]{1,0:T(8,128)(2,1)S(1)} %get-tuple-element.24), channel_id=1, source_target_pairs={{4,32},{32,4},{36,64},{64,36},{68,96},{96,68},{100,104},{104,100},... | collective-permute-start | bytes 1572872 | tf_op jit(solution)/shard_map/ppermute | solution.py:382
  60.4 3.6 %collective-permute-start.4 = (bf16[1024,256]{1,0:T(8,128)(2,1)S(1)}, bf16[1024,256]{1,0:T(8,128)(2,1)S(1)}, u32[]{:S(2)}, u32[]{:S(2)}) collective-permute-start(bf16[1024,256]{1,0:T(8,128)(2,1)S(1)} %get-tuple-element.23), channel_id=1, source_target_pairs={{4,32},{32,4},{36,64},{64,36},{68,96},{96,68},{100,104},{104,100},... | collective-permute-start | bytes 1572872 | tf_op jit(solution)/shard_map/ppermute | solution.py:382
  64.1 0.0 collective-permute-done.2._.refs_3_
  64.1 1.9 %collective-permute-start.3 = (bf16[1024,256]{1,0:T(8,128)(2,1)S(1)}, bf16[1024,256]{1,0:T(8,128)(2,1)S(1)}, u32[]{:S(2)}, u32[]{:S(2)}) collective-permute-start(bf16[1024,256]{1,0:T(8,128)(2,1)S(1)} %take_last.1), channel_id=1, source_target_pairs={{4,32},{32,4},{36,64},{64,36},{68,96},{96,68},{100,104},{104,100},... | collective-permute-start | bytes 1572872 | tf_op jit(solution)/shard_map/ppermute | solution.py:384
  66.1 2.9 %collective-permute-done.5.refs_4_ = bf16[1024,256]{1,0:T(8,128)(2,1)S(1)} collective-permute-done((bf16[1024,256]{1,0:T(8,128)(2,1)S(1)}, bf16[1024,256]{1,0:T(8,128)(2,1)S(1)}, u32[]{:S(2)}, u32[]{:S(2)}) %collective-permute-start.5) | collective-permute-done | bytes 524320 | tf_op jit(solution)/shard_map/ppermute | solution.py:382
  69.0 4.4 %head_grads.3 = (bf16[1024,1152]{1,0:T(8,128)(2,1)S(1)}, bf16[1024,768]{1,0:T(8,128)(2,1)S(1)}, bf16[1024,256]{1,0:T(8,128)(2,1)S(1)}) custom-call(f32[8,18,128]{2,1,0:T(8,128)S(1)} %copy.55.bias.refs_0_, bf16[1024,1536]{1,0:T(8,128)(2,1)S(1)} %bitcast.102, bf16[1024,1536]{1,0:T(8,128)(2,1)S(1)} %bitcast.103, ...), custom_call_target="tpu_custom_call" | custom-call | flops 1000000000 | bytes 4500000 | tf_op jit(solution)/shard_map/head_grads/pallas_call | solution.py:298
  73.4 2.1 %collective-permute-start.6 = (bf16[1024,256]{1,0:T(8,128)(2,1)S(1)}, bf16[1024,256]{1,0:T(8,128)(2,1)S(1)}, u32[]{:S(2)}, u32[]{:S(2)}) collective-permute-start(bf16[1024,256]{1,0:T(8,128)(2,1)S(1)} %get-tuple-element.30), channel_id=1, source_target_pairs={{4,32},{32,4},{36,64},{64,36},{68,96},{96,68},{100,104},{104,100},... | collective-permute-start | bytes 1572872 | tf_op jit(solution)/shard_map/ppermute | solution.py:386
  75.5 0.0 collective-permute-done.4.refs_4_
  75.5 4.4 %head_grads.4 = (bf16[1024,1152]{1,0:T(8,128)(2,1)S(1)}, bf16[1024,768]{1,0:T(8,128)(2,1)S(1)}, bf16[1024,256]{1,0:T(8,128)(2,1)S(1)}) custom-call(f32[8,18,128]{2,1,0:T(8,128)S(1)} %copy.55.bias.refs_0_, bf16[1024,1536]{1,0:T(8,128)(2,1)S(1)} %bitcast.104, bf16[1024,1536]{1,0:T(8,128)(2,1)S(1)} %bitcast.105, ...), custom_call_target="tpu_custom_call", output_to_operand_aliasing={{0}: (5, {}), {1}: (6, {})} | custom-call | flops 1000000000 | bytes 4500000 | tf_op jit(solution)/shard_map/head_grads/pallas_call | solution.py:298
  80.0 3.6 %collective-permute-start.7 = (bf16[1024,256]{1,0:T(8,128)(2,1)S(1)}, bf16[1024,256]{1,0:T(8,128)(2,1)S(1)}, u32[]{:S(2)}, u32[]{:S(2)}) collective-permute-start(bf16[1024,256]{1,0:T(8,128)(2,1)S(1)} %get-tuple-element.31), channel_id=1, source_target_pairs={{4,32},{32,4},{36,64},{64,36},{68,96},{96,68},{100,104},{104,100},... | collective-permute-start | bytes 1572872 | tf_op jit(solution)/shard_map/ppermute | solution.py:388
  83.6 0.0 collective-permute-done.3.refs_4_
  83.6 4.4 %head_grads.5 = (bf16[1024,1152]{1,0:T(8,128)(2,1)S(1)}, bf16[1024,768]{1,0:T(8,128)(2,1)S(1)}, bf16[1024,256]{1,0:T(8,128)(2,1)S(1)}) custom-call(f32[8,18,128]{2,1,0:T(8,128)S(1)} %copy.55.bias.refs_0_, bf16[1024,1536]{1,0:T(8,128)(2,1)S(1)} %bitcast.106, bf16[1024,1536]{1,0:T(8,128)(2,1)S(1)} %bitcast.107, ...), custom_call_target="tpu_custom_call", output_to_operand_aliasing={{0}: (5, {}), {1}: (6, {})} | custom-call | flops 3000000000 | bytes 4500000 | tf_op jit(solution)/shard_map/head_grads/pallas_call | solution.py:298
  88.0 1.9 %collective-permute-start.9 = (bf16[1024,256]{1,0:T(8,128)(2,1)S(1)}, bf16[1024,256]{1,0:T(8,128)(2,1)S(1)}, u32[]{:S(2)}, u32[]{:S(2)}) collective-permute-start(bf16[1024,256]{1,0:T(8,128)(2,1)S(1)} %get-tuple-element.33), channel_id=1, source_target_pairs={{4,32},{32,4},{36,64},{64,36},{68,96},{96,68},{100,104},{104,100},... | collective-permute-start | bytes 1572872 | tf_op jit(solution)/shard_map/ppermute | solution.py:392
  90.0 0.1 collective-permute-start.8
  90.1 0.0 collective-permute-done.6.halo
  90.1 0.4 add_halo.4.grads
  90.5 1.0 collective-permute-done.7.halo
  91.5 0.4 add_halo.5.grads
  91.9 1.6 %collective-permute-done.8.halo = bf16[1024,768]{1,0:T(8,128)(2,1)S(1)} collective-permute-done((bf16[1024,768]{1,0:T(8,128)(2,1)S(1)}, bf16[1024,768]{1,0:T(8,128)(2,1)S(1)}, u32[]{:S(2)}, u32[]{:S(2)}) %collective-permute-start.8) | collective-permute-done | bytes 1572896 | tf_op jit(solution)/shard_map/ppermute | solution.py:391
  93.5 1.3 add_halo.6.grads
  94.7 3.8 %collective-permute-done.9.halo = bf16[1024,256]{1,0:T(8,128)(2,1)S(1)} collective-permute-done((bf16[1024,256]{1,0:T(8,128)(2,1)S(1)}, bf16[1024,256]{1,0:T(8,128)(2,1)S(1)}, u32[]{:S(2)}, u32[]{:S(2)}) %collective-permute-start.9) | collective-permute-done | bytes 524320 | tf_op jit(solution)/shard_map/ppermute | solution.py:392
  98.6 0.4 add_halo.7
  99.0 36.4 %all_to_all.10 = bf16[32,32,1152]{2,1,0:T(8,128)(2,1)S(1)} all-to-all(bf16[32,32,1152]{2,1,0:T(8,128)(2,1)S(1)} %bitcast.108), channel_id=1, replica_groups=mesh['ctx'=32,'head'=4] {'ctx'}, dimensions={0} | all-to-all | bytes 4718592 | tf_op jit(solution)/shard_map/all_to_all | solution.py:397
  135.4 1.5 %unpack.1 = (bf16[8,2,4,8,768]{4,3,2,1,0:T(8,128)(2,1)}, bf16[8,2,4,8,768]{4,3,2,1,0:T(8,128)(2,1)}, bf16[8,2,4,8,768]{4,3,2,1,0:T(8,128)(2,1)}) custom-call(bf16[4,2,2,2,32,1152]{5,4,3,2,1,0:T(8,128)(2,1)S(1)} %bitcast.109), custom_call_target="tpu_custom_call" | custom-call | bytes 4700000 | tf_op jit(solution)/shard_map/unpack/pallas_call | solution.py:119
  (50 shorter events, 0.6 us)
Async XLA Ops:
  0.6 3.3 %copy-start = (s32[1,8,27]{2,1,0:T(8,128)S(1)}, s32[1,8,27]{2,1,0:T(8,128)}, u32[]{:S(2)}) copy-start(s32[1,8,27]{2,1,0:T(8,128)} %param.9) | copy-start | bytes 2596
  4.0 14.2 %collective-permute-start.1 = (s32[8,27]{1,0:T(8,128)S(1)}, s32[8,27]{1,0:T(8,128)S(1)}, u32[]{:S(2)}, u32[]{:S(2)}) collective-permute-start(s32[8,27]{1,0:T(8,128)S(1)} %bitcast.124), channel_id=1, source_target_pairs={{0,16},{4,20},{8,48},{12,52},{16,80},{20,84},{24,112},{28,116},{32... | collective-permute-start | bytes 2600 | tf_op jit(solution)/shard_map/ppermute | solution.py:58
  7.8 10.4 %collective-permute-start = (s32[8,27]{1,0:T(8,128)S(1)}, s32[8,27]{1,0:T(8,128)S(1)}, u32[]{:S(2)}, u32[]{:S(2)}) collective-permute-start(s32[8,27]{1,0:T(8,128)S(1)} %bitcast.125), channel_id=1, source_target_pairs={{0,0},{4,4},{8,32},{12,36},{16,64},{20,68},{24,96},{28,100},{32,10... | collective-permute-start | bytes 2600 | tf_op jit(solution)/shard_map/ppermute | solution.py:57
  8.4 49.4 %all-to-all-start = ((bf16[32,32,1536]{2,1,0:T(8,128)(2,1)}), bf16[32,32,1536]{2,1,0:T(8,128)(2,1)S(1)}, u32[]{:S(2)}, u32[]{:S(2)}) async-start(bf16[32,32,1536]{2,1,0:T(8,128)(2,1)} %bitcast.110), calls=%async_computation | async-start | bytes 6291456 | tf_op jit(solution)/shard_map/all_to_all | solution.py:379
  58.0 6.1 %collective-permute-start.2 = (bf16[1024,768]{1,0:T(8,128)(2,1)S(1)}, bf16[1024,768]{1,0:T(8,128)(2,1)S(1)}, u32[]{:S(2)}, u32[]{:S(2)}) collective-permute-start(bf16[1024,768]{1,0:T(8,128)(2,1)S(1)} %get-tuple-element.22), channel_id=1, source_target_pairs={{0,4},{4,0},{8,12},{12,8},{16,20},{20,16},{24,28},{28,24},{32,36},... | collective-permute-start | bytes 4718600 | tf_op jit(solution)/shard_map/ppermute | solution.py:383
  58.5 10.5 %collective-permute-start.5 = (bf16[1024,256]{1,0:T(8,128)(2,1)S(1)}, bf16[1024,256]{1,0:T(8,128)(2,1)S(1)}, u32[]{:S(2)}, u32[]{:S(2)}) collective-permute-start(bf16[1024,256]{1,0:T(8,128)(2,1)S(1)} %get-tuple-element.24), channel_id=1, source_target_pairs={{4,32},{32,4},{36,64},{64,36},{68,96},{96,68},{100,104},{104,100},... | collective-permute-start | bytes 1572872 | tf_op jit(solution)/shard_map/ppermute | solution.py:382
  60.4 15.1 %collective-permute-start.4 = (bf16[1024,256]{1,0:T(8,128)(2,1)S(1)}, bf16[1024,256]{1,0:T(8,128)(2,1)S(1)}, u32[]{:S(2)}, u32[]{:S(2)}) collective-permute-start(bf16[1024,256]{1,0:T(8,128)(2,1)S(1)} %get-tuple-element.23), channel_id=1, source_target_pairs={{4,32},{32,4},{36,64},{64,36},{68,96},{96,68},{100,104},{104,100},... | collective-permute-start | bytes 1572872 | tf_op jit(solution)/shard_map/ppermute | solution.py:382
  64.1 19.5 %collective-permute-start.3 = (bf16[1024,256]{1,0:T(8,128)(2,1)S(1)}, bf16[1024,256]{1,0:T(8,128)(2,1)S(1)}, u32[]{:S(2)}, u32[]{:S(2)}) collective-permute-start(bf16[1024,256]{1,0:T(8,128)(2,1)S(1)} %take_last.1), channel_id=1, source_target_pairs={{4,32},{32,4},{36,64},{64,36},{68,96},{96,68},{100,104},{104,100},... | collective-permute-start | bytes 1572872 | tf_op jit(solution)/shard_map/ppermute | solution.py:384
  73.4 16.7 %collective-permute-start.6 = (bf16[1024,256]{1,0:T(8,128)(2,1)S(1)}, bf16[1024,256]{1,0:T(8,128)(2,1)S(1)}, u32[]{:S(2)}, u32[]{:S(2)}) collective-permute-start(bf16[1024,256]{1,0:T(8,128)(2,1)S(1)} %get-tuple-element.30), channel_id=1, source_target_pairs={{4,32},{32,4},{36,64},{64,36},{68,96},{96,68},{100,104},{104,100},... | collective-permute-start | bytes 1572872 | tf_op jit(solution)/shard_map/ppermute | solution.py:386
  80.0 11.5 %collective-permute-start.7 = (bf16[1024,256]{1,0:T(8,128)(2,1)S(1)}, bf16[1024,256]{1,0:T(8,128)(2,1)S(1)}, u32[]{:S(2)}, u32[]{:S(2)}) collective-permute-start(bf16[1024,256]{1,0:T(8,128)(2,1)S(1)} %get-tuple-element.31), channel_id=1, source_target_pairs={{4,32},{32,4},{36,64},{64,36},{68,96},{96,68},{100,104},{104,100},... | collective-permute-start | bytes 1572872 | tf_op jit(solution)/shard_map/ppermute | solution.py:388
  88.0 10.5 %collective-permute-start.9 = (bf16[1024,256]{1,0:T(8,128)(2,1)S(1)}, bf16[1024,256]{1,0:T(8,128)(2,1)S(1)}, u32[]{:S(2)}, u32[]{:S(2)}) collective-permute-start(bf16[1024,256]{1,0:T(8,128)(2,1)S(1)} %get-tuple-element.33), channel_id=1, source_target_pairs={{4,32},{32,4},{36,64},{64,36},{68,96},{96,68},{100,104},{104,100},... | collective-permute-start | bytes 1572872 | tf_op jit(solution)/shard_map/ppermute | solution.py:392
  90.0 3.5 %collective-permute-start.8 = (bf16[1024,768]{1,0:T(8,128)(2,1)S(1)}, bf16[1024,768]{1,0:T(8,128)(2,1)S(1)}, u32[]{:S(2)}, u32[]{:S(2)}) collective-permute-start(bf16[1024,768]{1,0:T(8,128)(2,1)S(1)} %get-tuple-element.32), channel_id=1, source_target_pairs={{0,4},{4,0},{8,12},{12,8},{16,20},{20,16},{24,28},{28,24},{32,36},... | collective-permute-start | bytes 4718600 | tf_op jit(solution)/shard_map/ppermute | solution.py:391
